TPU v7x, 512 devices: a whole 4x8x8 slice. The times are simulated.
512 devices in a mesh: vis: 16 (over y, core), row: 4 (over x), col: 8 (over z).
Axes of the slice: x: 4, y: 8, z: 8, core: 2. Of those that a mesh axis runs over, the one named last changes fastest.
Arguments:
- images: bfloat16 [512, 6400], P(('vis', 'row', 'col')), may hold values from -6 to 6
- counts: int32 [16], replicated, may hold values from 1 to 32, 256 in all
- block_order: int32 [16], replicated, may hold values from 0 to 15, each once
- projector_norm_gain: float32 [6400], replicated, may hold values from 0.1 to 1.9
- proj_first: bfloat16 [6400, 4096], P('vis', ('row', 'col')), may hold values from -0.078125 to 0.078125
- proj_bias: float32 [4096], P(('row', 'col')), may hold values from -3 to 3
- proj_second: bfloat16 [4096, 4096], P(('row', 'col'), 'vis'), may hold values from -0.09375 to 0.09375
- gate_weight: bfloat16 [4096, 16384], P('vis', ('row', 'col')), may hold values from -0.09375 to 0.09375
- up_weight: bfloat16 [4096, 16384], P('vis', ('row', 'col')), may hold values from -0.09375 to 0.09375
- down_weight: bfloat16 [16384, 4096], P(('row', 'col'), 'vis'), may hold values from -0.046875 to 0.046875
- cotangent: bfloat16 [256, 4096], P(('row', 'col'), 'vis'), may hold values from -6 to 6
Outputs:
- block_out: bfloat16 [256, 4096], P(('row', 'col'), 'vis')
- image_slot_gradients: float32 [512, 6400], P(('vis', 'row', 'col'))
- first_grad: float32 [6400, 4096], P('vis', ('row', 'col'))
- second_grad: float32 [4096, 4096], P(('row', 'col'), 'vis')
Inputs may be any that keep to these rules, and one draw needn't show every extreme that they name: Vision device v's live rows are its first counts[v] slots; the counts sum to 256, and some device's slots are all live. `block_order`: each vision device's index once: the order in which the devices' live rows follow one another among the language rows.
All inputs are finite; a program needn't handle non-finite values.
Results may differ from a plain program's by a relative error of at most 0.034.
Values may be sent and summed in bfloat16 or wider, within the bound.
No kernel may reach another device: no remote copies, remote signals or barrier semaphores. Data moves between devices by JAX's collectives and lax.ppermute only.
A program may use at most 64 MiB of HBM per device.

v0:
```python
import jax
import jax.numpy as jnp
from jax import lax
from jax.sharding import Mesh
from jax.sharding import PartitionSpec as P

VIS = ("vis_0", "vis_1")
VIS_ROW_COL = ("vis_0", "vis_1", "row", "col")


def joined_along(blocks, dim):
    blocks = jnp.moveaxis(blocks, 0, dim)
    shape = blocks.shape
    return blocks.reshape(*shape[:dim], shape[dim] * shape[dim + 1], *shape[dim + 2 :])


def sent_to_all(shard, axis):
    length = lax.axis_size(axis)
    return lax.all_to_all(
        jnp.broadcast_to(shard[None], (length, *shard.shape)), axis, 0, 0, tiled=True
    )


def collect(shard, axis, dim):
    return joined_along(sent_to_all(shard, axis), dim)


def total_of_pieces(shard, axis):
    blocks = lax.all_gather(shard, axis).astype(jnp.float32)
    return blocks.sum(axis=0)


def in_blocks(shard, dim, length):
    before, after = (shard.shape[:dim], shard.shape[dim + 1 :])
    return jnp.moveaxis(shard.reshape(*before, length, -1, *after), dim, 0)


def summed_on_arrival(shard, axis, dim):
    length = lax.axis_size(axis)
    blocks = lax.all_to_all(in_blocks(shard, dim, length), axis, 0, 0, tiled=True)
    return jnp.sum(blocks.astype(jnp.float32), axis=0)


def rows_for(lines, length):
    spare = -lines.shape[0] % length
    if not spare:
        return lines
    return jnp.concatenate([lines, jnp.zeros((spare, *lines.shape[1:]), lines.dtype)])


def sum_by_parts(shard, axes):
    lines = shard.reshape(-1, shard.shape[-1])
    own = summed_on_arrival(rows_for(lines, lax.axis_size(axes)), axes, 0)
    whole = collect(own.astype(jnp.bfloat16), axes, 0)
    return whole[: len(lines)].reshape(shard.shape).astype(jnp.float32)


def whole_of(shard, axes, dim):
    far, near = axes
    blocks = sent_to_all(sent_to_all(shard, far), near)
    return joined_along(blocks.swapaxes(0, 1).reshape(-1, *shard.shape), dim)


def sum_by_axis(shard, axes, dim):
    far, near = axes
    own = summed_on_arrival(in_blocks(shard, dim, lax.axis_size(far)), near, dim + 1)
    return jnp.sum(
        lax.all_to_all(own.astype(jnp.bfloat16), far, 0, 0, tiled=True).astype(jnp.float32), axis=0
    )


def sum_by_parts_2(shard, axes):
    lines = shard.reshape(-1, shard.shape[-1])
    padded = rows_for(lines, lax.axis_size(axes[0]) * lax.axis_size(axes[1]))
    whole = whole_of(sum_by_axis(padded, axes, 0).astype(jnp.bfloat16), axes, 0)
    return lax.slice_in_dim(whole, 0, len(lines)).reshape(shard.shape).astype(jnp.float32)


def row_tables(counts, block_order, total_rows, per_device, group_size):
    vision = counts.shape[0]
    labels = jnp.arange(vision, dtype=jnp.int32)
    chosen = (block_order[:, None] == labels[None, :]).astype(jnp.int32)
    ordered = jnp.sum(chosen * counts[None, :], axis=1)
    block_ends = jnp.cumsum(ordered)
    block_starts = block_ends - ordered
    language = jnp.arange(total_rows, dtype=jnp.int32)
    block_of = jnp.sum((block_ends[None, :] <= language[:, None]).astype(jnp.int32), axis=1)
    picked = (block_of[:, None] == labels[None, :]).astype(jnp.int32)
    owner = jnp.sum(picked * block_order[None, :], axis=1)
    offset = language - jnp.sum(picked * block_starts[None, :], axis=1)
    stride = vision * per_device
    source = offset // per_device * stride + owner * per_device + offset % per_device
    slots = jnp.arange(stride * group_size, dtype=jnp.int32)
    within = slots % stride
    slot_owner = within // per_device
    slot_offset = slots // stride * per_device + within % per_device
    owner_start = jnp.sum(chosen * block_starts[:, None], axis=0)
    matched = (slot_owner[:, None] == labels[None, :]).astype(jnp.int32)
    start_of = jnp.sum(matched * owner_start[None, :], axis=1)
    count_of = jnp.sum(matched * counts[None, :], axis=1)
    live = slot_offset < count_of
    target = jnp.where(live, start_of + slot_offset, 0)
    return (source, target, live)


def gelu_parts(pre):
    normal_cdf = 0.5 * (1.0 + jax.scipy.special.erf(pre * 0.7071067811865476))
    density = jnp.exp(-0.5 * pre * pre) * 0.3989422804014327
    return (pre * normal_cdf, normal_cdf + pre * density)


def apply_layer_norm(images, projector_norm_gain):
    values = images.astype(jnp.float32)
    mean_removed = values - jnp.mean(values, axis=-1, keepdims=True)
    variance = jnp.mean(mean_removed * mean_removed, axis=-1, keepdims=True)
    inverse_scale = lax.rsqrt(variance + 1e-05)
    standardized_input = mean_removed * inverse_scale
    return (
        standardized_input,
        inverse_scale,
        (standardized_input * projector_norm_gain).astype(jnp.bfloat16),
    )


def norm_gradient_pass(gradient_tuple, standardized_input, inverse_scale, projector_norm_gain):
    gain_scaled = gradient_tuple * projector_norm_gain
    return inverse_scale * (
        gain_scaled
        - jnp.mean(gain_scaled, axis=-1, keepdims=True)
        - standardized_input * jnp.mean(gain_scaled * standardized_input, axis=-1, keepdims=True)
    )


def product(left, right):
    return jnp.dot(left, right, preferred_element_type=jnp.float32)


def feed_grads(hidden_grad, gate_sum, up_sum, gate_sigmoid):
    gate_grad = (
        hidden_grad * up_sum * gate_sigmoid * (1.0 + gate_sum * (1.0 - gate_sigmoid))
    ).astype(jnp.bfloat16)
    up_grad = (hidden_grad * gate_sum * gate_sigmoid).astype(jnp.bfloat16)
    return (gate_grad, up_grad)


def on_device(
    images,
    counts,
    block_order,
    projector_norm_gain,
    proj_first,
    proj_bias,
    proj_second,
    gate_weight,
    up_weight,
    down_weight,
    cotangent,
):
    group_size = lax.axis_size(("row", "col"))
    per_device = images.shape[0]
    local_rows = cotangent.shape[0]
    total_rows = local_rows * group_size
    position = lax.axis_index(("row", "col"))
    source, target, live = row_tables(counts, block_order, total_rows, per_device, group_size)
    standardized_input, inverse_scale, norm_output = apply_layer_norm(images, projector_norm_gain)
    columns = lax.all_to_all(norm_output, VIS, split_axis=1, concat_axis=0, tiled=True)
    gathered = collect(columns, ("row", "col"), 0)
    first_part = jnp.take(product(gathered, proj_first), source, axis=0)
    pre = total_of_pieces(first_part.astype(jnp.bfloat16), VIS).astype(jnp.float32) + proj_bias
    activated, slope = gelu_parts(pre)
    hidden_proj = activated.astype(jnp.bfloat16)
    inputs = sum_by_parts(
        product(hidden_proj, proj_second).astype(jnp.bfloat16), ("row", "col")
    ).astype(jnp.bfloat16)
    gate_part = product(inputs, gate_weight)
    up_part = product(inputs, up_weight)
    gate_sum, up_sum = (
        sum_by_parts_2(gate_part.astype(jnp.bfloat16), ("vis_0", "vis_1")),
        sum_by_parts_2(up_part.astype(jnp.bfloat16), ("vis_0", "vis_1")),
    )
    gate_sigmoid = jax.nn.sigmoid(gate_sum)
    hidden = (gate_sum * gate_sigmoid * up_sum).astype(jnp.bfloat16)
    block_part = summed_on_arrival(
        product(hidden, down_weight).astype(jnp.bfloat16), ("row", "col"), 0
    )
    own_inputs = lax.dynamic_slice_in_dim(inputs, position * local_rows, local_rows, 0)
    block_out = (own_inputs.astype(jnp.float32) + block_part).astype(jnp.bfloat16)
    upstream = collect(cotangent, ("row", "col"), 0)
    hidden_part = product(upstream, down_weight.T)
    hidden_grad = sum_by_parts(hidden_part.astype(jnp.bfloat16), VIS)
    gate_grad, up_grad = feed_grads(hidden_grad, gate_sum, up_sum, gate_sigmoid)
    input_part = product(gate_grad, gate_weight.T) + product(up_grad, up_weight.T)
    input_grad = (
        upstream.astype(jnp.float32) + sum_by_parts(input_part.astype(jnp.bfloat16), ("row", "col"))
    ).astype(jnp.bfloat16)
    second_grad = product(hidden_proj.T, input_grad)
    pre_part = product(input_grad, proj_second.T)
    pre_grad = total_of_pieces(pre_part.astype(jnp.bfloat16), VIS).astype(jnp.float32)
    act_grad = (pre_grad * slope).astype(jnp.bfloat16)
    slot_act = jnp.where(
        live[:, None], jnp.take(act_grad, target, axis=0), jnp.zeros((), jnp.bfloat16)
    )
    first_grad = product(gathered.T, slot_act)
    slot_part = summed_on_arrival(
        product(slot_act, proj_first.T).astype(jnp.bfloat16), ("row", "col"), 0
    )
    return_values = lax.all_to_all(slot_part, VIS, split_axis=0, concat_axis=1, tiled=True)
    image_slot_gradients = norm_gradient_pass(
        return_values, standardized_input, inverse_scale, projector_norm_gain
    )
    return (block_out, image_slot_gradients, first_grad, second_grad)


def solution(mesh):
    split = Mesh(
        mesh.devices.reshape(8, 2, mesh.shape["row"], mesh.shape["col"]),
        ("vis_0", "vis_1", "row", "col"),
    )
    return jax.shard_map(
        on_device,
        mesh=split,
        in_specs=(
            P(VIS_ROW_COL, None),
            P(),
            P(),
            P(),
            P(VIS, ("row", "col")),
            P(("row", "col")),
            P(("row", "col"), VIS),
            P(VIS, ("row", "col")),
            P(VIS, ("row", "col")),
            P(("row", "col"), VIS),
            P(("row", "col"), VIS),
        ),
        out_specs=(
            P(("row", "col"), VIS),
            P(VIS_ROW_COL, None),
            P(VIS, ("row", "col")),
            P(("row", "col"), VIS),
        ),
        check_vma=False,
    )
```

profile of v0, /device:TPU:1, one launch (start us, length us, event | category | flops | bytes accessed | tf_op | source)
XLA Modules:
  0.0 350.3 jit_solution(11522819560762727879)
XLA Ops:
  13.7 16.7 %all_to_all.120 = bf16[16,2,200]{2,1,0:T(2,128)(2,1)S(1)} all-to-all(bf16[16,2,200]{2,1,0:T(2,128)(2,1)S(1)} %reshape.313), channel_id=1, replica_groups=mesh['vis_0'=8,'vis_1'=2,'row'=4,'col'=8] {'vis_0','vis_1'}, dimensions={0} | all-to-all | bytes 25600 | tf_op jit(solution)/shard_map/all_to_all | solution.py:166
  31.3 11.9 %all-to-all-start.1 = ((bf16[32,16,400]{2,1,0:T(8,128)(2,1)}), bf16[32,16,400]{2,1,0:T(8,128)(2,1)S(1)}, u32[]{:S(2)}, u32[]{:S(2)}) async-start(bf16[32,16,400]{2,1,0:T(8,128)(2,1)} %broadcast_in_dim.52), calls=%async_computation.1 | async-start | bytes 1048576 | tf_op jit(solution)/shard_map/all_to_all | solution.py:19
  44.0 13.4 %all-to-all-done.1 = bf16[32,16,400]{2,1,0:T(8,128)(2,1)S(1)} async-done(((bf16[32,16,400]{2,1,0:T(8,128)(2,1)}), bf16[32,16,400]{2,1,0:T(8,128)(2,1)S(1)}, u32[]{:S(2)}, u32[]{:S(2)}) %all-to-all-start.1) | async-done | bytes 409632 | tf_op jit(solution)/shard_map/all_to_all | solution.py:19
  60.1 8.2 %all-to-all-start.13 = ((bf16[32,8,256]{2,1,0:T(8,128)(2,1)}), bf16[32,8,256]{2,1,0:T(8,128)(2,1)S(1)}, u32[]{:S(2)}, u32[]{:S(2)}) async-start(bf16[32,8,256]{2,1,0:T(8,128)(2,1)} %broadcast_in_dim.61), calls=%async_computation.13 | async-start | bytes 262144 | tf_op jit(solution)/shard_map/all_to_all | solution.py:19
  68.3 27.4 %all-gather.4.cloned.1.call-done = bf16[16,256,128]{2,1,0:T(8,128)(2,1)} async-done(((bf16[1,256,128]{2,1,0:T(8,128)(2,1)}), bf16[16,256,128]{2,1,0:T(8,128)(2,1)}) %all-gather.4.cloned.1.call-update) | async-done | bytes 1048592 | tf_op jit(solution)/shard_map/all_gather | solution.py:29
  98.0 10.0 %all-to-all-start.2 = ((bf16[32,8,256]{2,1,0:T(8,128)(2,1)}), bf16[32,8,256]{2,1,0:T(8,128)(2,1)S(1)}, u32[]{:S(2)}, u32[]{:S(2)}) async-start(bf16[32,8,256]{2,1,0:T(8,128)(2,1)} %fusion.3), calls=%async_computation.2 | async-start | bytes 262144 | tf_op jit(solution)/shard_map/all_to_all | solution.py:40
  108.9 8.2 %all-to-all-done.2 = bf16[32,8,256]{2,1,0:T(8,128)(2,1)S(1)} async-done(((bf16[32,8,256]{2,1,0:T(8,128)(2,1)}), bf16[32,8,256]{2,1,0:T(8,128)(2,1)S(1)}, u32[]{:S(2)}, u32[]{:S(2)}) %all-to-all-start.2) | async-done | bytes 131104 | tf_op jit(solution)/shard_map/all_to_all | solution.py:40
  117.1 6.6 %all-to-all-start.14 = ((bf16[16,16,512]{2,1,0:T(8,128)(2,1)}), bf16[16,16,512]{2,1,0:T(8,128)(2,1)S(1)}, u32[]{:S(2)}, u32[]{:S(2)}) async-start(bf16[16,16,512]{2,1,0:T(8,128)(2,1)} %bitcast.19), calls=%async_computation.14 | async-start | bytes 524288 | tf_op jit(solution)/shard_map/all_to_all | solution.py:40
  123.7 11.7 %all-to-all-done.14 = bf16[16,16,512]{2,1,0:T(8,128)(2,1)S(1)} async-done(((bf16[16,16,512]{2,1,0:T(8,128)(2,1)}), bf16[16,16,512]{2,1,0:T(8,128)(2,1)S(1)}, u32[]{:S(2)}, u32[]{:S(2)}) %all-to-all-start.14) | async-done | bytes 262176 | tf_op jit(solution)/shard_map/all_to_all | solution.py:40
  139.9 9.9 %all-to-all-done.3 = bf16[32,8,256]{2,1,0:T(8,128)(2,1)S(1)} async-done(((bf16[32,8,256]{2,1,0:T(8,128)(2,1)}), bf16[32,8,256]{2,1,0:T(8,128)(2,1)S(1)}, u32[]{:S(2)}, u32[]{:S(2)}) %all-to-all-start.3) | async-done | bytes 131104 | tf_op jit(solution)/shard_map/all_to_all | solution.py:19
  159.5 10.8 %all-to-all-done.15 = bf16[16,16,512]{2,1,0:T(8,128)(2,1)S(1)} async-done(((bf16[16,16,512]{2,1,0:T(8,128)(2,1)}), bf16[16,16,512]{2,1,0:T(8,128)(2,1)S(1)}, u32[]{:S(2)}, u32[]{:S(2)}) %all-to-all-start.15) | async-done | bytes 262176 | tf_op jit(solution)/shard_map/all_to_all | solution.py:19
  178.0 7.6 %all-to-all-done.9 = bf16[8,16,512]{2,1,0:T(8,128)(2,1)S(1)} async-done(((bf16[8,16,512]{2,1,0:T(8,128)(2,1)}), bf16[8,16,512]{2,1,0:T(8,128)(2,1)S(1)}, u32[]{:S(2)}, u32[]{:S(2)}) %all-to-all-start.9) | async-done | bytes 131104 | tf_op jit(solution)/shard_map/all_to_all | solution.py:68
  189.0 7.8 %all-to-all-done.5 = bf16[8,16,512]{2,1,0:T(8,128)(2,1)S(1)} async-done(((bf16[8,16,512]{2,1,0:T(8,128)(2,1)}), bf16[8,16,512]{2,1,0:T(8,128)(2,1)S(1)}, u32[]{:S(2)}, u32[]{:S(2)}) %all-to-all-start.5) | async-done | bytes 131104 | tf_op jit(solution)/shard_map/all_to_all | solution.py:68
  200.9 7.8 %all-to-all-done.10 = bf16[8,16,512]{2,1,0:T(8,128)(2,1)S(1)} async-done(((bf16[8,16,512]{2,1,0:T(8,128)(2,1)}), bf16[8,16,512]{2,1,0:T(8,128)(2,1)S(1)}, u32[]{:S(2)}, u32[]{:S(2)}) %all-to-all-start.10) | async-done | bytes 131104 | tf_op jit(solution)/shard_map/all_to_all | solution.py:19
  208.7 7.5 %all_to_all.123 = bf16[2,8,16,512]{3,2,1,0:T(8,128)(2,1)S(1)} all-to-all(bf16[2,8,16,512]{3,2,1,0:T(8,128)(2,1)S(1)} %broadcast_in_dim.58), channel_id=1, replica_groups=mesh['vis_0'=8,'vis_1'=2,'row'=4,'col'=8] {'vis_1'}, dimensions={0} | all-to-all | bytes 524288 | tf_op jit(solution)/shard_map/all_to_all | solution.py:19
  220.4 8.2 %all-to-all-done.6 = bf16[8,16,512]{2,1,0:T(8,128)(2,1)S(1)} async-done(((bf16[8,16,512]{2,1,0:T(8,128)(2,1)}), bf16[8,16,512]{2,1,0:T(8,128)(2,1)S(1)}, u32[]{:S(2)}, u32[]{:S(2)}) %all-to-all-start.6) | async-done | bytes 131104 | tf_op jit(solution)/shard_map/all_to_all | solution.py:19
  228.6 5.2 %all_to_all.124 = bf16[2,8,16,512]{3,2,1,0:T(8,128)(2,1)S(1)} all-to-all(bf16[2,8,16,512]{3,2,1,0:T(8,128)(2,1)S(1)} %broadcast_in_dim.56), channel_id=1, replica_groups=mesh['vis_0'=8,'vis_1'=2,'row'=4,'col'=8] {'vis_1'}, dimensions={0} | all-to-all | bytes 524288 | tf_op jit(solution)/shard_map/all_to_all | solution.py:19
  234.7 13.4 %all_to_all.125 = bf16[32,8,256]{2,1,0:T(8,128)(2,1)S(1)} all-to-all(bf16[32,8,256]{2,1,0:T(8,128)(2,1)S(1)} %fusion.2), channel_id=1, replica_groups=mesh['vis_0'=8,'vis_1'=2,'row'=4,'col'=8] {'row','col'}, dimensions={0} | all-to-all | bytes 262144 | tf_op jit(solution)/shard_map/all_to_all | solution.py:40
  248.1 13.3 %all_to_all.126 = bf16[32,8,256]{2,1,0:T(8,128)(2,1)S(1)} all-to-all(bf16[32,8,256]{2,1,0:T(8,128)(2,1)S(1)} %broadcast_in_dim.63), channel_id=1, replica_groups=mesh['vis_0'=8,'vis_1'=2,'row'=4,'col'=8] {'row','col'}, dimensions={0} | all-to-all | bytes 262144 | tf_op jit(solution)/shard_map/all_to_all | solution.py:19
  267.3 28.4 %all-gather.6.cloned.1.call-done = bf16[4096,128]{1,0:T(8,128)(2,1)} async-done(((bf16[256,128]{1,0:T(8,128)(2,1)}), bf16[4096,128]{1,0:T(8,128)(2,1)}) %all-gather.6.cloned.1.call-update) | async-done | bytes 1048592 | tf_op jit(solution)/shard_map/all_gather | solution.py:29
  299.9 9.9 %all-to-all-start.18 = ((bf16[32,16,400]{2,1,0:T(8,128)(2,1)}), bf16[32,16,400]{2,1,0:T(8,128)(2,1)S(1)}, u32[]{:S(2)}, u32[]{:S(2)}) async-start(bf16[32,16,400]{2,1,0:T(8,128)(2,1)} %bitcast.28), calls=%async_computation.18 | async-start | bytes 1048576 | tf_op jit(solution)/shard_map/all_to_all | solution.py:40
  311.3 12.5 %all-to-all-done.18 = bf16[32,16,400]{2,1,0:T(8,128)(2,1)S(1)} async-done(((bf16[32,16,400]{2,1,0:T(8,128)(2,1)}), bf16[32,16,400]{2,1,0:T(8,128)(2,1)S(1)}, u32[]{:S(2)}, u32[]{:S(2)}) %all-to-all-start.18) | async-done | bytes 409632 | tf_op jit(solution)/shard_map/all_to_all | solution.py:40
  324.5 8.2 %all-to-all-start.19 = ((f32[16,1,400]{2,1,0:T(1,128)}), f32[16,1,400]{2,1,0:T(1,128)S(1)}, u32[]{:S(2)}, u32[]{:S(2)}) async-start(f32[16,1,400]{2,1,0:T(1,128)} %all_to_all.96), calls=%async_computation.19 | async-start | bytes 65536 | tf_op jit(solution)/shard_map/all_to_all | solution.py:207
  333.8 6.2 %all-to-all-done.19 = f32[16,1,400]{2,1,0:T(1,128)S(1)} async-done(((f32[16,1,400]{2,1,0:T(1,128)}), f32[16,1,400]{2,1,0:T(1,128)S(1)}, u32[]{:S(2)}, u32[]{:S(2)}) %all-to-all-start.19) | async-done | bytes 25632 | tf_op jit(solution)/shard_map/all_to_all | solution.py:207
  (113 shorter events, 62.5 us)
Async XLA Ops:
  7.2 151.4 %copy-start = (bf16[256,512]{1,0:T(8,128)(2,1)S(1)}, bf16[256,512]{1,0:T(8,128)(2,1)}, u32[]{:S(2)}) copy-start(bf16[256,512]{1,0:T(8,128)(2,1)} %param.18) | copy-start | bytes 786436
  7.2 36.2 %copy-start.9 = (s32[16]{0:T(128)S(1)}, s32[16]{0:T(128)}, u32[]{:S(2)}) copy-start(s32[16]{0:T(128)} %param.12) | copy-start | bytes 196
  7.2 36.2 %copy-start.10 = (s32[16]{0:T(128)S(1)}, s32[16]{0:T(128)}, u32[]{:S(2)}) copy-start(s32[16]{0:T(128)} %param.13) | copy-start | bytes 196
  7.2 50.3 %copy-start.4 = (bf16[400,128]{1,0:T(8,128)(2,1)S(1)}, bf16[400,128]{1,0:T(8,128)(2,1)}, u32[]{:S(2)}) copy-start(bf16[400,128]{1,0:T(8,128)(2,1)} %param.15) | copy-start | bytes 307204
  31.3 26.1 %all-to-all-start.1 = ((bf16[32,16,400]{2,1,0:T(8,128)(2,1)}), bf16[32,16,400]{2,1,0:T(8,128)(2,1)S(1)}, u32[]{:S(2)}, u32[]{:S(2)}) async-start(bf16[32,16,400]{2,1,0:T(8,128)(2,1)} %broadcast_in_dim.52), calls=%async_computation.1 | async-start | bytes 1048576 | tf_op jit(solution)/shard_map/all_to_all | solution.py:19
  43.3 52.4 %all-gather.4.cloned.1.call-start = ((), (), s32[]{:S(2)}) async-start(), calls=%async_computation.20 | async-start | bytes 1114112 | tf_op jit(solution)/shard_map/all_gather | solution.py:29
  57.8 39.3 %copy-start.8 = (f32[128]{0:T(128)S(1)}, f32[128]{0:T(128)}, u32[]{:S(2)}) copy-start(f32[128]{0:T(128)} %param.16) | copy-start | bytes 1540
  58.6 38.5 %copy-start.5 = (bf16[128,256]{1,0:T(8,128)(2,1)S(1)}, bf16[128,256]{1,0:T(8,128)(2,1)}, u32[]{:S(2)}) copy-start(bf16[128,256]{1,0:T(8,128)(2,1)} %param.17) | copy-start | bytes 196612
  60.1 47.9 %copy-start.2 = (bf16[512,256]{1,0:T(8,128)(2,1)S(1)}, bf16[512,256]{1,0:T(8,128)(2,1)}, u32[]{:S(2)}) copy-start(bf16[512,256]{1,0:T(8,128)(2,1)} %param.20) | copy-start | bytes 786436
  60.1 37.9 %all-to-all-start.13 = ((bf16[32,8,256]{2,1,0:T(8,128)(2,1)}), bf16[32,8,256]{2,1,0:T(8,128)(2,1)S(1)}, u32[]{:S(2)}, u32[]{:S(2)}) async-start(bf16[32,8,256]{2,1,0:T(8,128)(2,1)} %broadcast_in_dim.61), calls=%async_computation.13 | async-start | bytes 262144 | tf_op jit(solution)/shard_map/all_to_all | solution.py:19
  98.0 19.1 %all-to-all-start.2 = ((bf16[32,8,256]{2,1,0:T(8,128)(2,1)}), bf16[32,8,256]{2,1,0:T(8,128)(2,1)S(1)}, u32[]{:S(2)}, u32[]{:S(2)}) async-start(bf16[32,8,256]{2,1,0:T(8,128)(2,1)} %fusion.3), calls=%async_computation.2 | async-start | bytes 262144 | tf_op jit(solution)/shard_map/all_to_all | solution.py:40
  108.0 41.9 %copy-start.1 = (bf16[256,512]{1,0:T(8,128)(2,1)S(1)}, bf16[256,512]{1,0:T(8,128)(2,1)}, u32[]{:S(2)}) copy-start(bf16[256,512]{1,0:T(8,128)(2,1)} %param.19) | copy-start | bytes 786436
  117.1 18.3 %all-to-all-start.14 = ((bf16[16,16,512]{2,1,0:T(8,128)(2,1)}), bf16[16,16,512]{2,1,0:T(8,128)(2,1)S(1)}, u32[]{:S(2)}, u32[]{:S(2)}) async-start(bf16[16,16,512]{2,1,0:T(8,128)(2,1)} %bitcast.19), calls=%async_computation.14 | async-start | bytes 524288 | tf_op jit(solution)/shard_map/all_to_all | solution.py:40
  136.0 13.8 %all-to-all-start.3 = ((bf16[32,8,256]{2,1,0:T(8,128)(2,1)}), bf16[32,8,256]{2,1,0:T(8,128)(2,1)S(1)}, u32[]{:S(2)}, u32[]{:S(2)}) async-start(bf16[32,8,256]{2,1,0:T(8,128)(2,1)} %broadcast_in_dim.54), calls=%async_computation.3 | async-start | bytes 262144 | tf_op jit(solution)/shard_map/all_to_all | solution.py:19
  154.8 15.5 %all-to-all-start.15 = ((bf16[16,16,512]{2,1,0:T(8,128)(2,1)}), bf16[16,16,512]{2,1,0:T(8,128)(2,1)S(1)}, u32[]{:S(2)}, u32[]{:S(2)}) async-start(bf16[16,16,512]{2,1,0:T(8,128)(2,1)} %broadcast_in_dim.62), calls=%async_computation.15 | async-start | bytes 524288 | tf_op jit(solution)/shard_map/all_to_all | solution.py:19
  173.9 11.7 %all-to-all-start.9 = ((bf16[8,16,512]{2,1,0:T(8,128)(2,1)}), bf16[8,16,512]{2,1,0:T(8,128)(2,1)S(1)}, u32[]{:S(2)}, u32[]{:S(2)}) async-start(bf16[8,16,512]{2,1,0:T(8,128)(2,1)} %reduce_sum.239), calls=%async_computation.9 | async-start | bytes 262144 | tf_op jit(solution)/shard_map/all_to_all | solution.py:68
  185.6 11.2 %all-to-all-start.5 = ((bf16[8,16,512]{2,1,0:T(8,128)(2,1)}), bf16[8,16,512]{2,1,0:T(8,128)(2,1)S(1)}, u32[]{:S(2)}, u32[]{:S(2)}) async-start(bf16[8,16,512]{2,1,0:T(8,128)(2,1)} %reduce_sum.237), calls=%async_computation.5 | async-start | bytes 262144 | tf_op jit(solution)/shard_map/all_to_all | solution.py:68
  197.5 11.2 %all-to-all-start.10 = ((bf16[8,16,512]{2,1,0:T(8,128)(2,1)}), bf16[8,16,512]{2,1,0:T(8,128)(2,1)S(1)}, u32[]{:S(2)}, u32[]{:S(2)}) async-start(bf16[8,16,512]{2,1,0:T(8,128)(2,1)} %broadcast_in_dim.57), calls=%async_computation.10 | async-start | bytes 262144 | tf_op jit(solution)/shard_map/all_to_all | solution.py:19
  216.9 11.7 %all-to-all-start.6 = ((bf16[8,16,512]{2,1,0:T(8,128)(2,1)}), bf16[8,16,512]{2,1,0:T(8,128)(2,1)S(1)}, u32[]{:S(2)}, u32[]{:S(2)}) async-start(bf16[8,16,512]{2,1,0:T(8,128)(2,1)} %broadcast_in_dim.55), calls=%async_computation.6 | async-start | bytes 262144 | tf_op jit(solution)/shard_map/all_to_all | solution.py:19
  220.3 75.4 %all-gather.6.cloned.1.call-start = ((), (), s32[]{:S(2)}) async-start(), calls=%async_computation.21 | async-start | bytes 1114112 | tf_op jit(solution)/shard_map/all_gather | solution.py:29
  263.4 36.5 %all-to-all-start.12 = ((bf16[32,8,256]{2,1,0:T(8,128)(2,1)}), bf16[32,8,256]{2,1,0:T(8,128)(2,1)S(1)}, u32[]{:S(2)}, u32[]{:S(2)}) async-start(bf16[32,8,256]{2,1,0:T(8,128)(2,1)} %fusion.1), calls=%async_computation.12 | async-start | bytes 262144 | tf_op jit(solution)/shard_map/all_to_all | solution.py:40
  299.9 23.9 %all-to-all-start.18 = ((bf16[32,16,400]{2,1,0:T(8,128)(2,1)}), bf16[32,16,400]{2,1,0:T(8,128)(2,1)S(1)}, u32[]{:S(2)}, u32[]{:S(2)}) async-start(bf16[32,16,400]{2,1,0:T(8,128)(2,1)} %bitcast.28), calls=%async_computation.18 | async-start | bytes 1048576 | tf_op jit(solution)/shard_map/all_to_all | solution.py:40
  310.5 31.1 %copy-start.3 = (bf16[1,6400]{1,0:T(2,128)(2,1)S(1)}, bf16[1,6400]{1,0:T(2,128)(2,1)}, u32[]{:S(2)}) copy-start(bf16[1,6400]{1,0:T(2,128)(2,1)} %param.11) | copy-start | bytes 38404
  324.5 15.6 %all-to-all-start.19 = ((f32[16,1,400]{2,1,0:T(1,128)}), f32[16,1,400]{2,1,0:T(1,128)S(1)}, u32[]{:S(2)}, u32[]{:S(2)}) async-start(f32[16,1,400]{2,1,0:T(1,128)} %all_to_all.96), calls=%async_computation.19 | async-start | bytes 65536 | tf_op jit(solution)/shard_map/all_to_all | solution.py:207
  (2 other events, 45.9 us)
Sparse Core Ops, SparseCore 0:
  59.5 36.1 all-gather.3
  262.4 33.1 all-gather.5
where the time goes:
time: 352 us; the launch traced here: 350 us
  waiting for transfers between devices  160 us (45%)
  starting transfers between devices  79.8 us (23%)
  blocking collectives  63.6 us (18%)
  between operations  17.1 us (5%)
  other arithmetic  13.5 us (4%)
  local copies, waits for them, and re-layouts  9.19 us (3%)
  matrix products  7.19 us (2%)
    all_gather x2, waiting for transfers between devices, total_of_pieces(): blocks = lax.all_gather(shard, axis).astype(jnp.float32)  55.8 us
    all_to_all x6, waiting for transfers between devices, sent_to_all(): lax.all_to_all(jnp.broadcast_to(shard[None], (length, *shard.shape)), axi...  50.1 us
    all_to_all x6, starting transfers between devices, sent_to_all(): lax.all_to_all(jnp.broadcast_to(shard[None], (length, *shard.shape)), axi...  34.6 us
    all_to_all x4, waiting for transfers between devices, summed_on_arrival(): lax.all_to_all(in_blocks(shard, dim, length), axis, 0, 0, tiled=True)  32.3 us
    all_to_all x4, starting transfers between devices, summed_on_arrival(): lax.all_to_all(in_blocks(shard, dim, length), axis, 0, 0, tiled=True)  30.3 us
    all_to_all x3, blocking collectives, sent_to_all(): lax.all_to_all(jnp.broadcast_to(shard[None], (length, *shard.shape)), axi...  26 us
    all_to_all x3, blocking collectives, summed_on_arrival(): lax.all_to_all(in_blocks(shard, dim, length), axis, 0, 0, tiled=True)  20.9 us
    all_to_all x1, blocking collectives, on_device(): lax.all_to_all(norm_output, VIS, split_axis=1, concat_axis=0, tiled=True)  16.7 us
  transfers between devices with their start and end apart: 15, of which 13 were waited for; matrix products, arithmetic and copies ran while one was open for 4% of the time, Pallas kernels for 0%

commit v1 on v0

v1 whole, which is shorter than its diff:
```python
import functools

import jax
import jax.numpy as jnp
from jax import lax
from jax.experimental import pallas as pl
from jax.experimental.pallas import tpu as pltpu
from jax.sharding import PartitionSpec as P

VIS = 16
RC = 32
CAP = 32
SPLIT = 400
LANES = 512
F32 = jnp.float32
BF16 = jnp.bfloat16
GROUP = ("row", "col")


def vmem():
    return pl.BlockSpec(memory_space=pltpu.VMEM)


def smem():
    return pl.BlockSpec(memory_space=pltpu.SMEM)


def struct(shape, dtype):
    return jax.ShapeDtypeStruct(shape, dtype)


def params():
    return pltpu.CompilerParams(vmem_limit_bytes=40 * 1024 * 1024)


def dot(a, b, ca=1, cb=0):
    return lax.dot_general(a, b, (((ca,), (cb,)), ((), ())), preferred_element_type=F32)


def block_starts(counts_ref, order_ref, starts):
    def body(j, total):
        block = order_ref[j]
        starts[block] = total
        return total + counts_ref[block]

    lax.fori_loop(0, VIS, body, jnp.int32(0))


def pack_kernel(gate_ref, up_ref, down_ref, first_ref, out_ref):
    out_ref[0:256, :] = gate_ref[:, 0:256]
    out_ref[256:512, :] = gate_ref[:, 256:512]
    out_ref[512:768, :] = up_ref[:, 0:256]
    out_ref[768:1024, :] = up_ref[:, 256:512]
    out_ref[1024:1536, :] = down_ref[...]
    out_ref[1536:1792, 0:128] = first_ref[0:256, :]
    out_ref[1536:1680, 128:256] = first_ref[256:400, :]
    out_ref[1680:1792, 128:256] = jnp.zeros((112, 128), BF16)


def norm_kernel(images_ref, gain_ref, message_ref, hat_ref, gain_out, scale_ref, values, gains):
    values[...] = jnp.zeros_like(values)
    gains[...] = jnp.zeros_like(gains)
    row = images_ref[...].astype(F32)
    gain_row = gain_ref[...]
    for v in range(VIS):
        values[v : v + 1, 0:SPLIT] = row[:, v * SPLIT : (v + 1) * SPLIT]
        gains[v : v + 1, 0:SPLIT] = gain_row[:, v * SPLIT : (v + 1) * SPLIT]
    inside = lax.broadcasted_iota(jnp.int32, (VIS, LANES), 1) < SPLIT
    x = values[...]
    mean = jnp.sum(x, keepdims=True) * (1.0 / (VIS * SPLIT))
    centred = jnp.where(inside, x - mean, 0.0)
    variance = jnp.sum(centred * centred, keepdims=True) * (1.0 / (VIS * SPLIT))
    scale = lax.rsqrt(variance + 1e-05)
    hat = centred * scale
    hat_ref[...] = hat
    gain_out[...] = gains[...]
    scale_ref[...] = jnp.broadcast_to(scale, scale_ref.shape)
    normed = (hat * gains[...]).astype(BF16).astype(F32)
    message_ref[...] = jnp.zeros_like(message_ref)
    for j in range(4):
        message_ref[:, j, :] = normed[:, 128 * j : 128 * j + 128]


def spread_kernel(arrived_ref, cotangent_ref, out_ref):
    parts = [arrived_ref[:, j, :] for j in range(4)]
    cot = cotangent_ref[...].astype(F32)
    parts.append(jnp.concatenate([cot[:, 0:128], cot[:, 128:256]], axis=0))
    block = jnp.concatenate(parts, axis=1).astype(BF16)
    for r in range(RC):
        out_ref[r] = block


def first_kernel(counts_ref, order_ref, rows_ref, first_ref, out_ref, weight, sums, chosen, starts):
    block_starts(counts_ref, order_ref, starts)
    weight[SPLIT:LANES, :] = jnp.zeros((LANES - SPLIT, 128), BF16)
    weight[0:SPLIT, :] = first_ref[...]
    rows = rows_ref[:, :, 0:LANES].reshape(RC * VIS, LANES)
    sums[...] = dot(rows, weight[...])
    language = lax.broadcasted_iota(jnp.int32, (CAP, 256), 1)
    slot = lax.broadcasted_iota(jnp.int32, (CAP, 256), 0)
    for v in range(VIS):
        hit = jnp.logical_and(slot < counts_ref[v], language == slot + starts[v])
        chosen[v * CAP : (v + 1) * CAP, :] = jnp.where(hit, 1.0, 0.0).astype(BF16)
    cot = rows_ref[:, :, LANES : LANES + 128].astype(F32)
    cot = jnp.concatenate(
        [cot[:, 0:8, :].reshape(256, 128), cot[:, 8:16, :].reshape(256, 128)], axis=1
    ).astype(BF16)
    placed = dot(chosen[...], cot).astype(BF16)
    for v in range(VIS):
        out_ref[v, :, 0:256] = placed[v * CAP : (v + 1) * CAP, :]
        out_ref[v, :, 256:384] = sums[pl.ds(v, CAP, stride=VIS), :].astype(BF16)


def second_kernel(arrived_ref, bias_ref, weight_ref, out_ref, hidden_ref, slope_ref):
    pre = jnp.zeros((CAP, 128), F32)
    for v in range(VIS):
        pre = pre + arrived_ref[v, :, 256:384].astype(F32)
    pre = pre + bias_ref[...]
    cdf = 0.5 * (1.0 + lax.erf(pre * 0.7071067811865476))
    density = jnp.exp(-0.5 * pre * pre) * 0.3989422804014327
    hidden = (pre * cdf).astype(BF16)
    hidden_ref[...] = hidden
    slope_ref[...] = cdf + pre * density
    for v in range(VIS):
        y = dot(hidden, weight_ref[v]).astype(BF16)
        out_ref[2 * v] = y[:, 0:128]
        out_ref[2 * v + 1] = y[:, 128:256]


def input_sum_kernel(arrived_ref, out_ref, own_ref):
    total = jnp.zeros((CAP, 128), F32)
    for r in range(RC):
        total = total + arrived_ref[r].astype(F32)
    own = total.astype(BF16)
    own_ref[...] = own
    for r in range(RC):
        out_ref[r] = own


def block_kernel(inputs_ref, cot_ref, w_ref, out_ref, gate, up, grad, gate_b, up_b, hidden_b):
    phase = pl.program_id(0)
    v = pl.program_id(1)

    @pl.when(jnp.logical_and(phase == 0, v == 0))
    def _():
        gate[...] = jnp.zeros_like(gate)
        up[...] = jnp.zeros_like(up)
        grad[...] = jnp.zeros_like(grad)

    @pl.when(phase == 0)
    def _():
        x = jnp.concatenate([inputs_ref[0], inputs_ref[1]], axis=1)
        cot = cot_ref[0, :, 0:256]
        gate[:, 0:256] += dot(x, w_ref[0, 0:256, :])
        gate[:, 256:512] += dot(x, w_ref[0, 256:512, :])
        up[:, 0:256] += dot(x, w_ref[0, 512:768, :])
        up[:, 256:512] += dot(x, w_ref[0, 768:1024, :])
        grad[...] += dot(cot, w_ref[0, 1024:1536, :], 1, 1)

    @pl.when(jnp.logical_and(phase == 1, v == 0))
    def _():
        g, u, h = gate[...], up[...], grad[...]
        s = jax.nn.sigmoid(g)
        hidden_b[...] = (g * s * u).astype(BF16)
        gate_b[...] = (h * u * s * (1.0 + g * (1.0 - s))).astype(BF16)
        up_b[...] = (h * g * s).astype(BF16)

    @pl.when(phase == 1)
    def _():
        y = dot(gate_b[:, 0:256], w_ref[0, 0:256, :], 1, 1)
        y += dot(gate_b[:, 256:512], w_ref[0, 256:512, :], 1, 1)
        y += dot(up_b[:, 0:256], w_ref[0, 512:768, :], 1, 1)
        y += dot(up_b[:, 256:512], w_ref[0, 768:1024, :], 1, 1)
        y = y.astype(BF16)
        z = dot(hidden_b[...], w_ref[0, 1024:1536, :]).astype(BF16)
        out_ref[0, 0:32, :] = y[:, 0:128]
        out_ref[1, 0:32, :] = y[:, 128:256]
        out_ref[0, 32:64, :] = z[:, 0:128]
        out_ref[1, 32:64, :] = z[:, 128:256]


def grad_sum_kernel(arrived_ref, cot_ref, own_ref, out_ref):
    r = lax.axis_index("row") * 8 + lax.axis_index("col")
    total = jnp.zeros((2 * CAP, 128), F32)
    for i in range(RC):
        total = total + arrived_ref[i].astype(F32)
    pair = cot_ref[r // 2]
    cot = jnp.where(r % 2 == 0, pair[:, 0:128].astype(F32), pair[:, 128:256].astype(F32))
    added = jnp.concatenate([cot, own_ref[...].astype(F32)], axis=0)
    result = (total + added).astype(BF16)
    for i in range(RC):
        out_ref[i] = result


def back_kernel(grad_ref, second_ref, slope_ref, hidden_ref, first_ref, sent_ref, slots_ref, spread):
    acc = jnp.zeros((CAP, 128), F32)
    for v in range(VIS):
        ig = jnp.concatenate([grad_ref[2 * v, 0:32, :], grad_ref[2 * v + 1, 0:32, :]], axis=1)
        acc = acc + dot(ig, second_ref[v], 1, 1)
    act = (acc * slope_ref[...]).astype(BF16)
    both = jnp.concatenate([hidden_ref[...], act], axis=1)
    for v in range(VIS):
        sent_ref[v] = both
    for v in range(VIS):
        for half in range(2):
            y = dot(act, first_ref[v, :, 128 * half : 128 * half + 128], 1, 1)
            spread[2 * half, pl.ds(v, CAP, stride=VIS), :] = y[:, 0:128]
            spread[2 * half + 1, pl.ds(v, CAP, stride=VIS), :] = y[:, 128:256]
    for k in range(4):
        slots_ref[:, :, 128 * k : 128 * k + 128] = spread[k].astype(BF16).reshape(CAP, VIS, 128)


def weight_grad_kernel(
    counts_ref, order_ref, block_ref, act_ref, rows_ref, first_ref, second_ref, out_ref, acts, starts
):
    block_starts(counts_ref, order_ref, starts)
    hidden = act_ref[:, :, 0:128].reshape(VIS * CAP, 128)
    ig = jnp.concatenate(
        [block_ref[:, 0, 0:32, :].reshape(512, 128), block_ref[:, 1, 0:32, :].reshape(512, 128)], axis=1
    )
    second_ref[...] = dot(hidden, ig, 0, 0)
    for v in range(VIS):
        acts[pl.ds(v, CAP, stride=VIS), :] = act_ref[v, :, 128:256].astype(F32)
    rows = rows_ref[:, :, 0:LANES].reshape(RC * VIS, LANES)
    first_ref[...] = dot(rows, acts[...].astype(BF16), 0, 0)[0:SPLIT, :]
    r = lax.axis_index("row") * 8 + lax.axis_index("col")
    lane = lax.broadcasted_iota(jnp.int32, (8, VIS * CAP), 1)
    want = lax.broadcasted_iota(jnp.int32, (8, VIS * CAP), 0) + r * 8
    hit = jnp.zeros((8, VIS * CAP), F32)
    for v in range(VIS):
        slot = lane - v * CAP
        here = jnp.logical_and(slot >= 0, slot < counts_ref[v])
        hit = hit + jnp.where(jnp.logical_and(here, slot + starts[v] == want), 1.0, 0.0)
    out = jnp.concatenate(
        [block_ref[:, 0, 32:64, :].reshape(512, 128), block_ref[:, 1, 32:64, :].reshape(512, 128)], axis=1
    )
    out_ref[...] = dot(hit.astype(BF16), out).astype(BF16)


def norm_back_kernel(arrived_ref, hat_ref, gain_ref, scale_ref, out_ref):
    total = jnp.zeros((VIS, LANES), F32)
    for r in range(RC):
        total = total + arrived_ref[r].astype(F32)
    hat = hat_ref[...]
    g = total * gain_ref[...]
    inside = lax.broadcasted_iota(jnp.int32, (VIS, LANES), 1) < SPLIT
    g = jnp.where(inside, g, 0.0)
    mean = jnp.sum(g, keepdims=True) * (1.0 / (VIS * SPLIT))
    cross = jnp.sum(g * hat, keepdims=True) * (1.0 / (VIS * SPLIT))
    result = scale_ref[0:1, 0:1] * (g - mean - hat * cross)
    for v in range(VIS):
        out_ref[:, v * SPLIT : (v + 1) * SPLIT] = result[v : v + 1, 0:SPLIT]


def call(kernel, outs, ins, scratch=(), cost=0):
    return pl.pallas_call(
        kernel,
        out_shape=outs,
        in_specs=ins,
        out_specs=jax.tree.map(lambda _: vmem(), outs),
        scratch_shapes=list(scratch),
        compiler_params=params(),
        cost_estimate=pl.CostEstimate(flops=1000, bytes_accessed=cost, transcendentals=0) if cost else None,
    )


def swap(blocks, axes):
    return lax.all_to_all(blocks, axes, 0, 0, tiled=True)


def on_device(
    images, counts, block_order, gain, proj_first, bias, proj_second, gate_w, up_w, down_w, cotangent
):
    packed = call(pack_kernel, struct((1792, 256), BF16), [vmem()] * 4)(gate_w, up_w, down_w, proj_first)
    weights = lax.all_gather(packed, "vis")
    message, hat, gains, scale = call(
        norm_kernel,
        (
            struct((VIS, 8, 128), F32),
            struct((VIS, LANES), F32),
            struct((VIS, LANES), F32),
            struct((8, 128), F32),
        ),
        [vmem()] * 2,
        [pltpu.VMEM((VIS, LANES), F32), pltpu.VMEM((VIS, LANES), F32)],
    )(images, gain.reshape(1, -1))
    arrived = swap(message, "vis")
    spread = call(spread_kernel, struct((RC, VIS, 640), BF16), [vmem()] * 2)(arrived, cotangent)
    rows = swap(spread, GROUP)
    seconds = swap(jnp.broadcast_to(proj_second[None], (VIS, 128, 256)), "vis")
    partial = call(
        first_kernel,
        struct((VIS, CAP, 384), BF16),
        [smem(), smem(), vmem(), vmem()],
        [
            pltpu.VMEM((LANES, 128), BF16),
            pltpu.VMEM((RC * VIS, 128), F32),
            pltpu.VMEM((VIS * CAP, 256), BF16),
            pltpu.SMEM((VIS,), jnp.int32),
        ],
    )(counts, block_order, rows, proj_first)
    pieces = swap(partial, "vis")
    input_part, hidden_proj, slope = call(
        second_kernel,
        (struct((RC, CAP, 128), BF16), struct((CAP, 128), BF16), struct((CAP, 128), F32)),
        [vmem()] * 3,
    )(pieces, bias.reshape(1, -1), seconds)
    arrived = swap(input_part, GROUP)
    spread, own = call(
        input_sum_kernel, (struct((RC, CAP, 128), BF16), struct((CAP, 128), BF16)), [vmem()]
    )(arrived)
    inputs = swap(spread, GROUP)
    block_part = pl.pallas_call(
        block_kernel,
        out_shape=struct((RC, 2 * CAP, 128), BF16),
        grid=(2, VIS),
        in_specs=[
            pl.BlockSpec((2, CAP, 128), lambda p, v: ((1 - p) * v, 0, 0)),
            pl.BlockSpec((1, CAP, 384), lambda p, v: ((1 - p) * v, 0, 0)),
            pl.BlockSpec((1, 1536, 256), lambda p, v: (v, 0, 0)),
        ],
        out_specs=pl.BlockSpec((2, 2 * CAP, 128), lambda p, v: (p * v, 0, 0)),
        scratch_shapes=[pltpu.VMEM((CAP, 512), F32)] * 3 + [pltpu.VMEM((CAP, 512), BF16)] * 3,
        compiler_params=params(),
    )(inputs, pieces, weights)
    arrived = swap(block_part, GROUP)
    spread = call(grad_sum_kernel, struct((RC, 2 * CAP, 128), BF16), [vmem()] * 3)(arrived, pieces, own)
    whole = swap(spread, GROUP)
    blocks = swap(whole.reshape(VIS, 4 * CAP, 128), "vis")
    sent, slot_part = pl.pallas_call(
        back_kernel,
        grid=(1,),
        out_shape=(struct((VIS, CAP, 256), BF16), struct((CAP, VIS, LANES), BF16)),
        in_specs=[
            pl.BlockSpec((RC, 2 * CAP, 128), lambda i: (0, 0, 0)),
            pl.BlockSpec((VIS, 128, 256), lambda i: (0, 0, 0)),
            pl.BlockSpec((CAP, 128), lambda i: (0, 0)),
            pl.BlockSpec((CAP, 128), lambda i: (0, 0)),
            pl.BlockSpec((VIS, 256, 256), lambda i: (0, 6, 0)),
        ],
        out_specs=(
            pl.BlockSpec((VIS, CAP, 256), lambda i: (0, 0, 0)),
            pl.BlockSpec((CAP, VIS, LANES), lambda i: (0, 0, 0)),
        ),
        scratch_shapes=[pltpu.VMEM((4, CAP * VIS, 128), F32)],
        compiler_params=params(),
    )(whole, seconds, slope, hidden_proj, weights)
    slots = swap(slot_part, GROUP)
    acts = swap(sent, "vis")
    first_grad, second_grad, block_out = call(
        weight_grad_kernel,
        (struct((SPLIT, 128), F32), struct((128, 256), F32), struct((8, 256), BF16)),
        [smem(), smem(), vmem(), vmem(), vmem()],
        [pltpu.VMEM((RC * VIS, 128), F32), pltpu.SMEM((VIS,), jnp.int32)],
    )(counts, block_order, blocks.reshape(VIS, 2, 2 * CAP, 128), acts, rows)
    image_grad = call(norm_back_kernel, struct((1, VIS * SPLIT), F32), [vmem()] * 4)(
        slots, hat, gains, scale
    )
    return block_out, image_grad, first_grad, second_grad


def solution(mesh):
    every = ("vis", "row", "col")
    return jax.shard_map(
        on_device,
        mesh=mesh,
        in_specs=(
            P(every, None),
            P(),
            P(),
            P(),
            P("vis", GROUP),
            P(GROUP),
            P(GROUP, "vis"),
            P("vis", GROUP),
            P("vis", GROUP),
            P(GROUP, "vis"),
            P(GROUP, "vis"),
        ),
        out_specs=(P(GROUP, "vis"), P(every, None), P("vis", GROUP), P(GROUP, "vis")),
        check_vma=False,
    )
```

time: 352 us -> 302 us (0.86)
  blocking collectives: 63.6 us -> 180 us
  waiting for transfers between devices: 160 us -> 49.2 us
  starting transfers between devices: 79.8 us -> 12.3 us
  Pallas kernels: 0 us -> 34 us
  other arithmetic: 13.5 us -> 0 us
  matrix products: 7.19 us -> 0 us
    all_to_all x7 -> x9, blocking collectives: 63.6 us -> 180 us  [swap(): return lax.all_to_all(blocks, axes, 0, 0, tiled=True)]
    all_to_all x13 -> x2, starting transfers between devices: 79.8 us -> 12.2 us  [swap(): return lax.all_to_all(blocks, axes, 0, 0, tiled=True)]
    all_gather x2 -> x1, waiting for transfers between devices: 55.8 us -> 0.01 us  [on_device(): weights = lax.all_gather(packed, 'vis')]
    all_to_all x13 -> x2, waiting for transfers between devices: 104 us -> 49.2 us  [swap(): return lax.all_to_all(blocks, axes, 0, 0, tiled=True)]
    pallas_call x0 -> x11, Pallas kernels: none -> 34 us  [the longest x1 24.3 us: on_device(): pl.pallas_call(block_kernel, out_shape=struct((RC, 2 * CAP, 128), BF16),...]
    reduce_sum x20 -> x0, other arithmetic: 9.13 us -> none  [the longest x2 2.75 us: total_of_pieces(): return blocks.sum(axis=0)]
    unnamed x26 -> x24, local copies, waits for them, and re-layouts: 0.76 us -> 8.03 us
    dot_general x12 -> x0, matrix products: 7.19 us -> none  [product(): return jnp.dot(left, right, preferred_element_type=jnp.float32)]
  transfers between devices with their start and end apart: 15 -> 3, of which waited for: 13 -> 2; matrix products, arithmetic and copies ran while one was open for 4% -> 1% of each run, Pallas kernels for 0% -> 1%
where the time goes in v1:
time: 302 us; the launch traced here: 300 us
  blocking collectives  180 us (60%)
  waiting for transfers between devices  49.2 us (16%)
  Pallas kernels  34 us (11%)
  between operations  14.2 us (5%)
  starting transfers between devices  12.3 us (4%)
  local copies, waits for them, and re-layouts  10.7 us (4%)
    all_to_all x9, blocking collectives, swap(): return lax.all_to_all(blocks, axes, 0, 0, tiled=True)  180 us
    all_to_all x2, waiting for transfers between devices, swap(): return lax.all_to_all(blocks, axes, 0, 0, tiled=True)  49.2 us
    pallas_call x1, Pallas kernels, on_device(): pl.pallas_call(block_kernel, out_shape=struct((RC, 2 * CAP, 128), BF16),...  24.3 us
    all_to_all x2, starting transfers between devices, swap(): return lax.all_to_all(blocks, axes, 0, 0, tiled=True)  12.2 us
    unnamed x24, local copies, waits for them, and re-layouts  8.03 us
  transfers between devices with their start and end apart: 3, of which 2 were waited for; matrix products, arithmetic and copies ran while one was open for 1% of the time, Pallas kernels for 1%

profile of v1, /device:TPU:1, one launch (start us, length us, event | category | flops | bytes accessed | tf_op | source)
XLA Modules:
  0.0 300.1 jit_solution(9039498949819544947)
XLA Ops:
  8.1 0.9 copy-done.2
  9.1 0.9 copy-done.3
  10.0 0.9 copy-done.4
  11.0 1.0 shard_map.143
  13.9 17.1 %all_to_all.55.arrived_ref = f32[16,8,128]{2,1,0:T(8,128)S(1)} all-to-all(f32[16,8,128]{2,1,0:T(8,128)S(1)} %get-tuple-element.18), channel_id=1, replica_groups=mesh['vis'=16,'row'=4,'col'=8] {'vis'}, dimensions={0} | all-to-all | bytes 131072 | tf_op jit(solution)/shard_map/all_to_all | solution.py:268
  31.8 29.0 %all_to_all.56.rows_ref = bf16[32,16,640]{2,1,0:T(8,128)(2,1)S(1)} all-to-all(bf16[32,16,640]{2,1,0:T(8,128)(2,1)S(1)} %shard_map.139), channel_id=1, replica_groups=mesh['vis'=16,'row'=4,'col'=8] {'row','col'}, dimensions={0} | all-to-all | bytes 1310720 | tf_op jit(solution)/shard_map/all_to_all | solution.py:268
  60.8 1.9 broadcast_in_dim.2
  62.7 6.8 %all-to-all-start.3 = ((bf16[16,128,256]{2,1,0:T(8,128)(2,1)}), bf16[16,128,256]{2,1,0:T(8,128)(2,1)S(1)}, u32[]{:S(2)}, u32[]{:S(2)}) async-start(bf16[16,128,256]{2,1,0:T(8,128)(2,1)} %broadcast_in_dim.2), calls=%async_computation.3 | async-start | bytes 2097152 | tf_op jit(solution)/shard_map/all_to_all | solution.py:268
  69.5 0.9 copy-done.1
  71.7 1.1 shard_map.140
  72.8 34.4 %all-to-all-done.3.weight_ref.second_ref = bf16[16,128,256]{2,1,0:T(8,128)(2,1)S(1)} async-done(((bf16[16,128,256]{2,1,0:T(8,128)(2,1)}), bf16[16,128,256]{2,1,0:T(8,128)(2,1)S(1)}, u32[]{:S(2)}, u32[]{:S(2)}) %all-to-all-start.3) | async-done | bytes 1048608 | tf_op jit(solution)/shard_map/all_to_all | solution.py:268
  107.2 23.4 %all_to_all.57.arrived_ref.cot_ref = bf16[16,32,384]{2,1,0:T(8,128)(2,1)S(1)} all-to-all(bf16[16,32,384]{2,1,0:T(8,128)(2,1)S(1)} %shard_map.140), channel_id=1, replica_groups=mesh['vis'=16,'row'=4,'col'=8] {'vis'}, dimensions={0} | all-to-all | bytes 786432 | tf_op jit(solution)/shard_map/all_to_all | solution.py:268
  131.6 15.7 %all_to_all.58.arrived_ref = bf16[32,32,128]{2,1,0:T(8,128)(2,1)S(1)} all-to-all(bf16[32,32,128]{2,1,0:T(8,128)(2,1)S(1)} %get-tuple-element.19), channel_id=1, replica_groups=mesh['vis'=16,'row'=4,'col'=8] {'row','col'}, dimensions={0} | all-to-all | bytes 524288 | tf_op jit(solution)/shard_map/all_to_all | solution.py:268
  147.4 15.5 %all_to_all.59.inputs_ref = bf16[32,32,128]{2,1,0:T(8,128)(2,1)S(1)} all-to-all(bf16[32,32,128]{2,1,0:T(8,128)(2,1)S(1)} %get-tuple-element.20), channel_id=1, replica_groups=mesh['vis'=16,'row'=4,'col'=8] {'row','col'}, dimensions={0} | all-to-all | bytes 524288 | tf_op jit(solution)/shard_map/all_to_all | solution.py:268
  162.9 24.3 %shard_map.144 = bf16[32,64,128]{2,1,0:T(8,128)(2,1)S(1)} custom-call(bf16[32,32,128]{2,1,0:T(8,128)(2,1)S(1)} %all_to_all.59.inputs_ref, bf16[16,32,384]{2,1,0:T(8,128)(2,1)S(1)} %all_to_all.57.arrived_ref.cot_ref, bf16[16,1792,256]{2,1,0:T(8,128)(2,1)} %bitcast.7), custom_call_target="tpu_custom_call" | custom-call | tf_op jit(solution)/shard_map/pallas_call | solution.py:313
  187.2 18.8 %all_to_all.60.arrived_ref = bf16[32,64,128]{2,1,0:T(8,128)(2,1)S(1)} all-to-all(bf16[32,64,128]{2,1,0:T(8,128)(2,1)S(1)} %shard_map.144), channel_id=1, replica_groups=mesh['vis'=16,'row'=4,'col'=8] {'row','col'}, dimensions={0} | all-to-all | bytes 1048576 | tf_op jit(solution)/shard_map/all_to_all | solution.py:268
  206.1 20.1 %all_to_all.61.grad_ref = bf16[32,64,128]{2,1,0:T(8,128)(2,1)S(1)} all-to-all(bf16[32,64,128]{2,1,0:T(8,128)(2,1)S(1)} %shard_map.145), channel_id=1, replica_groups=mesh['vis'=16,'row'=4,'col'=8] {'row','col'}, dimensions={0} | all-to-all | bytes 1048576 | tf_op jit(solution)/shard_map/all_to_all | solution.py:268
  226.2 4.2 %shard_map.146 = (bf16[16,32,256]{2,1,0:T(8,128)(2,1)S(1)}, bf16[32,16,512]{2,1,0:T(8,128)(2,1)}) custom-call(bf16[32,64,128]{2,1,0:T(8,128)(2,1)S(1)} %all_to_all.61.grad_ref, bf16[16,128,256]{2,1,0:T(8,128)(2,1)S(1)} %all-to-all-done.3.weight_ref.second_ref, f32[32,128]{1,0:T(8,128)S(1)} %get-tuple-element.22.slope_ref, ...), custom_call_target="tpu_custom_call" | custom-call | tf_op jit(solution)/shard_map/pallas_call | solution.py:330
  230.3 20.0 %all_to_all.62.act_ref = bf16[16,32,256]{2,1,0:T(8,128)(2,1)S(1)} all-to-all(bf16[16,32,256]{2,1,0:T(8,128)(2,1)S(1)} %get-tuple-element.24), channel_id=1, replica_groups=mesh['vis'=16,'row'=4,'col'=8] {'vis'}, dimensions={0} | all-to-all | bytes 524288 | tf_op jit(solution)/shard_map/all_to_all | solution.py:268
  250.4 20.0 %all_to_all.63 = bf16[16,128,128]{2,1,0:T(8,128)(2,1)S(1)} all-to-all(bf16[16,128,128]{2,1,0:T(8,128)(2,1)S(1)} %bitcast.4), channel_id=1, replica_groups=mesh['vis'=16,'row'=4,'col'=8] {'vis'}, dimensions={0} | all-to-all | bytes 1048576 | tf_op jit(solution)/shard_map/all_to_all | solution.py:268
  270.4 5.4 %all-to-all-start.10 = ((bf16[32,16,512]{2,1,0:T(8,128)(2,1)}), bf16[32,16,512]{2,1,0:T(8,128)(2,1)S(1)}, u32[]{:S(2)}, u32[]{:S(2)}) async-start(bf16[32,16,512]{2,1,0:T(8,128)(2,1)} %get-tuple-element.26), calls=%async_computation.10 | async-start | bytes 1048576 | tf_op jit(solution)/shard_map/all_to_all | solution.py:268
  275.8 1.8 shard_map.147
  277.6 14.8 %all-to-all-done.10.arrived_ref = bf16[32,16,512]{2,1,0:T(8,128)(2,1)S(1)} async-done(((bf16[32,16,512]{2,1,0:T(8,128)(2,1)}), bf16[32,16,512]{2,1,0:T(8,128)(2,1)S(1)}, u32[]{:S(2)}, u32[]{:S(2)}) %all-to-all-start.10) | async-done | bytes 524320 | tf_op jit(solution)/shard_map/all_to_all | solution.py:268
  292.3 0.9 shard_map.148
  (29 shorter events, 6.0 us)
Async XLA Ops:
  7.2 155.7 %all-gather.3.cloned.1.call-start = ((), (), s32[]{:S(2)}) async-start(), calls=%async_computation.11 | async-start | bytes 15597568 | tf_op jit(solution)/shard_map/all_gather | solution.py:275
  7.2 0.9 copy-start
  8.1 0.9 copy-start.2
  9.1 0.9 copy-start.3
  10.0 0.9 copy-start.4
  12.8 0.7 copy-start.5
  31.0 0.7 copy-start.6
  62.7 44.5 %all-to-all-start.3 = ((bf16[16,128,256]{2,1,0:T(8,128)(2,1)}), bf16[16,128,256]{2,1,0:T(8,128)(2,1)S(1)}, u32[]{:S(2)}, u32[]{:S(2)}) async-start(bf16[16,128,256]{2,1,0:T(8,128)(2,1)} %broadcast_in_dim.2), calls=%async_computation.3 | async-start | bytes 2097152 | tf_op jit(solution)/shard_map/all_to_all | solution.py:268
  69.5 0.9 copy-start.1
  70.4 0.7 copy-start.7
  71.1 0.7 copy-start.9
  130.6 0.7 copy-start.11
  187.2 88.6 %copy-start.8 = (s32[16]{0:T(128)S(1)}, s32[16]{0:T(128)}, u32[]{:S(2)}) copy-start(s32[16]{0:T(128)} %counts_ref.3) | copy-start | bytes 196
  187.2 88.6 %copy-start.10 = (s32[16]{0:T(128)S(1)}, s32[16]{0:T(128)}, u32[]{:S(2)}) copy-start(s32[16]{0:T(128)} %order_ref.3) | copy-start | bytes 196
  270.4 22.0 %all-to-all-start.10 = ((bf16[32,16,512]{2,1,0:T(8,128)(2,1)}), bf16[32,16,512]{2,1,0:T(8,128)(2,1)S(1)}, u32[]{:S(2)}, u32[]{:S(2)}) async-start(bf16[32,16,512]{2,1,0:T(8,128)(2,1)} %get-tuple-element.26), calls=%async_computation.10 | async-start | bytes 1048576 | tf_op jit(solution)/shard_map/all_to_all | solution.py:268
Sparse Core Ops, SparseCore 0:
  12.1 124.6 all-gather.2

commit v2 on v1

v2 whole, which is shorter than its diff:
```python
import jax
import jax.numpy as jnp
from jax import lax
from jax.experimental import pallas as pl
from jax.experimental.pallas import tpu as pltpu
from jax.sharding import PartitionSpec as P

VIS = 16
RC = 32
ROWS = 256
OWN = 16
SPLIT = 400
LANES = 512
F32 = jnp.float32
BF16 = jnp.bfloat16
GROUP = ("row", "col")


def struct(shape, dtype):
    return jax.ShapeDtypeStruct(shape, dtype)


def params():
    return pltpu.CompilerParams(vmem_limit_bytes=40 * 1024 * 1024)


def dot(a, b, ca=1, cb=0):
    return lax.dot_general(a, b, (((ca,), (cb,)), ((), ())), preferred_element_type=F32)


def group_index():
    return lax.axis_index("row") * lax.axis_size("col") + lax.axis_index("col")


def pack_kernel(gate_ref, up_ref, out_ref):
    out_ref[0:256, :] = gate_ref[:, 0:256]
    out_ref[256:512, :] = gate_ref[:, 256:512]
    out_ref[512:768, :] = up_ref[:, 0:256]
    out_ref[768:1024, :] = up_ref[:, 256:512]


def norm_kernel(images_ref, gain_ref, message_ref, hat_ref, gain_out, scale_ref, values, gains):
    values[...] = jnp.zeros_like(values)
    gains[...] = jnp.zeros_like(gains)
    row = images_ref[...].astype(F32)
    gain_row = gain_ref[...]
    for v in range(VIS):
        values[v : v + 1, 0:SPLIT] = row[:, v * SPLIT : (v + 1) * SPLIT]
        gains[v : v + 1, 0:SPLIT] = gain_row[:, v * SPLIT : (v + 1) * SPLIT]
    inside = lax.broadcasted_iota(jnp.int32, (VIS, LANES), 1) < SPLIT
    x = values[...]
    mean = jnp.sum(x, keepdims=True) * (1.0 / (VIS * SPLIT))
    centred = jnp.where(inside, x - mean, 0.0)
    variance = jnp.sum(centred * centred, keepdims=True) * (1.0 / (VIS * SPLIT))
    scale = lax.rsqrt(variance + 1e-05)
    hat = centred * scale
    hat_ref[...] = hat
    gain_out[...] = gains[...]
    scale_ref[...] = jnp.broadcast_to(scale, scale_ref.shape)
    normed = (hat * gains[...]).astype(BF16).astype(F32)
    message_ref[...] = jnp.zeros_like(message_ref)
    for j in range(4):
        message_ref[:, j, :] = normed[:, 128 * j : 128 * j + 128]


def spread_kernel(arrived_ref, cotangent_ref, out_ref):
    parts = [arrived_ref[:, j, :] for j in range(4)]
    cot = cotangent_ref[...].astype(F32)
    parts.append(jnp.concatenate([cot[:, 0:128], cot[:, 128:256]], axis=0))
    block = jnp.concatenate(parts, axis=1).astype(BF16)
    for r in range(RC):
        out_ref[r] = block


def selection(target_ref):
    language = lax.broadcasted_iota(jnp.int32, (ROWS, RC * VIS), 0)
    return jnp.where(language == target_ref[0:1, :], 1.0, 0.0).astype(BF16)


def first_kernel(counts_ref, order_ref, rows_ref, first_ref, down_ref, out_ref, target_ref, weight, starts):
    def body(j, total):
        block = order_ref[j]
        starts[block] = total
        return total + counts_ref[block]

    lax.fori_loop(0, VIS, body, jnp.int32(0))
    lane = lax.broadcasted_iota(jnp.int32, (8, RC * VIS), 1)
    owner = lane % VIS
    slot = lane // VIS
    target = jnp.full((8, RC * VIS), -1, jnp.int32)
    for v in range(VIS):
        live = jnp.logical_and(owner == v, slot < counts_ref[v])
        target = jnp.where(live, slot + starts[v], target)
    target_ref[...] = target
    weight[SPLIT:LANES, :] = jnp.zeros((LANES - SPLIT, 128), BF16)
    weight[0:SPLIT, :] = first_ref[...]
    rows = rows_ref[:, :, 0:LANES].reshape(RC * VIS, LANES)
    pre = dot(rows, weight[...]).astype(BF16)
    pre = dot(selection(target_ref), pre).astype(BF16)
    cot = rows_ref[:, :, LANES : LANES + 128].astype(F32)
    cot = jnp.concatenate(
        [cot[:, 0:8, :].reshape(ROWS, 128), cot[:, 8:16, :].reshape(ROWS, 128)], axis=1
    ).astype(BF16)
    grad = dot(cot, down_ref[...], 1, 1).astype(BF16)
    out_ref[:, :, 0:512] = grad.reshape(VIS, OWN, 512)
    out_ref[:, :, 512:768] = cot.reshape(VIS, OWN, 256)
    out_ref[:, :, 768:896] = pre.reshape(VIS, OWN, 128)


def second_kernel(arrived_ref, bias_ref, weight_ref, out_ref, hidden_ref, slope_ref):
    pre = jnp.zeros((OWN, 128), F32)
    for v in range(VIS):
        pre = pre + arrived_ref[v, :, 768:896].astype(F32)
    pre = pre + bias_ref[...]
    cdf = 0.5 * (1.0 + lax.erf(pre * 0.7071067811865476))
    density = jnp.exp(-0.5 * pre * pre) * 0.3989422804014327
    hidden = (pre * cdf).astype(BF16)
    hidden_ref[...] = hidden
    slope_ref[...] = cdf + pre * density
    for v in range(VIS):
        y = dot(hidden, weight_ref[v]).astype(BF16)
        out_ref[2 * v] = y[:, 0:128]
        out_ref[2 * v + 1] = y[:, 128:256]


def input_sum_kernel(arrived_ref, out_ref):
    total = jnp.zeros((OWN, 128), F32)
    for r in range(RC):
        total = total + arrived_ref[r].astype(F32)
    own = total.astype(BF16)
    for r in range(RC):
        out_ref[r] = own


def block_kernel(inputs_ref, pieces_ref, w_ref, out_ref, hidden_ref, gate, up, gate_b, up_b):
    phase = pl.program_id(0)
    v = pl.program_id(1)

    @pl.when(jnp.logical_and(phase == 0, v == 0))
    def _():
        gate[...] = jnp.zeros_like(gate)
        up[...] = jnp.zeros_like(up)

    @pl.when(phase == 0)
    def _():
        x = jnp.concatenate([inputs_ref[0], inputs_ref[1]], axis=1)
        gate[:, 0:256] += dot(x, w_ref[0, 0:256, :])
        gate[:, 256:512] += dot(x, w_ref[0, 256:512, :])
        up[:, 0:256] += dot(x, w_ref[0, 512:768, :])
        up[:, 256:512] += dot(x, w_ref[0, 768:1024, :])

    @pl.when(jnp.logical_and(phase == 1, v == 0))
    def _():
        h = jnp.zeros((OWN, 512), F32)
        for i in range(VIS):
            h = h + pieces_ref[i, :, 0:512].astype(F32)
        g, u = gate[...], up[...]
        s = jax.nn.sigmoid(g)
        hidden_ref[...] = (g * s * u).astype(BF16)
        gate_b[...] = (h * u * s * (1.0 + g * (1.0 - s))).astype(BF16)
        up_b[...] = (h * g * s).astype(BF16)

    @pl.when(phase == 1)
    def _():
        y = dot(gate_b[:, 0:256], w_ref[0, 0:256, :], 1, 1)
        y += dot(gate_b[:, 256:512], w_ref[0, 256:512, :], 1, 1)
        y += dot(up_b[:, 0:256], w_ref[0, 512:768, :], 1, 1)
        y += dot(up_b[:, 256:512], w_ref[0, 768:1024, :], 1, 1)
        y = y.astype(BF16)
        out_ref[0] = y[:, 0:128]
        out_ref[1] = y[:, 128:256]


def grad_sum_kernel(arrived_ref, pieces_ref, out_ref):
    r = group_index()
    total = jnp.zeros((OWN, 128), F32)
    for i in range(RC):
        total = total + arrived_ref[i].astype(F32)
    piece = pieces_ref[r // 2]
    cot = jnp.where(r % 2 == 0, piece[:, 512:640].astype(F32), piece[:, 640:768].astype(F32))
    result = (total + cot).astype(BF16)
    for i in range(RC):
        out_ref[i] = result


def back_kernel(grad_ref, second_ref, slope_ref, act_ref, hidden_ref, inputs_ref, out_ref):
    acc = jnp.zeros((OWN, 128), F32)
    for v in range(VIS):
        ig = jnp.concatenate([grad_ref[2 * v], grad_ref[2 * v + 1]], axis=1)
        acc = acc + dot(ig, second_ref[v], 1, 1)
        out_ref[v, :, 0:256] = ig
        out_ref[v, :, 1024:1152] = inputs_ref[2 * v]
        out_ref[v, :, 1152:1280] = inputs_ref[2 * v + 1]
    act = (acc * slope_ref[...]).astype(BF16)
    both = jnp.concatenate([act, act_ref[...], hidden_ref[...]], axis=1)
    for v in range(VIS):
        out_ref[v, :, 256:1024] = both


def slot_kernel(target_ref, pieces_ref, first_ref, down_ref, out_ref, act_ref, weight):
    weight[SPLIT:LANES, :] = jnp.zeros((LANES - SPLIT, 128), BF16)
    weight[0:SPLIT, :] = first_ref[...]
    act = pieces_ref[:, :, 256:384].reshape(ROWS, 128)
    act = dot(selection(target_ref), act, 0, 0).astype(BF16)
    act_ref[...] = act
    out_ref[:, :, 0:LANES] = dot(act, weight[...], 1, 1).astype(BF16).reshape(RC, VIS, LANES)
    block = dot(pieces_ref[:, :, 512:1024].reshape(ROWS, 512), down_ref[...])
    block = jnp.concatenate(
        [block[:, 0:128].reshape(RC, 8, 128), block[:, 128:256].reshape(RC, 8, 128)], axis=1
    )
    out_ref[:, :, LANES : LANES + 128] = block.astype(BF16)


def weight_grad_kernel(pieces_ref, act_ref, rows_ref, first_ref, second_ref):
    hidden = pieces_ref[:, :, 384:512].reshape(ROWS, 128)
    ig = pieces_ref[:, :, 0:256].reshape(ROWS, 256)
    second_ref[...] = dot(hidden, ig, 0, 0)
    rows = rows_ref[:, :, 0:LANES].reshape(RC * VIS, LANES)
    first_ref[...] = dot(rows, act_ref[...], 0, 0)[0:SPLIT, :]


def slot_sum_kernel(arrived_ref, pieces_ref, message_ref, out_ref):
    r = group_index()
    total = jnp.zeros((VIS, LANES + 128), F32)
    for i in range(RC):
        total = total + arrived_ref[i].astype(F32)
    message_ref[...] = jnp.zeros_like(message_ref)
    for j in range(4):
        message_ref[:, j, :] = total[:, 128 * j : 128 * j + 128]
    part = total[:, LANES : LANES + 128]
    part = jnp.concatenate([part[0:8], part[8:16]], axis=1)
    piece = pieces_ref[r // 2].astype(F32)[:, 1024:1280]
    out_ref[...] = (jnp.where(r % 2 == 0, piece[0:8], piece[8:16]) + part).astype(BF16)


def norm_back_kernel(arrived_ref, hat_ref, gain_ref, scale_ref, out_ref):
    total = jnp.concatenate([arrived_ref[:, j, :] for j in range(4)], axis=1)
    hat = hat_ref[...]
    g = total * gain_ref[...]
    mean = jnp.sum(g, keepdims=True) * (1.0 / (VIS * SPLIT))
    cross = jnp.sum(g * hat, keepdims=True) * (1.0 / (VIS * SPLIT))
    result = scale_ref[0:1, 0:1] * (g - mean - hat * cross)
    for v in range(VIS):
        out_ref[:, v * SPLIT : (v + 1) * SPLIT] = result[v : v + 1, 0:SPLIT]


def full(shape):
    zeros = (0,) * len(shape)
    return pl.BlockSpec(shape, lambda i: zeros)


def call(kernel, outs, *args, scratch=()):
    ins = [
        pl.BlockSpec(memory_space=pltpu.SMEM) if a.dtype == jnp.int32 and a.ndim == 1 else full(a.shape)
        for a in args
    ]
    return pl.pallas_call(
        kernel,
        grid=(1,),
        out_shape=outs,
        in_specs=ins,
        out_specs=jax.tree.map(lambda o: full(o.shape), outs),
        scratch_shapes=list(scratch),
        compiler_params=params(),
    )(*args)


def swap(blocks, axes):
    return lax.all_to_all(blocks, axes, 0, 0, tiled=True)


def on_device(
    images, counts, block_order, gain, proj_first, bias, proj_second, gate_w, up_w, down_w, cotangent
):
    seconds = lax.all_gather(proj_second, "vis")
    packed = call(pack_kernel, struct((1024, 256), BF16), gate_w, up_w)
    weights = lax.all_gather(packed, "vis")
    message, hat, gains, scale = call(
        norm_kernel,
        (
            struct((VIS, 8, 128), F32),
            struct((VIS, LANES), F32),
            struct((VIS, LANES), F32),
            struct((8, 128), F32),
        ),
        images,
        gain.reshape(1, -1),
        scratch=[pltpu.VMEM((VIS, LANES), F32), pltpu.VMEM((VIS, LANES), F32)],
    )
    arrived = swap(message, "vis")
    spread = call(spread_kernel, struct((RC, VIS, 640), BF16), arrived, cotangent)
    rows = swap(spread, GROUP)
    partial, target = call(
        first_kernel,
        (struct((VIS, OWN, 896), BF16), struct((8, RC * VIS), jnp.int32)),
        counts,
        block_order,
        rows,
        proj_first,
        down_w,
        scratch=[pltpu.VMEM((LANES, 128), BF16), pltpu.SMEM((VIS,), jnp.int32)],
    )
    pieces = swap(partial, "vis")
    input_part, hidden_proj, slope = call(
        second_kernel,
        (struct((RC, OWN, 128), BF16), struct((OWN, 128), BF16), struct((OWN, 128), F32)),
        pieces,
        bias.reshape(1, -1),
        seconds,
    )
    spread = call(input_sum_kernel, struct((RC, OWN, 128), BF16), swap(input_part, GROUP))
    inputs = swap(spread, GROUP)
    block_part, hidden = pl.pallas_call(
        block_kernel,
        out_shape=(struct((RC, OWN, 128), BF16), struct((OWN, 512), BF16)),
        grid=(2, VIS),
        in_specs=[
            pl.BlockSpec((2, OWN, 128), lambda p, v: ((1 - p) * v, 0, 0)),
            pl.BlockSpec((VIS, OWN, 896), lambda p, v: (0, 0, 0)),
            pl.BlockSpec((1, 1024, 256), lambda p, v: (v, 0, 0)),
        ],
        out_specs=(
            pl.BlockSpec((2, OWN, 128), lambda p, v: (p * v, 0, 0)),
            pl.BlockSpec((OWN, 512), lambda p, v: (0, 0)),
        ),
        scratch_shapes=[pltpu.VMEM((OWN, 512), F32)] * 2 + [pltpu.VMEM((OWN, 512), BF16)] * 2,
        compiler_params=params(),
    )(inputs, pieces, weights)
    spread = call(grad_sum_kernel, struct((RC, OWN, 128), BF16), swap(block_part, GROUP), pieces)
    whole = swap(spread, GROUP)
    sent = call(
        back_kernel, struct((VIS, OWN, 1280), BF16), whole, seconds, slope, hidden_proj, hidden, inputs
    )
    blocks = swap(sent, "vis")
    slot_part, acts = call(
        slot_kernel,
        (struct((RC, VIS, 640), BF16), struct((RC * VIS, 128), BF16)),
        target,
        blocks,
        proj_first,
        down_w,
        scratch=[pltpu.VMEM((LANES, 128), BF16)],
    )
    slots = swap(slot_part, GROUP)
    first_grad, second_grad = call(
        weight_grad_kernel,
        (struct((SPLIT, 128), F32), struct((128, 256), F32)),
        blocks,
        acts,
        rows,
    )
    message, block_out = call(
        slot_sum_kernel, (struct((VIS, 8, 128), F32), struct((8, 256), BF16)), slots, blocks
    )
    image_grad = call(
        norm_back_kernel, struct((1, VIS * SPLIT), F32), swap(message, "vis"), hat, gains, scale
    )
    return block_out, image_grad, first_grad, second_grad


def solution(mesh):
    every = ("vis", "row", "col")
    return jax.shard_map(
        on_device,
        mesh=mesh,
        in_specs=(
            P(every, None),
            P(),
            P(),
            P(),
            P("vis", GROUP),
            P(GROUP),
            P(GROUP, "vis"),
            P("vis", GROUP),
            P("vis", GROUP),
            P(GROUP, "vis"),
            P(GROUP, "vis"),
        ),
        out_specs=(P(GROUP, "vis"), P(every, None), P("vis", GROUP), P(GROUP, "vis")),
        check_vma=False,
    )
```

time: 302 us -> 237 us (0.78)
  blocking collectives: 180 us -> 151 us
  Pallas kernels: 34 us -> 14.5 us
  waiting for transfers between devices: 49.2 us -> 31.3 us
    all_to_all x9 -> x8, blocking collectives: 180 us -> 151 us  [swap(): return lax.all_to_all(blocks, axes, 0, 0, tiled=True)]
    all_to_all x2, waiting for transfers between devices: 49.2 us -> 26.7 us  [swap(): return lax.all_to_all(blocks, axes, 0, 0, tiled=True)]
    pallas_call x11 -> x13, Pallas kernels: 34 us -> 14.5 us  [the longest x12 7.41 us: call(): pl.pallas_call(kernel, grid=(1,), out_shape=outs, in_specs=ins, out_specs...]
    all_gather x1, waiting for transfers between devices: 0.01 us -> 3.88 us  [on_device(): weights = lax.all_gather(packed, 'vis')]
    unnamed x24 -> x28, local copies, waits for them, and re-layouts: 8.03 us -> 11.7 us
  transfers between devices with their start and end apart: 3 -> 4, of which waited for: 2 -> 3; matrix products, arithmetic and copies ran while one was open for 1% -> 0% of each run, Pallas kernels for 1% -> 2%
where the time goes in v2:
time: 237 us; the launch traced here: 236 us
  blocking collectives  151 us (64%)
  waiting for transfers between devices  31.3 us (13%)
  Pallas kernels  14.5 us (6%)
  between operations  14.1 us (6%)
  starting transfers between devices  12.9 us (5%)
  local copies, waits for them, and re-layouts  12.5 us (5%)
    all_to_all x8, blocking collectives, swap(): return lax.all_to_all(blocks, axes, 0, 0, tiled=True)  151 us
    all_to_all x2, waiting for transfers between devices, swap(): return lax.all_to_all(blocks, axes, 0, 0, tiled=True)  26.7 us
    all_to_all x2, starting transfers between devices, swap(): return lax.all_to_all(blocks, axes, 0, 0, tiled=True)  12.8 us
    unnamed x28, local copies, waits for them, and re-layouts  11.7 us
    pallas_call x12, Pallas kernels, call(): pl.pallas_call(kernel, grid=(1,), out_shape=outs, in_specs=ins, out_specs...  7.41 us
    pallas_call x1, Pallas kernels, on_device(): pl.pallas_call(block_kernel, out_shape=(struct((RC, OWN, 128), BF16), str...  7.05 us
  transfers between devices with their start and end apart: 4, of which 3 were waited for; matrix products, arithmetic and copies ran while one was open for 0% of the time, Pallas kernels for 2%

profile of v2, /device:TPU:1, one launch (start us, length us, event | category | flops | bytes accessed | tf_op | source)
XLA Modules:
  0.0 236.3 jit_solution(14893880847286860479)
XLA Ops:
  8.0 0.9 copy-done.7
  8.9 0.9 copy-done.8
  9.8 0.8 shard_map.143
  12.6 17.1 %all_to_all.50.arrived_ref = f32[16,8,128]{2,1,0:T(8,128)S(1)} all-to-all(f32[16,8,128]{2,1,0:T(8,128)S(1)} %get-tuple-element.21), channel_id=1, replica_groups=mesh['vis'=16,'row'=4,'col'=8] {'vis'}, dimensions={0} | all-to-all | bytes 131072 | tf_op jit(solution)/shard_map/all_to_all | solution.py:269
  30.5 28.5 %all_to_all.51.rows_ref = bf16[32,16,640]{2,1,0:T(8,128)(2,1)S(1)} all-to-all(bf16[32,16,640]{2,1,0:T(8,128)(2,1)S(1)} %shard_map.139), channel_id=1, replica_groups=mesh['vis'=16,'row'=4,'col'=8] {'row','col'}, dimensions={0} | all-to-all | bytes 1310720 | tf_op jit(solution)/shard_map/all_to_all | solution.py:269
  59.0 0.9 copy-done.3
  60.0 0.9 copy-done.5
  62.2 2.2 shard_map.140
  64.4 7.4 %all-to-all-start.2 = ((bf16[16,16,896]{2,1,0:T(8,128)(2,1)}), bf16[16,16,896]{2,1,0:T(8,128)(2,1)S(1)}, u32[]{:S(2)}, u32[]{:S(2)}) async-start(bf16[16,16,896]{2,1,0:T(8,128)(2,1)} %get-tuple-element.23), calls=%async_computation.2 | async-start | bytes 917504 | tf_op jit(solution)/shard_map/all_to_all | solution.py:269
  71.8 19.9 %all-to-all-done.2.arrived_ref.pieces_ref = bf16[16,16,896]{2,1,0:T(8,128)(2,1)S(1)} async-done(((bf16[16,16,896]{2,1,0:T(8,128)(2,1)}), bf16[16,16,896]{2,1,0:T(8,128)(2,1)S(1)}, u32[]{:S(2)}, u32[]{:S(2)}) %all-to-all-start.2) | async-done | bytes 458784 | tf_op jit(solution)/shard_map/all_to_all | solution.py:269
  91.7 1.2 copy-done.1
  93.9 14.8 %all_to_all.52.arrived_ref = bf16[32,16,128]{2,1,0:T(8,128)(2,1)S(1)} all-to-all(bf16[32,16,128]{2,1,0:T(8,128)(2,1)S(1)} %get-tuple-element.24), channel_id=1, replica_groups=mesh['vis'=16,'row'=4,'col'=8] {'row','col'}, dimensions={0} | all-to-all | bytes 262144 | tf_op jit(solution)/shard_map/all_to_all | solution.py:269
  108.7 13.6 %all_to_all.53.inputs_ref = bf16[32,16,128]{2,1,0:T(8,128)(2,1)S(1)} all-to-all(bf16[32,16,128]{2,1,0:T(8,128)(2,1)S(1)} %shard_map.142), channel_id=1, replica_groups=mesh['vis'=16,'row'=4,'col'=8] {'row','col'}, dimensions={0} | all-to-all | bytes 262144 | tf_op jit(solution)/shard_map/all_to_all | solution.py:269
  122.3 3.9 %all-gather.7.cloned.1.call-done = bf16[16384,256]{1,0:T(8,128)(2,1)} async-done(((bf16[1024,256]{1,0:T(8,128)(2,1)}), bf16[16384,256]{1,0:T(8,128)(2,1)}) %all-gather.7.cloned.1.call-update) | async-done | bytes 8388624 | tf_op jit(solution)/shard_map/all_gather | solution.py:277
  126.1 3.4 %copy-done = bf16[16384,256]{1,0:T(8,128)(2,1)S(1)} copy-done((bf16[16384,256]{1,0:T(8,128)(2,1)S(1)}, bf16[16384,256]{1,0:T(8,128)(2,1)}, u32[]{:S(2)}) %copy-start) | copy-done | bytes 8388632
  129.5 7.0 %shard_map.144 = (bf16[32,16,128]{2,1,0:T(8,128)(2,1)S(1)}, bf16[16,512]{1,0:T(8,128)(2,1)S(1)}) custom-call(bf16[32,16,128]{2,1,0:T(8,128)(2,1)S(1)} %all_to_all.53.inputs_ref, bf16[16,16,896]{2,1,0:T(8,128)(2,1)S(1)} %all-to-all-done.2.arrived_ref.pieces_ref, bf16[16,1024,256]{2,1,0:T(8,128)(2,1)S(1)} %bitcast.3), custom_call_target="tpu_custom_call" | custom-call | tf_op jit(solution)/shard_map/pallas_call | solution.py:313
  136.6 15.0 %all_to_all.54.arrived_ref = bf16[32,16,128]{2,1,0:T(8,128)(2,1)S(1)} all-to-all(bf16[32,16,128]{2,1,0:T(8,128)(2,1)S(1)} %get-tuple-element.25), channel_id=1, replica_groups=mesh['vis'=16,'row'=4,'col'=8] {'row','col'}, dimensions={0} | all-to-all | bytes 262144 | tf_op jit(solution)/shard_map/all_to_all | solution.py:269
  151.6 13.4 %all_to_all.55.grad_ref = bf16[32,16,128]{2,1,0:T(8,128)(2,1)S(1)} all-to-all(bf16[32,16,128]{2,1,0:T(8,128)(2,1)S(1)} %shard_map.145), channel_id=1, replica_groups=mesh['vis'=16,'row'=4,'col'=8] {'row','col'}, dimensions={0} | all-to-all | bytes 262144 | tf_op jit(solution)/shard_map/all_to_all | solution.py:269
  165.4 27.2 %all_to_all.56.pieces_ref = bf16[16,16,1280]{2,1,0:T(8,128)(2,1)S(1)} all-to-all(bf16[16,16,1280]{2,1,0:T(8,128)(2,1)S(1)} %shard_map.146), channel_id=1, replica_groups=mesh['vis'=16,'row'=4,'col'=8] {'vis'}, dimensions={0} | all-to-all | bytes 1310720 | tf_op jit(solution)/shard_map/all_to_all | solution.py:269
  193.2 21.4 %all_to_all.57.arrived_ref = bf16[32,16,640]{2,1,0:T(8,128)(2,1)S(1)} all-to-all(bf16[32,16,640]{2,1,0:T(8,128)(2,1)S(1)} %get-tuple-element.29), channel_id=1, replica_groups=mesh['vis'=16,'row'=4,'col'=8] {'row','col'}, dimensions={0} | all-to-all | bytes 1310720 | tf_op jit(solution)/shard_map/all_to_all | solution.py:269
  215.3 5.4 %all-to-all-start.9 = ((f32[16,8,128]{2,1,0:T(8,128)}), f32[16,8,128]{2,1,0:T(8,128)S(1)}, u32[]{:S(2)}, u32[]{:S(2)}) async-start(f32[16,8,128]{2,1,0:T(8,128)} %get-tuple-element.31), calls=%async_computation.9 | async-start | bytes 131072 | tf_op jit(solution)/shard_map/all_to_all | solution.py:269
  220.8 1.0 shard_map.150
  221.8 6.8 %all-to-all-done.9.arrived_ref = f32[16,8,128]{2,1,0:T(8,128)S(1)} async-done(((f32[16,8,128]{2,1,0:T(8,128)}), f32[16,8,128]{2,1,0:T(8,128)S(1)}, u32[]{:S(2)}, u32[]{:S(2)}) %all-to-all-start.9) | async-done | bytes 65568 | tf_op jit(solution)/shard_map/all_to_all | solution.py:269
  228.6 0.8 shard_map.149
  (36 shorter events, 7.4 us)
Async XLA Ops:
  7.2 64.6 %all-gather.5.cloned.1.call-start = ((), (), s32[]{:S(2)}) async-start(), calls=%async_computation.10 | async-start | bytes 1114112 | tf_op jit(solution)/shard_map/all_gather | solution.py:275
  7.9 118.2 %all-gather.7.cloned.1.call-start = ((), (), s32[]{:S(2)}) async-start(), calls=%async_computation.11 | async-start | bytes 8912896 | tf_op jit(solution)/shard_map/all_gather | solution.py:277
  7.9 1.0 copy-start.7
  8.9 0.9 copy-start.8
  11.5 0.7 copy-start.9
  29.7 0.7 copy-start.10
  59.0 1.0 copy-start.3
  59.9 0.9 copy-start.5
  60.8 0.7 copy-start.11
  61.5 0.7 copy-start.12
  64.4 128.3 %copy-start.4 = (bf16[512,256]{1,0:T(8,128)(2,1)S(1)}, bf16[512,256]{1,0:T(8,128)(2,1)}, u32[]{:S(2)}) copy-start(bf16[512,256]{1,0:T(8,128)(2,1)} %down_ref.3) | copy-start | bytes 786436
  64.4 128.3 %copy-start.6 = (bf16[400,128]{1,0:T(8,128)(2,1)S(1)}, bf16[400,128]{1,0:T(8,128)(2,1)}, u32[]{:S(2)}) copy-start(bf16[400,128]{1,0:T(8,128)(2,1)} %first_ref.3) | copy-start | bytes 307204
  64.4 27.4 %all-to-all-start.2 = ((bf16[16,16,896]{2,1,0:T(8,128)(2,1)}), bf16[16,16,896]{2,1,0:T(8,128)(2,1)S(1)}, u32[]{:S(2)}, u32[]{:S(2)}) async-start(bf16[16,16,896]{2,1,0:T(8,128)(2,1)} %get-tuple-element.23), calls=%async_computation.2 | async-start | bytes 917504 | tf_op jit(solution)/shard_map/all_to_all | solution.py:269
  91.7 1.2 copy-start.1
  93.0 0.7 copy-start.13
  93.6 71.4 %copy-start.2 = (bf16[2048,256]{1,0:T(8,128)(2,1)S(1)}, bf16[2048,256]{1,0:T(8,128)(2,1)}, u32[]{:S(2)}) copy-start(bf16[2048,256]{1,0:T(8,128)(2,1)} %all-gather.5.cloned.1.call-done) | copy-start | bytes 3145732
  126.1 3.4 %copy-start = (bf16[16384,256]{1,0:T(8,128)(2,1)S(1)}, bf16[16384,256]{1,0:T(8,128)(2,1)}, u32[]{:S(2)}) copy-start(bf16[16384,256]{1,0:T(8,128)(2,1)} %all-gather.7.cloned.1.call-done) | copy-start | bytes 25165828
  215.3 13.3 %all-to-all-start.9 = ((f32[16,8,128]{2,1,0:T(8,128)}), f32[16,8,128]{2,1,0:T(8,128)S(1)}, u32[]{:S(2)}, u32[]{:S(2)}) async-start(f32[16,8,128]{2,1,0:T(8,128)} %get-tuple-element.31), calls=%async_computation.9 | async-start | bytes 131072 | tf_op jit(solution)/shard_map/all_to_all | solution.py:269
Sparse Core Ops, SparseCore 0:
  10.1 46.6 all-gather.4
  59.0 67.1 all-gather.6

commit v3 on v2

--- a/solution.py
+++ b/solution.py
@@ -32,11 +32,12 @@
     return lax.axis_index("row") * lax.axis_size("col") + lax.axis_index("col")
 
 
-def pack_kernel(gate_ref, up_ref, out_ref):
+def pack_kernel(gate_ref, up_ref, second_ref, out_ref):
     out_ref[0:256, :] = gate_ref[:, 0:256]
     out_ref[256:512, :] = gate_ref[:, 256:512]
     out_ref[512:768, :] = up_ref[:, 0:256]
     out_ref[768:1024, :] = up_ref[:, 256:512]
+    out_ref[1024:1152, :] = second_ref[...]
 
 
 def norm_kernel(images_ref, gain_ref, message_ref, hat_ref, gain_out, scale_ref, values, gains):
@@ -77,7 +78,14 @@
     return jnp.where(language == target_ref[0:1, :], 1.0, 0.0).astype(BF16)
 
 
-def first_kernel(counts_ref, order_ref, rows_ref, first_ref, down_ref, out_ref, target_ref, weight, starts):
+def language_cotangent(rows_ref):
+    cot = rows_ref[:, :, LANES : LANES + 128].astype(F32)
+    return jnp.concatenate([cot[:, 0:8, :].reshape(ROWS, 128), cot[:, 8:16, :].reshape(ROWS, 128)], axis=1)
+
+
+def first_kernel(
+    counts_ref, order_ref, rows_ref, first_ref, second_ref, down_ref, out_ref, target_ref, weight, starts
+):
     def body(j, total):
         block = order_ref[j]
         starts[block] = total
@@ -97,21 +105,20 @@
     rows = rows_ref[:, :, 0:LANES].reshape(RC * VIS, LANES)
     pre = dot(rows, weight[...]).astype(BF16)
     pre = dot(selection(target_ref), pre).astype(BF16)
-    cot = rows_ref[:, :, LANES : LANES + 128].astype(F32)
-    cot = jnp.concatenate(
-        [cot[:, 0:8, :].reshape(ROWS, 128), cot[:, 8:16, :].reshape(ROWS, 128)], axis=1
-    ).astype(BF16)
+    cot = language_cotangent(rows_ref).astype(BF16)
     grad = dot(cot, down_ref[...], 1, 1).astype(BF16)
+    back = dot(cot, second_ref[...], 1, 1).astype(BF16)
     out_ref[:, :, 0:512] = grad.reshape(VIS, OWN, 512)
-    out_ref[:, :, 512:768] = cot.reshape(VIS, OWN, 256)
-    out_ref[:, :, 768:896] = pre.reshape(VIS, OWN, 128)
-
-
-def second_kernel(arrived_ref, bias_ref, weight_ref, out_ref, hidden_ref, slope_ref):
-    pre = jnp.zeros((OWN, 128), F32)
-    for v in range(VIS):
-        pre = pre + arrived_ref[v, :, 768:896].astype(F32)
-    pre = pre + bias_ref[...]
+    out_ref[:, :, 512:640] = pre.reshape(VIS, OWN, 128)
+    out_ref[:, :, 640:768] = back.reshape(VIS, OWN, 128)
+
+
+def second_kernel(arrived_ref, bias_ref, weight_ref, out_ref, hidden_ref, slope_ref, back_ref):
+    both = jnp.zeros((OWN, 256), F32)
+    for v in range(VIS):
+        both = both + arrived_ref[v, :, 512:768].astype(F32)
+    pre = both[:, 0:128] + bias_ref[...]
+    back_ref[...] = both[:, 128:256]
     cdf = 0.5 * (1.0 + lax.erf(pre * 0.7071067811865476))
     density = jnp.exp(-0.5 * pre * pre) * 0.3989422804014327
     hidden = (pre * cdf).astype(BF16)
@@ -123,7 +130,7 @@
         out_ref[2 * v + 1] = y[:, 128:256]
 
 
-def input_sum_kernel(arrived_ref, out_ref):
+def sum_kernel(arrived_ref, out_ref):
     total = jnp.zeros((OWN, 128), F32)
     for r in range(RC):
         total = total + arrived_ref[r].astype(F32)
@@ -132,7 +139,7 @@
         out_ref[r] = own
 
 
-def block_kernel(inputs_ref, pieces_ref, w_ref, out_ref, hidden_ref, gate, up, gate_b, up_b):
+def block_kernel(inputs_ref, pieces_ref, act_ref, w_ref, out_ref, bundle_ref, gate, up, gate_b, up_b):
     phase = pl.program_id(0)
     v = pl.program_id(1)
 
@@ -140,9 +147,12 @@
     def _():
         gate[...] = jnp.zeros_like(gate)
         up[...] = jnp.zeros_like(up)
+        bundle_ref[36] = act_ref[...]
 
     @pl.when(phase == 0)
     def _():
+        bundle_ref[2 * v] = inputs_ref[0]
+        bundle_ref[2 * v + 1] = inputs_ref[1]
         x = jnp.concatenate([inputs_ref[0], inputs_ref[1]], axis=1)
         gate[:, 0:256] += dot(x, w_ref[0, 0:256, :])
         gate[:, 256:512] += dot(x, w_ref[0, 256:512, :])
@@ -153,10 +163,12 @@
     def _():
         h = jnp.zeros((OWN, 512), F32)
         for i in range(VIS):
-            h = h + pieces_ref[i, :, 0:512].astype(F32)
+            h = h + pieces_ref[i].astype(F32)
         g, u = gate[...], up[...]
         s = jax.nn.sigmoid(g)
-        hidden_ref[...] = (g * s * u).astype(BF16)
+        hidden = (g * s * u).astype(BF16)
+        for k in range(4):
+            bundle_ref[32 + k] = hidden[:, 128 * k : 128 * k + 128]
         gate_b[...] = (h * u * s * (1.0 + g * (1.0 - s))).astype(BF16)
         up_b[...] = (h * g * s).astype(BF16)
 
@@ -171,56 +183,45 @@
         out_ref[1] = y[:, 128:256]
 
 
-def grad_sum_kernel(arrived_ref, pieces_ref, out_ref):
-    r = group_index()
-    total = jnp.zeros((OWN, 128), F32)
-    for i in range(RC):
-        total = total + arrived_ref[i].astype(F32)
-    piece = pieces_ref[r // 2]
-    cot = jnp.where(r % 2 == 0, piece[:, 512:640].astype(F32), piece[:, 640:768].astype(F32))
-    result = (total + cot).astype(BF16)
-    for i in range(RC):
-        out_ref[i] = result
-
-
-def back_kernel(grad_ref, second_ref, slope_ref, act_ref, hidden_ref, inputs_ref, out_ref):
-    acc = jnp.zeros((OWN, 128), F32)
+def back_kernel(grad_ref, slope_ref, back_ref, second_ref, out_ref):
+    acc = back_ref[...]
     for v in range(VIS):
         ig = jnp.concatenate([grad_ref[2 * v], grad_ref[2 * v + 1]], axis=1)
         acc = acc + dot(ig, second_ref[v], 1, 1)
         out_ref[v, :, 0:256] = ig
-        out_ref[v, :, 1024:1152] = inputs_ref[2 * v]
-        out_ref[v, :, 1152:1280] = inputs_ref[2 * v + 1]
     act = (acc * slope_ref[...]).astype(BF16)
-    both = jnp.concatenate([act, act_ref[...], hidden_ref[...]], axis=1)
-    for v in range(VIS):
-        out_ref[v, :, 256:1024] = both
-
-
-def slot_kernel(target_ref, pieces_ref, first_ref, down_ref, out_ref, act_ref, weight):
+    for v in range(VIS):
+        out_ref[v, :, 256:384] = act
+
+
+def slot_kernel(target_ref, pieces_ref, first_ref, down_ref, hidden_ref, out_ref, act_ref, weight):
     weight[SPLIT:LANES, :] = jnp.zeros((LANES - SPLIT, 128), BF16)
     weight[0:SPLIT, :] = first_ref[...]
     act = pieces_ref[:, :, 256:384].reshape(ROWS, 128)
     act = dot(selection(target_ref), act, 0, 0).astype(BF16)
     act_ref[...] = act
     out_ref[:, :, 0:LANES] = dot(act, weight[...], 1, 1).astype(BF16).reshape(RC, VIS, LANES)
-    block = dot(pieces_ref[:, :, 512:1024].reshape(ROWS, 512), down_ref[...])
+    hidden = jnp.concatenate([hidden_ref[:, k].reshape(ROWS, 128) for k in range(4)], axis=1)
+    block = dot(hidden, down_ref[...])
     block = jnp.concatenate(
         [block[:, 0:128].reshape(RC, 8, 128), block[:, 128:256].reshape(RC, 8, 128)], axis=1
     )
     out_ref[:, :, LANES : LANES + 128] = block.astype(BF16)
 
 
-def weight_grad_kernel(pieces_ref, act_ref, rows_ref, first_ref, second_ref):
-    hidden = pieces_ref[:, :, 384:512].reshape(ROWS, 128)
-    ig = pieces_ref[:, :, 0:256].reshape(ROWS, 256)
-    second_ref[...] = dot(hidden, ig, 0, 0)
+def weight_grad_kernel(pieces_ref, act_ref, rows_ref, hidden_ref, first_ref, second_ref):
+    hidden = hidden_ref[:, 0].reshape(ROWS, 128)
+    ig = pieces_ref[:, :, 0:256].reshape(ROWS, 256).astype(F32) + language_cotangent(rows_ref)
+    second_ref[...] = dot(hidden, ig.astype(BF16), 0, 0)
     rows = rows_ref[:, :, 0:LANES].reshape(RC * VIS, LANES)
     first_ref[...] = dot(rows, act_ref[...], 0, 0)[0:SPLIT, :]
 
 
-def slot_sum_kernel(arrived_ref, pieces_ref, message_ref, out_ref):
+def slot_sum_kernel(arrived_ref, bundles_ref, message_ref, out_ref, inputs, sem):
     r = group_index()
+    v = lax.axis_index("vis")
+    copy = pltpu.make_async_copy(bundles_ref.at[r // 2, pl.ds(2 * v, 2)], inputs, sem)
+    copy.start()
     total = jnp.zeros((VIS, LANES + 128), F32)
     for i in range(RC):
         total = total + arrived_ref[i].astype(F32)
@@ -229,7 +230,8 @@
         message_ref[:, j, :] = total[:, 128 * j : 128 * j + 128]
     part = total[:, LANES : LANES + 128]
     part = jnp.concatenate([part[0:8], part[8:16]], axis=1)
-    piece = pieces_ref[r // 2].astype(F32)[:, 1024:1280]
+    copy.wait()
+    piece = jnp.concatenate([inputs[0].astype(F32), inputs[1].astype(F32)], axis=1)
     out_ref[...] = (jnp.where(r % 2 == 0, piece[0:8], piece[8:16]) + part).astype(BF16)
 
 
@@ -249,11 +251,17 @@
     return pl.BlockSpec(shape, lambda i: zeros)
 
 
-def call(kernel, outs, *args, scratch=()):
+def in_hbm(array):
+    return pltpu.with_memory_space_constraint(array, pltpu.HBM)
+
+
+def call(kernel, outs, *args, scratch=(), specs=()):
     ins = [
         pl.BlockSpec(memory_space=pltpu.SMEM) if a.dtype == jnp.int32 and a.ndim == 1 else full(a.shape)
         for a in args
     ]
+    if specs:
+        ins[-len(specs) :] = specs
     return pl.pallas_call(
         kernel,
         grid=(1,),
@@ -272,9 +280,12 @@
 def on_device(
     images, counts, block_order, gain, proj_first, bias, proj_second, gate_w, up_w, down_w, cotangent
 ):
-    seconds = lax.all_gather(proj_second, "vis")
-    packed = call(pack_kernel, struct((1024, 256), BF16), gate_w, up_w)
-    weights = lax.all_gather(packed, "vis")
+    proj_first, proj_second, gate_w, up_w, down_w = map(
+        in_hbm, (proj_first, proj_second, gate_w, up_w, down_w)
+    )
+    packed = call(pack_kernel, struct((1152, 256), BF16), gate_w, up_w, proj_second)
+    weights = in_hbm(lax.all_gather(packed, "vis"))
+    seconds = pl.BlockSpec((VIS, 128, 256), lambda i: (0, 8, 0))
     message, hat, gains, scale = call(
         norm_kernel,
         (
@@ -283,54 +294,61 @@
             struct((VIS, LANES), F32),
             struct((8, 128), F32),
         ),
-        images,
+        in_hbm(images),
         gain.reshape(1, -1),
         scratch=[pltpu.VMEM((VIS, LANES), F32), pltpu.VMEM((VIS, LANES), F32)],
     )
     arrived = swap(message, "vis")
-    spread = call(spread_kernel, struct((RC, VIS, 640), BF16), arrived, cotangent)
+    spread = call(spread_kernel, struct((RC, VIS, 640), BF16), arrived, in_hbm(cotangent))
     rows = swap(spread, GROUP)
     partial, target = call(
         first_kernel,
-        (struct((VIS, OWN, 896), BF16), struct((8, RC * VIS), jnp.int32)),
-        counts,
-        block_order,
+        (struct((VIS, OWN, 768), BF16), struct((8, RC * VIS), jnp.int32)),
+        in_hbm(counts),
+        in_hbm(block_order),
         rows,
         proj_first,
+        proj_second,
         down_w,
         scratch=[pltpu.VMEM((LANES, 128), BF16), pltpu.SMEM((VIS,), jnp.int32)],
     )
     pieces = swap(partial, "vis")
-    input_part, hidden_proj, slope = call(
+    input_part, hidden_proj, slope, back = call(
         second_kernel,
-        (struct((RC, OWN, 128), BF16), struct((OWN, 128), BF16), struct((OWN, 128), F32)),
+        (
+            struct((RC, OWN, 128), BF16),
+            struct((OWN, 128), BF16),
+            struct((OWN, 128), F32),
+            struct((OWN, 128), F32),
+        ),
         pieces,
-        bias.reshape(1, -1),
-        seconds,
-    )
-    spread = call(input_sum_kernel, struct((RC, OWN, 128), BF16), swap(input_part, GROUP))
+        in_hbm(bias.reshape(1, -1)),
+        weights,
+        specs=[seconds],
+    )
+    spread = call(sum_kernel, struct((RC, OWN, 128), BF16), swap(input_part, GROUP))
     inputs = swap(spread, GROUP)
-    block_part, hidden = pl.pallas_call(
+    block_part, bundle = pl.pallas_call(
         block_kernel,
-        out_shape=(struct((RC, OWN, 128), BF16), struct((OWN, 512), BF16)),
+        out_shape=(struct((RC, OWN, 128), BF16), struct((37, OWN, 128), BF16)),
         grid=(2, VIS),
         in_specs=[
             pl.BlockSpec((2, OWN, 128), lambda p, v: ((1 - p) * v, 0, 0)),
-            pl.BlockSpec((VIS, OWN, 896), lambda p, v: (0, 0, 0)),
+            pl.BlockSpec((VIS, OWN, 512), lambda p, v: (0, 0, 0)),
+            pl.BlockSpec((OWN, 128), lambda p, v: (0, 0)),
             pl.BlockSpec((1, 1024, 256), lambda p, v: (v, 0, 0)),
         ],
         out_specs=(
             pl.BlockSpec((2, OWN, 128), lambda p, v: (p * v, 0, 0)),
-            pl.BlockSpec((OWN, 512), lambda p, v: (0, 0)),
+            pl.BlockSpec((37, OWN, 128), lambda p, v: (0, 0, 0)),
         ),
         scratch_shapes=[pltpu.VMEM((OWN, 512), F32)] * 2 + [pltpu.VMEM((OWN, 512), BF16)] * 2,
         compiler_params=params(),
-    )(inputs, pieces, weights)
-    spread = call(grad_sum_kernel, struct((RC, OWN, 128), BF16), swap(block_part, GROUP), pieces)
+    )(inputs, pieces, hidden_proj, weights)
+    bundles = in_hbm(lax.all_gather(bundle, "vis"))
+    spread = call(sum_kernel, struct((RC, OWN, 128), BF16), swap(block_part, GROUP))
     whole = swap(spread, GROUP)
-    sent = call(
-        back_kernel, struct((VIS, OWN, 1280), BF16), whole, seconds, slope, hidden_proj, hidden, inputs
-    )
+    sent = call(back_kernel, struct((VIS, OWN, 384), BF16), whole, slope, back, weights, specs=[seconds])
     blocks = swap(sent, "vis")
     slot_part, acts = call(
         slot_kernel,
@@ -339,7 +357,9 @@
         blocks,
         proj_first,
         down_w,
+        bundles,
         scratch=[pltpu.VMEM((LANES, 128), BF16)],
+        specs=[pl.BlockSpec((VIS, 4, OWN, 128), lambda i: (0, 8, 0, 0))],
     )
     slots = swap(slot_part, GROUP)
     first_grad, second_grad = call(
@@ -348,9 +368,16 @@
         blocks,
         acts,
         rows,
+        bundles,
+        specs=[pl.BlockSpec((VIS, 1, OWN, 128), lambda i: (0, 36, 0, 0))],
     )
     message, block_out = call(
-        slot_sum_kernel, (struct((VIS, 8, 128), F32), struct((8, 256), BF16)), slots, blocks
+        slot_sum_kernel,
+        (struct((VIS, 8, 128), F32), struct((8, 256), BF16)),
+        slots,
+        bundles,
+        scratch=[pltpu.VMEM((2, OWN, 128), BF16), pltpu.SemaphoreType.DMA],
+        specs=[pl.BlockSpec(memory_space=pl.ANY)],
     )
     image_grad = call(
         norm_back_kernel, struct((1, VIS * SPLIT), F32), swap(message, "vis"), hat, gains, scale

time: 237 us -> 237 us (level)
  waiting for transfers between devices: 31.3 us -> 9.31 us
  Pallas kernels: 14.5 us -> 36.3 us
  blocking collectives: 151 us -> 168 us
  local copies, waits for them, and re-layouts: 12.5 us -> 0.77 us
  starting transfers between devices: 12.9 us -> 7.49 us
    all_to_all x2 -> x1, waiting for transfers between devices: 26.7 us -> 5.92 us  [swap(): return lax.all_to_all(blocks, axes, 0, 0, tiled=True)]
    all_to_all x8 -> x9, blocking collectives: 151 us -> 168 us  [swap(): return lax.all_to_all(blocks, axes, 0, 0, tiled=True)]
    pallas_call x1, Pallas kernels: 7.05 us -> 21.6 us  [on_device(): pl.pallas_call(block_kernel, out_shape=(struct((RC, OWN, 128), BF16), str...]
    unnamed x28 -> x0, local copies, waits for them, and re-layouts: 11.7 us -> none
    pallas_call x12, Pallas kernels: 7.41 us -> 14.7 us  [call(): pl.pallas_call(kernel, grid=(1,), out_shape=outs, in_specs=ins, out_specs...]
    all_to_all x2 -> x1, starting transfers between devices: 12.8 us -> 7.41 us  [swap(): return lax.all_to_all(blocks, axes, 0, 0, tiled=True)]
  transfers between devices with their start and end apart: 4 -> 3, of which waited for: 3 -> 2; matrix products, arithmetic and copies ran while one was open for 0% -> 0% of each run, Pallas kernels for 2% -> 3%
where the time goes in v3:
time: 237 us; the launch traced here: 236 us
  blocking collectives  168 us (71%)
  Pallas kernels  36.3 us (15%)
  between operations  14.1 us (6%)
  waiting for transfers between devices  9.31 us (4%)
  starting transfers between devices  7.49 us (3%)
    all_to_all x9, blocking collectives, swap(): return lax.all_to_all(blocks, axes, 0, 0, tiled=True)  168 us
    pallas_call x1, Pallas kernels, on_device(): pl.pallas_call(block_kernel, out_shape=(struct((RC, OWN, 128), BF16), str...  21.6 us
    pallas_call x12, Pallas kernels, call(): pl.pallas_call(kernel, grid=(1,), out_shape=outs, in_specs=ins, out_specs...  14.7 us
    all_to_all x1, starting transfers between devices, swap(): return lax.all_to_all(blocks, axes, 0, 0, tiled=True)  7.41 us
    all_to_all x1, waiting for transfers between devices, swap(): return lax.all_to_all(blocks, axes, 0, 0, tiled=True)  5.92 us
  transfers between devices with their start and end apart: 3, of which 2 were waited for; matrix products, arithmetic and copies ran while one was open for 0% of the time, Pallas kernels for 3%

profile of v3, /device:TPU:1, one launch (start us, length us, event | category | flops | bytes accessed | tf_op | source)
XLA Modules:
  0.0 235.8 jit_solution(8454087229786704799)
XLA Ops:
  7.2 1.9 shard_map.141
  9.2 0.8 reshape.14.gain_ref
  10.0 1.1 shard_map.138
  11.1 17.1 %all_to_all.50.arrived_ref = f32[16,8,128]{2,1,0:T(8,128)S(1)} all-to-all(f32[16,8,128]{2,1,0:T(8,128)S(1)} %get-tuple-element.22), channel_id=1, replica_groups=mesh['vis'=16,'row'=4,'col'=8] {'vis'}, dimensions={0} | all-to-all | bytes 131072 | tf_op jit(solution)/shard_map/all_to_all | solution.py:277
  28.2 0.7 shard_map.139
  28.9 28.5 %all_to_all.51.rows_ref = bf16[32,16,640]{2,1,0:T(8,128)(2,1)S(1)} all-to-all(bf16[32,16,640]{2,1,0:T(8,128)(2,1)S(1)} %shard_map.139), channel_id=1, replica_groups=mesh['vis'=16,'row'=4,'col'=8] {'row','col'}, dimensions={0} | all-to-all | bytes 1310720 | tf_op jit(solution)/shard_map/all_to_all | solution.py:277
  57.5 2.0 shard_map.140
  59.5 24.8 %all_to_all.52.arrived_ref.pieces_ref = bf16[16,16,768]{2,1,0:T(8,128)(2,1)S(1)} all-to-all(bf16[16,16,768]{2,1,0:T(8,128)(2,1)S(1)} %get-tuple-element.24), channel_id=1, replica_groups=mesh['vis'=16,'row'=4,'col'=8] {'vis'}, dimensions={0} | all-to-all | bytes 786432 | tf_op jit(solution)/shard_map/all_to_all | solution.py:277
  84.3 3.4 %all-gather.5.cloned.1.call-done = bf16[18432,256]{1,0:T(8,128)(2,1)} async-done(((bf16[1152,256]{1,0:T(8,128)(2,1)}), bf16[18432,256]{1,0:T(8,128)(2,1)}) %all-gather.5.cloned.1.call-update) | async-done | bytes 9437200 | tf_op jit(solution)/shard_map/all_gather | solution.py:287
  87.6 1.5 shard_map.142
  89.1 18.9 %all_to_all.53.arrived_ref = bf16[32,16,128]{2,1,0:T(8,128)(2,1)S(1)} all-to-all(bf16[32,16,128]{2,1,0:T(8,128)(2,1)S(1)} %get-tuple-element.25), channel_id=1, replica_groups=mesh['vis'=16,'row'=4,'col'=8] {'row','col'}, dimensions={0} | all-to-all | bytes 262144 | tf_op jit(solution)/shard_map/all_to_all | solution.py:277
  108.1 13.4 %all_to_all.54.inputs_ref = bf16[32,16,128]{2,1,0:T(8,128)(2,1)S(1)} all-to-all(bf16[32,16,128]{2,1,0:T(8,128)(2,1)S(1)} %shard_map.143), channel_id=1, replica_groups=mesh['vis'=16,'row'=4,'col'=8] {'row','col'}, dimensions={0} | all-to-all | bytes 262144 | tf_op jit(solution)/shard_map/all_to_all | solution.py:277
  121.4 21.6 %shard_map.144 = (bf16[32,16,128]{2,1,0:T(8,128)(2,1)S(1)}, bf16[37,16,128]{2,1,0:T(8,128)(2,1)}) custom-call(bf16[32,16,128]{2,1,0:T(8,128)(2,1)S(1)} %all_to_all.54.inputs_ref, bf16[16,16,768]{2,1,0:T(8,128)(2,1)S(1)} %all_to_all.52.arrived_ref.pieces_ref, bf16[16,128]{1,0:T(8,128)(2,1)S(1)} %get-tuple-element.26.act_ref, bf16[16,1152,256]{2,1,0:T(8,128)(2,1)} %bitcast.4), custom_call_target="tpu_custom_call" | custom-call | tf_op jit(solution)/shard_map/pallas_call | solution.py:331
  143.0 12.7 %all_to_all.55.arrived_ref = bf16[32,16,128]{2,1,0:T(8,128)(2,1)S(1)} all-to-all(bf16[32,16,128]{2,1,0:T(8,128)(2,1)S(1)} %get-tuple-element.27), channel_id=1, replica_groups=mesh['vis'=16,'row'=4,'col'=8] {'row','col'}, dimensions={0} | all-to-all | bytes 262144 | tf_op jit(solution)/shard_map/all_to_all | solution.py:277
  155.8 12.7 %all_to_all.56.grad_ref = bf16[32,16,128]{2,1,0:T(8,128)(2,1)S(1)} all-to-all(bf16[32,16,128]{2,1,0:T(8,128)(2,1)S(1)} %shard_map.145), channel_id=1, replica_groups=mesh['vis'=16,'row'=4,'col'=8] {'row','col'}, dimensions={0} | all-to-all | bytes 262144 | tf_op jit(solution)/shard_map/all_to_all | solution.py:277
  168.5 1.7 shard_map.146
  170.2 19.4 %all_to_all.57.pieces_ref = bf16[16,16,384]{2,1,0:T(8,128)(2,1)S(1)} all-to-all(bf16[16,16,384]{2,1,0:T(8,128)(2,1)S(1)} %shard_map.146), channel_id=1, replica_groups=mesh['vis'=16,'row'=4,'col'=8] {'vis'}, dimensions={0} | all-to-all | bytes 393216 | tf_op jit(solution)/shard_map/all_to_all | solution.py:277
  189.6 1.7 shard_map.147
  191.3 20.3 %all_to_all.58.arrived_ref = bf16[32,16,640]{2,1,0:T(8,128)(2,1)S(1)} all-to-all(bf16[32,16,640]{2,1,0:T(8,128)(2,1)S(1)} %get-tuple-element.31), channel_id=1, replica_groups=mesh['vis'=16,'row'=4,'col'=8] {'row','col'}, dimensions={0} | all-to-all | bytes 1310720 | tf_op jit(solution)/shard_map/all_to_all | solution.py:277
  211.6 1.3 shard_map.148
  212.9 7.4 %all-to-all-start.9 = ((f32[16,8,128]{2,1,0:T(8,128)}), f32[16,8,128]{2,1,0:T(8,128)S(1)}, u32[]{:S(2)}, u32[]{:S(2)}) async-start(f32[16,8,128]{2,1,0:T(8,128)} %get-tuple-element.33), calls=%async_computation.9 | async-start | bytes 131072 | tf_op jit(solution)/shard_map/all_to_all | solution.py:277
  220.3 1.9 shard_map.150
  222.2 5.9 %all-to-all-done.9.arrived_ref = f32[16,8,128]{2,1,0:T(8,128)S(1)} async-done(((f32[16,8,128]{2,1,0:T(8,128)}), f32[16,8,128]{2,1,0:T(8,128)S(1)}, u32[]{:S(2)}, u32[]{:S(2)}) %all-to-all-start.9) | async-done | bytes 65568 | tf_op jit(solution)/shard_map/all_to_all | solution.py:277
  228.1 0.8 shard_map.149
  (7 shorter events, 0.2 us)
Async XLA Ops:
  7.2 80.4 %all-gather.5.cloned.1.call-start = ((), (), s32[]{:S(2)}) async-start(), calls=%async_computation.10 | async-start | bytes 10027008 | tf_op jit(solution)/shard_map/all_gather | solution.py:287
  9.1 180.5 %all-gather.7.cloned.1.call-start = ((), (), s32[]{:S(2)}) async-start(), calls=%async_computation.11 | async-start | bytes 2576384 | tf_op jit(solution)/shard_map/all_gather | solution.py:348
  212.9 15.2 %all-to-all-start.9 = ((f32[16,8,128]{2,1,0:T(8,128)}), f32[16,8,128]{2,1,0:T(8,128)S(1)}, u32[]{:S(2)}, u32[]{:S(2)}) async-start(f32[16,8,128]{2,1,0:T(8,128)} %get-tuple-element.33), calls=%async_computation.9 | async-start | bytes 131072 | tf_op jit(solution)/shard_map/all_to_all | solution.py:277
Sparse Core Ops, SparseCore 0:
  10.1 77.4 all-gather.4
  143.2 37.3 all-gather.6

commit v4 on v3

--- a/solution.py
+++ b/solution.py
@@ -284,7 +284,8 @@
         in_hbm, (proj_first, proj_second, gate_w, up_w, down_w)
     )
     packed = call(pack_kernel, struct((1152, 256), BF16), gate_w, up_w, proj_second)
-    weights = in_hbm(lax.all_gather(packed, "vis"))
+    gathered = lax.all_gather(packed, "vis")
+    weights = in_hbm(gathered)
     seconds = pl.BlockSpec((VIS, 128, 256), lambda i: (0, 8, 0))
     message, hat, gains, scale = call(
         norm_kernel,
@@ -344,7 +345,7 @@
         ),
         scratch_shapes=[pltpu.VMEM((OWN, 512), F32)] * 2 + [pltpu.VMEM((OWN, 512), BF16)] * 2,
         compiler_params=params(),
-    )(inputs, pieces, hidden_proj, weights)
+    )(inputs, pieces, hidden_proj, gathered)
     bundles = in_hbm(lax.all_gather(bundle, "vis"))
     spread = call(sum_kernel, struct((RC, OWN, 128), BF16), swap(block_part, GROUP))
     whole = swap(spread, GROUP)

time: 237 us -> 223 us (0.941)
  Pallas kernels: 36.3 us -> 22.7 us
    pallas_call x1, Pallas kernels: 21.6 us -> 7.78 us  [on_device(): pl.pallas_call(block_kernel, out_shape=(struct((RC, OWN, 128), BF16), str...]
where the time goes in v4:
time: 223 us; the launch traced here: 222 us
  blocking collectives  168 us (75%)
  Pallas kernels  22.7 us (10%)
  between operations  14.1 us (6%)
  waiting for transfers between devices  9.32 us (4%)
  starting transfers between devices  7.49 us (3%)
    all_to_all x9, blocking collectives, swap(): return lax.all_to_all(blocks, axes, 0, 0, tiled=True)  168 us
    pallas_call x12, Pallas kernels, call(): pl.pallas_call(kernel, grid=(1,), out_shape=outs, in_specs=ins, out_specs...  14.9 us
    pallas_call x1, Pallas kernels, on_device(): pl.pallas_call(block_kernel, out_shape=(struct((RC, OWN, 128), BF16), str...  7.78 us
    all_to_all x1, starting transfers between devices, swap(): return lax.all_to_all(blocks, axes, 0, 0, tiled=True)  7.4 us
    all_to_all x1, waiting for transfers between devices, swap(): return lax.all_to_all(blocks, axes, 0, 0, tiled=True)  5.92 us
  transfers between devices with their start and end apart: 3, of which 2 were waited for; matrix products, arithmetic and copies ran while one was open for 0% of the time, Pallas kernels for 3%

profile of v4, /device:TPU:1, one launch (start us, length us, event | category | flops | bytes accessed | tf_op | source)
XLA Modules:
  0.0 222.4 jit_solution(13962951577610951941)
XLA Ops:
  7.2 1.9 shard_map.141
  9.2 0.8 reshape.14.gain_ref
  9.9 1.1 shard_map.138
  11.1 17.1 %all_to_all.50.arrived_ref = f32[16,8,128]{2,1,0:T(8,128)S(1)} all-to-all(f32[16,8,128]{2,1,0:T(8,128)S(1)} %get-tuple-element.22), channel_id=1, replica_groups=mesh['vis'=16,'row'=4,'col'=8] {'vis'}, dimensions={0} | all-to-all | bytes 131072 | tf_op jit(solution)/shard_map/all_to_all | solution.py:277
  28.2 0.7 shard_map.139
  28.9 28.5 %all_to_all.51.rows_ref = bf16[32,16,640]{2,1,0:T(8,128)(2,1)S(1)} all-to-all(bf16[32,16,640]{2,1,0:T(8,128)(2,1)S(1)} %shard_map.139), channel_id=1, replica_groups=mesh['vis'=16,'row'=4,'col'=8] {'row','col'}, dimensions={0} | all-to-all | bytes 1310720 | tf_op jit(solution)/shard_map/all_to_all | solution.py:277
  57.5 2.0 shard_map.140
  59.5 24.8 %all_to_all.52.arrived_ref.pieces_ref = bf16[16,16,768]{2,1,0:T(8,128)(2,1)S(1)} all-to-all(bf16[16,16,768]{2,1,0:T(8,128)(2,1)S(1)} %get-tuple-element.24), channel_id=1, replica_groups=mesh['vis'=16,'row'=4,'col'=8] {'vis'}, dimensions={0} | all-to-all | bytes 786432 | tf_op jit(solution)/shard_map/all_to_all | solution.py:277
  84.2 3.4 %all-gather.5.cloned.1.call-done = bf16[18432,256]{1,0:T(8,128)(2,1)} async-done(((bf16[1152,256]{1,0:T(8,128)(2,1)}), bf16[18432,256]{1,0:T(8,128)(2,1)}) %all-gather.5.cloned.1.call-update) | async-done | bytes 9437200 | tf_op jit(solution)/shard_map/all_gather | solution.py:287
  87.6 1.6 shard_map.142
  89.3 19.2 %all_to_all.53.arrived_ref = bf16[32,16,128]{2,1,0:T(8,128)(2,1)S(1)} all-to-all(bf16[32,16,128]{2,1,0:T(8,128)(2,1)S(1)} %get-tuple-element.25), channel_id=1, replica_groups=mesh['vis'=16,'row'=4,'col'=8] {'row','col'}, dimensions={0} | all-to-all | bytes 262144 | tf_op jit(solution)/shard_map/all_to_all | solution.py:277
  108.5 13.4 %all_to_all.54.inputs_ref = bf16[32,16,128]{2,1,0:T(8,128)(2,1)S(1)} all-to-all(bf16[32,16,128]{2,1,0:T(8,128)(2,1)S(1)} %shard_map.143), channel_id=1, replica_groups=mesh['vis'=16,'row'=4,'col'=8] {'row','col'}, dimensions={0} | all-to-all | bytes 262144 | tf_op jit(solution)/shard_map/all_to_all | solution.py:277
  121.8 7.8 %shard_map.144 = (bf16[32,16,128]{2,1,0:T(8,128)(2,1)S(1)}, bf16[37,16,128]{2,1,0:T(8,128)(2,1)}) custom-call(bf16[32,16,128]{2,1,0:T(8,128)(2,1)S(1)} %all_to_all.54.inputs_ref, bf16[16,16,768]{2,1,0:T(8,128)(2,1)S(1)} %all_to_all.52.arrived_ref.pieces_ref, bf16[16,128]{1,0:T(8,128)(2,1)S(1)} %get-tuple-element.26.act_ref, bf16[16,1152,256]{2,1,0:T(8,128)(2,1)S(1)} %bitcast.5), custom_call_target="tpu_custom_call" | custom-call | tf_op jit(solution)/shard_map/pallas_call | solution.py:332
  129.6 12.7 %all_to_all.55.arrived_ref = bf16[32,16,128]{2,1,0:T(8,128)(2,1)S(1)} all-to-all(bf16[32,16,128]{2,1,0:T(8,128)(2,1)S(1)} %get-tuple-element.27), channel_id=1, replica_groups=mesh['vis'=16,'row'=4,'col'=8] {'row','col'}, dimensions={0} | all-to-all | bytes 262144 | tf_op jit(solution)/shard_map/all_to_all | solution.py:277
  142.4 12.7 %all_to_all.56.grad_ref = bf16[32,16,128]{2,1,0:T(8,128)(2,1)S(1)} all-to-all(bf16[32,16,128]{2,1,0:T(8,128)(2,1)S(1)} %shard_map.145), channel_id=1, replica_groups=mesh['vis'=16,'row'=4,'col'=8] {'row','col'}, dimensions={0} | all-to-all | bytes 262144 | tf_op jit(solution)/shard_map/all_to_all | solution.py:277
  155.1 1.6 shard_map.146
  156.8 19.4 %all_to_all.57.pieces_ref = bf16[16,16,384]{2,1,0:T(8,128)(2,1)S(1)} all-to-all(bf16[16,16,384]{2,1,0:T(8,128)(2,1)S(1)} %shard_map.146), channel_id=1, replica_groups=mesh['vis'=16,'row'=4,'col'=8] {'vis'}, dimensions={0} | all-to-all | bytes 393216 | tf_op jit(solution)/shard_map/all_to_all | solution.py:277
  176.2 1.7 shard_map.147
  177.9 20.3 %all_to_all.58.arrived_ref = bf16[32,16,640]{2,1,0:T(8,128)(2,1)S(1)} all-to-all(bf16[32,16,640]{2,1,0:T(8,128)(2,1)S(1)} %get-tuple-element.31), channel_id=1, replica_groups=mesh['vis'=16,'row'=4,'col'=8] {'row','col'}, dimensions={0} | all-to-all | bytes 1310720 | tf_op jit(solution)/shard_map/all_to_all | solution.py:277
  198.2 1.3 shard_map.148
  199.5 7.4 %all-to-all-start.9 = ((f32[16,8,128]{2,1,0:T(8,128)}), f32[16,8,128]{2,1,0:T(8,128)S(1)}, u32[]{:S(2)}, u32[]{:S(2)}) async-start(f32[16,8,128]{2,1,0:T(8,128)} %get-tuple-element.33), calls=%async_computation.9 | async-start | bytes 131072 | tf_op jit(solution)/shard_map/all_to_all | solution.py:277
  206.9 1.9 shard_map.150
  208.8 5.9 %all-to-all-done.9.arrived_ref = f32[16,8,128]{2,1,0:T(8,128)S(1)} async-done(((f32[16,8,128]{2,1,0:T(8,128)}), f32[16,8,128]{2,1,0:T(8,128)S(1)}, u32[]{:S(2)}, u32[]{:S(2)}) %all-to-all-start.9) | async-done | bytes 65568 | tf_op jit(solution)/shard_map/all_to_all | solution.py:277
  214.7 0.8 shard_map.149
  (9 shorter events, 0.2 us)
Async XLA Ops:
  7.2 80.4 %all-gather.5.cloned.1.call-start = ((), (), s32[]{:S(2)}) async-start(), calls=%async_computation.10 | async-start | bytes 10027008 | tf_op jit(solution)/shard_map/all_gather | solution.py:287
  9.1 167.1 %all-gather.7.cloned.1.call-start = ((), (), s32[]{:S(2)}) async-start(), calls=%async_computation.11 | async-start | bytes 2576384 | tf_op jit(solution)/shard_map/all_gather | solution.py:349
  87.6 34.2 %copy-start = (bf16[18432,256]{1,0:T(8,128)(2,1)S(1)}, bf16[18432,256]{1,0:T(8,128)(2,1)}, u32[]{:S(2)}) copy-start(bf16[18432,256]{1,0:T(8,128)(2,1)} %all-gather.5.cloned.1.call-done) | copy-start | bytes 28311556
  199.5 15.2 %all-to-all-start.9 = ((f32[16,8,128]{2,1,0:T(8,128)}), f32[16,8,128]{2,1,0:T(8,128)S(1)}, u32[]{:S(2)}, u32[]{:S(2)}) async-start(f32[16,8,128]{2,1,0:T(8,128)} %get-tuple-element.33), calls=%async_computation.9 | async-start | bytes 131072 | tf_op jit(solution)/shard_map/all_to_all | solution.py:277
Sparse Core Ops, SparseCore 0:
  10.1 77.4 all-gather.4
  129.8 37.3 all-gather.6

commit v5 on v4

--- a/solution.py
+++ b/solution.py
@@ -3,6 +3,7 @@
 from jax import lax
 from jax.experimental import pallas as pl
 from jax.experimental.pallas import tpu as pltpu
+from jax.sharding import Mesh
 from jax.sharding import PartitionSpec as P
 
 VIS = 16
@@ -13,7 +14,10 @@
 LANES = 512
 F32 = jnp.float32
 BF16 = jnp.bfloat16
+PAIR = 2
+CHIPS = VIS // PAIR
 GROUP = ("row", "col")
+OWNERS = ("chip", "core")
 
 
 def struct(shape, dtype):
@@ -32,12 +36,20 @@
     return lax.axis_index("row") * lax.axis_size("col") + lax.axis_index("col")
 
 
-def pack_kernel(gate_ref, up_ref, second_ref, out_ref):
-    out_ref[0:256, :] = gate_ref[:, 0:256]
-    out_ref[256:512, :] = gate_ref[:, 256:512]
-    out_ref[512:768, :] = up_ref[:, 0:256]
-    out_ref[768:1024, :] = up_ref[:, 256:512]
-    out_ref[1024:1152, :] = second_ref[...]
+def pack_kernel(gate_ref, up_ref, second_ref, out_ref, sems):
+    parts = [(gate_ref, 0), (gate_ref, 256), (up_ref, 0), (up_ref, 256), (second_ref, 0)]
+    copies = []
+    for i, (ref, column) in enumerate(parts):
+        rows = ref.shape[0]
+        copies.append(
+            pltpu.make_async_copy(
+                ref.at[:, pl.ds(column, 256)], out_ref.at[pl.ds(256 * i, rows), :], sems.at[i]
+            )
+        )
+    for copy in copies:
+        copy.start()
+    for copy in copies:
+        copy.wait()
 
 
 def norm_kernel(images_ref, gain_ref, message_ref, hat_ref, gain_out, scale_ref, values, gains):
@@ -108,14 +120,20 @@
     cot = language_cotangent(rows_ref).astype(BF16)
     grad = dot(cot, down_ref[...], 1, 1).astype(BF16)
     back = dot(cot, second_ref[...], 1, 1).astype(BF16)
-    out_ref[:, :, 0:512] = grad.reshape(VIS, OWN, 512)
-    out_ref[:, :, 512:640] = pre.reshape(VIS, OWN, 128)
-    out_ref[:, :, 640:768] = back.reshape(VIS, OWN, 128)
+    for i in range(VIS):
+        own = slice(OWN * i, OWN * i + OWN)
+        out_ref[i % PAIR, i // PAIR, :, 0:512] = grad[own]
+        out_ref[i % PAIR, i // PAIR, :, 512:640] = pre[own]
+        out_ref[i % PAIR, i // PAIR, :, 640:768] = back[own]
+
+
+def pair_kernel(arrived_ref, out_ref):
+    out_ref[...] = (arrived_ref[0].astype(F32) + arrived_ref[1].astype(F32)).astype(BF16)
 
 
 def second_kernel(arrived_ref, bias_ref, weight_ref, out_ref, hidden_ref, slope_ref, back_ref):
     both = jnp.zeros((OWN, 256), F32)
-    for v in range(VIS):
+    for v in range(CHIPS):
         both = both + arrived_ref[v, :, 512:768].astype(F32)
     pre = both[:, 0:128] + bias_ref[...]
     back_ref[...] = both[:, 128:256]
@@ -162,7 +180,7 @@
     @pl.when(jnp.logical_and(phase == 1, v == 0))
     def _():
         h = jnp.zeros((OWN, 512), F32)
-        for i in range(VIS):
+        for i in range(CHIPS):
             h = h + pieces_ref[i].astype(F32)
         g, u = gate[...], up[...]
         s = jax.nn.sigmoid(g)
@@ -219,7 +237,7 @@
 
 def slot_sum_kernel(arrived_ref, bundles_ref, message_ref, out_ref, inputs, sem):
     r = group_index()
-    v = lax.axis_index("vis")
+    v = lax.axis_index("chip") * PAIR + lax.axis_index("core")
     copy = pltpu.make_async_copy(bundles_ref.at[r // 2, pl.ds(2 * v, 2)], inputs, sem)
     copy.start()
     total = jnp.zeros((VIS, LANES + 128), F32)
@@ -280,11 +298,14 @@
 def on_device(
     images, counts, block_order, gain, proj_first, bias, proj_second, gate_w, up_w, down_w, cotangent
 ):
-    proj_first, proj_second, gate_w, up_w, down_w = map(
-        in_hbm, (proj_first, proj_second, gate_w, up_w, down_w)
-    )
-    packed = call(pack_kernel, struct((1152, 256), BF16), gate_w, up_w, proj_second)
-    gathered = lax.all_gather(packed, "vis")
+    packed = pl.pallas_call(
+        pack_kernel,
+        out_shape=struct((1152, 256), BF16),
+        in_specs=[pl.BlockSpec(memory_space=pl.ANY)] * 3,
+        out_specs=pl.BlockSpec(memory_space=pl.ANY),
+        scratch_shapes=[pltpu.SemaphoreType.DMA((5,))],
+    )(in_hbm(gate_w), in_hbm(up_w), in_hbm(proj_second))
+    gathered = lax.all_gather(packed, OWNERS)
     weights = in_hbm(gathered)
     seconds = pl.BlockSpec((VIS, 128, 256), lambda i: (0, 8, 0))
     message, hat, gains, scale = call(
@@ -299,21 +320,22 @@
         gain.reshape(1, -1),
         scratch=[pltpu.VMEM((VIS, LANES), F32), pltpu.VMEM((VIS, LANES), F32)],
     )
-    arrived = swap(message, "vis")
+    arrived = swap(message, OWNERS)
     spread = call(spread_kernel, struct((RC, VIS, 640), BF16), arrived, in_hbm(cotangent))
     rows = swap(spread, GROUP)
     partial, target = call(
         first_kernel,
-        (struct((VIS, OWN, 768), BF16), struct((8, RC * VIS), jnp.int32)),
+        (struct((PAIR, CHIPS, OWN, 768), BF16), struct((8, RC * VIS), jnp.int32)),
         in_hbm(counts),
         in_hbm(block_order),
         rows,
-        proj_first,
-        proj_second,
-        down_w,
+        in_hbm(proj_first),
+        in_hbm(proj_second),
+        in_hbm(down_w),
         scratch=[pltpu.VMEM((LANES, 128), BF16), pltpu.SMEM((VIS,), jnp.int32)],
     )
-    pieces = swap(partial, "vis")
+    pairs = call(pair_kernel, struct((CHIPS, OWN, 768), BF16), swap(partial, "core"))
+    pieces = swap(pairs, "chip")
     input_part, hidden_proj, slope, back = call(
         second_kernel,
         (
@@ -335,7 +357,7 @@
         grid=(2, VIS),
         in_specs=[
             pl.BlockSpec((2, OWN, 128), lambda p, v: ((1 - p) * v, 0, 0)),
-            pl.BlockSpec((VIS, OWN, 512), lambda p, v: (0, 0, 0)),
+            pl.BlockSpec((CHIPS, OWN, 512), lambda p, v: (0, 0, 0)),
             pl.BlockSpec((OWN, 128), lambda p, v: (0, 0)),
             pl.BlockSpec((1, 1024, 256), lambda p, v: (v, 0, 0)),
         ],
@@ -346,11 +368,11 @@
         scratch_shapes=[pltpu.VMEM((OWN, 512), F32)] * 2 + [pltpu.VMEM((OWN, 512), BF16)] * 2,
         compiler_params=params(),
     )(inputs, pieces, hidden_proj, gathered)
-    bundles = in_hbm(lax.all_gather(bundle, "vis"))
+    bundles = in_hbm(lax.all_gather(bundle, OWNERS))
     spread = call(sum_kernel, struct((RC, OWN, 128), BF16), swap(block_part, GROUP))
     whole = swap(spread, GROUP)
     sent = call(back_kernel, struct((VIS, OWN, 384), BF16), whole, slope, back, weights, specs=[seconds])
-    blocks = swap(sent, "vis")
+    blocks = swap(sent, OWNERS)
     slot_part, acts = call(
         slot_kernel,
         (struct((RC, VIS, 640), BF16), struct((RC * VIS, 128), BF16)),
@@ -381,29 +403,33 @@
         specs=[pl.BlockSpec(memory_space=pl.ANY)],
     )
     image_grad = call(
-        norm_back_kernel, struct((1, VIS * SPLIT), F32), swap(message, "vis"), hat, gains, scale
+        norm_back_kernel, struct((1, VIS * SPLIT), F32), swap(message, OWNERS), hat, gains, scale
     )
     return block_out, image_grad, first_grad, second_grad
 
 
 def solution(mesh):
-    every = ("vis", "row", "col")
+    every = (*OWNERS, *GROUP)
+    split = Mesh(
+        mesh.devices.reshape(CHIPS, PAIR, mesh.shape["row"], mesh.shape["col"]),
+        ("chip", "core", "row", "col"),
+    )
     return jax.shard_map(
         on_device,
-        mesh=mesh,
+        mesh=split,
         in_specs=(
             P(every, None),
             P(),
             P(),
             P(),
-            P("vis", GROUP),
+            P(OWNERS, GROUP),
             P(GROUP),
-            P(GROUP, "vis"),
-            P("vis", GROUP),
-            P("vis", GROUP),
-            P(GROUP, "vis"),
-            P(GROUP, "vis"),
+            P(GROUP, OWNERS),
+            P(OWNERS, GROUP),
+            P(OWNERS, GROUP),
+            P(GROUP, OWNERS),
+            P(GROUP, OWNERS),
         ),
-        out_specs=(P(GROUP, "vis"), P(every, None), P("vis", GROUP), P(GROUP, "vis")),
+        out_specs=(P(GROUP, OWNERS), P(every, None), P(OWNERS, GROUP), P(GROUP, OWNERS)),
         check_vma=False,
     )

time: 223 us -> 235 us (1.054)
  Pallas kernels: 22.7 us -> 39.7 us
  waiting for transfers between devices: 9.32 us -> 5.95 us
    pallas_call x0 -> x1, Pallas kernels: none -> 19 us  [on_device(): pl.pallas_call(pack_kernel, out_shape=struct((1152, 256), BF16), in_specs...]
    all_gather x2, waiting for transfers between devices: 3.36 us -> 0.01 us  [the longest x1 0.01 us: on_device(): gathered = lax.all_gather(packed, OWNERS)]
    all_to_all x9 -> x10, blocking collectives: 168 us -> 166 us  [swap(): return lax.all_to_all(blocks, axes, 0, 0, tiled=True)]
  transfers between devices with their start and end apart: 3 -> 3, of which waited for: 2 -> 1; matrix products, arithmetic and copies ran while one was open for 0% -> 0% of each run, Pallas kernels for 3% -> 3%
where the time goes in v5:
time: 235 us; the launch traced here: 234 us
  blocking collectives  166 us (71%)
  Pallas kernels  39.7 us (17%)
  between operations  14.1 us (6%)
  starting transfers between devices  7.44 us (3%)
  waiting for transfers between devices  5.95 us (3%)
    all_to_all x10, blocking collectives, swap(): return lax.all_to_all(blocks, axes, 0, 0, tiled=True)  166 us
    pallas_call x1, Pallas kernels, on_device(): pl.pallas_call(pack_kernel, out_shape=struct((1152, 256), BF16), in_specs...  19 us
    pallas_call x12, Pallas kernels, call(): pl.pallas_call(kernel, grid=(1,), out_shape=outs, in_specs=ins, out_specs...  12.9 us
    pallas_call x1, Pallas kernels, on_device(): pl.pallas_call(block_kernel, out_shape=(struct((RC, OWN, 128), BF16), str...  7.77 us
    all_to_all x1, starting transfers between devices, swap(): return lax.all_to_all(blocks, axes, 0, 0, tiled=True)  7.36 us
    all_to_all x1, waiting for transfers between devices, swap(): return lax.all_to_all(blocks, axes, 0, 0, tiled=True)  5.91 us
  transfers between devices with their start and end apart: 3, of which 1 were waited for; matrix products, arithmetic and copies ran while one was open for 0% of the time, Pallas kernels for 3%

profile of v5, /device:TPU:1, one launch (start us, length us, event | category | flops | bytes accessed | tf_op | source)
XLA Modules:
  0.0 234.3 jit_solution(319105729261625459)
XLA Ops:
  7.2 19.0 %shard_map.142 = bf16[1152,256]{1,0:T(8,128)(2,1)} custom-call(bf16[256,512]{1,0:T(8,128)(2,1)} %gate_ref.1, bf16[256,512]{1,0:T(8,128)(2,1)} %up_ref.1, bf16[128,256]{1,0:T(8,128)(2,1)} %second_ref.3), custom_call_target="tpu_custom_call" | custom-call | tf_op jit(solution)/shard_map/pallas_call | solution.py:301
  26.3 0.8 reshape.14.gain_ref
  27.1 1.1 shard_map.138
  28.2 17.1 %all_to_all.55.arrived_ref = f32[16,8,128]{2,1,0:T(8,128)S(1)} all-to-all(f32[16,8,128]{2,1,0:T(8,128)S(1)} %get-tuple-element.22), channel_id=1, replica_groups=mesh['chip'=8,'core'=2,'row'=4,'col'=8] {'chip','core'}, dimensions={0} | all-to-all | bytes 131072 | tf_op jit(solution)/shard_map/all_to_all | solution.py:295
  45.3 0.7 shard_map.139
  46.1 28.9 %all_to_all.56.rows_ref = bf16[32,16,640]{2,1,0:T(8,128)(2,1)S(1)} all-to-all(bf16[32,16,640]{2,1,0:T(8,128)(2,1)S(1)} %shard_map.139), channel_id=1, replica_groups=mesh['chip'=8,'core'=2,'row'=4,'col'=8] {'row','col'}, dimensions={0} | all-to-all | bytes 1310720 | tf_op jit(solution)/shard_map/all_to_all | solution.py:295
  75.0 2.0 shard_map.140
  77.0 7.1 %all_to_all.57.arrived_ref = bf16[2,8,16,768]{3,2,1,0:T(8,128)(2,1)S(1)} all-to-all(bf16[2,8,16,768]{3,2,1,0:T(8,128)(2,1)S(1)} %get-tuple-element.24), channel_id=1, replica_groups=mesh['chip'=8,'core'=2,'row'=4,'col'=8] {'core'}, dimensions={0} | all-to-all | bytes 786432 | tf_op jit(solution)/shard_map/all_to_all | solution.py:295
  84.2 15.1 %all_to_all.58.arrived_ref.pieces_ref = bf16[8,16,768]{2,1,0:T(8,128)(2,1)S(1)} all-to-all(bf16[8,16,768]{2,1,0:T(8,128)(2,1)S(1)} %shard_map.141), channel_id=1, replica_groups=mesh['chip'=8,'core'=2,'row'=4,'col'=8] {'chip'}, dimensions={0} | all-to-all | bytes 393216 | tf_op jit(solution)/shard_map/all_to_all | solution.py:295
  99.3 1.6 shard_map.143
  100.9 19.5 %all_to_all.59.arrived_ref = bf16[32,16,128]{2,1,0:T(8,128)(2,1)S(1)} all-to-all(bf16[32,16,128]{2,1,0:T(8,128)(2,1)S(1)} %get-tuple-element.25), channel_id=1, replica_groups=mesh['chip'=8,'core'=2,'row'=4,'col'=8] {'row','col'}, dimensions={0} | all-to-all | bytes 262144 | tf_op jit(solution)/shard_map/all_to_all | solution.py:295
  120.5 13.4 %all_to_all.60.inputs_ref = bf16[32,16,128]{2,1,0:T(8,128)(2,1)S(1)} all-to-all(bf16[32,16,128]{2,1,0:T(8,128)(2,1)S(1)} %shard_map.144), channel_id=1, replica_groups=mesh['chip'=8,'core'=2,'row'=4,'col'=8] {'row','col'}, dimensions={0} | all-to-all | bytes 262144 | tf_op jit(solution)/shard_map/all_to_all | solution.py:295
  133.8 7.8 %shard_map.145 = (bf16[32,16,128]{2,1,0:T(8,128)(2,1)S(1)}, bf16[37,16,128]{2,1,0:T(8,128)(2,1)}) custom-call(bf16[32,16,128]{2,1,0:T(8,128)(2,1)S(1)} %all_to_all.60.inputs_ref, bf16[8,16,768]{2,1,0:T(8,128)(2,1)S(1)} %all_to_all.58.arrived_ref.pieces_ref, bf16[16,128]{1,0:T(8,128)(2,1)S(1)} %get-tuple-element.26.act_ref, bf16[16,1152,256]{2,1,0:T(8,128)(2,1)S(1)} %bitcast.5), custom_call_target="tpu_custom_call" | custom-call | tf_op jit(solution)/shard_map/pallas_call | solution.py:354
  141.6 12.7 %all_to_all.61.arrived_ref = bf16[32,16,128]{2,1,0:T(8,128)(2,1)S(1)} all-to-all(bf16[32,16,128]{2,1,0:T(8,128)(2,1)S(1)} %get-tuple-element.27), channel_id=1, replica_groups=mesh['chip'=8,'core'=2,'row'=4,'col'=8] {'row','col'}, dimensions={0} | all-to-all | bytes 262144 | tf_op jit(solution)/shard_map/all_to_all | solution.py:295
  154.4 12.7 %all_to_all.62.grad_ref = bf16[32,16,128]{2,1,0:T(8,128)(2,1)S(1)} all-to-all(bf16[32,16,128]{2,1,0:T(8,128)(2,1)S(1)} %shard_map.146), channel_id=1, replica_groups=mesh['chip'=8,'core'=2,'row'=4,'col'=8] {'row','col'}, dimensions={0} | all-to-all | bytes 262144 | tf_op jit(solution)/shard_map/all_to_all | solution.py:295
  167.1 1.7 shard_map.147
  168.8 19.4 %all_to_all.63.pieces_ref = bf16[16,16,384]{2,1,0:T(8,128)(2,1)S(1)} all-to-all(bf16[16,16,384]{2,1,0:T(8,128)(2,1)S(1)} %shard_map.147), channel_id=1, replica_groups=mesh['chip'=8,'core'=2,'row'=4,'col'=8] {'chip','core'}, dimensions={0} | all-to-all | bytes 393216 | tf_op jit(solution)/shard_map/all_to_all | solution.py:295
  188.2 1.5 shard_map.148
  189.8 20.3 %all_to_all.64.arrived_ref = bf16[32,16,640]{2,1,0:T(8,128)(2,1)S(1)} all-to-all(bf16[32,16,640]{2,1,0:T(8,128)(2,1)S(1)} %get-tuple-element.31), channel_id=1, replica_groups=mesh['chip'=8,'core'=2,'row'=4,'col'=8] {'row','col'}, dimensions={0} | all-to-all | bytes 1310720 | tf_op jit(solution)/shard_map/all_to_all | solution.py:295
  210.1 1.4 shard_map.149
  211.5 7.4 %all-to-all-start.10 = ((f32[16,8,128]{2,1,0:T(8,128)}), f32[16,8,128]{2,1,0:T(8,128)S(1)}, u32[]{:S(2)}, u32[]{:S(2)}) async-start(f32[16,8,128]{2,1,0:T(8,128)} %get-tuple-element.33), calls=%async_computation.10 | async-start | bytes 131072 | tf_op jit(solution)/shard_map/all_to_all | solution.py:295
  218.8 1.9 shard_map.151
  220.7 5.9 %all-to-all-done.10.arrived_ref = f32[16,8,128]{2,1,0:T(8,128)S(1)} async-done(((f32[16,8,128]{2,1,0:T(8,128)}), f32[16,8,128]{2,1,0:T(8,128)S(1)}, u32[]{:S(2)}, u32[]{:S(2)}) %all-to-all-start.10) | async-done | bytes 65568 | tf_op jit(solution)/shard_map/all_to_all | solution.py:295
  226.6 0.8 shard_map.150
  (15 shorter events, 0.3 us)
Async XLA Ops:
  7.2 92.1 %all-gather.5.cloned.1.call-start = ((), (), s32[]{:S(2)}) async-start(), calls=%async_computation.11 | async-start | bytes 10027008 | tf_op jit(solution)/shard_map/all_gather | solution.py:308
  26.3 162.0 %all-gather.7.cloned.1.call-start = ((), (), s32[]{:S(2)}) async-start(), calls=%async_computation.12 | async-start | bytes 2576384 | tf_op jit(solution)/shard_map/all_gather | solution.py:371
  99.3 34.6 %copy-start = (bf16[18432,256]{1,0:T(8,128)(2,1)S(1)}, bf16[18432,256]{1,0:T(8,128)(2,1)}, u32[]{:S(2)}) copy-start(bf16[18432,256]{1,0:T(8,128)(2,1)} %all-gather.5.cloned.1.call-done) | copy-start | bytes 28311556
  133.8 54.4 %copy-start.1 = (bf16[512,256]{1,0:T(8,128)(2,1)S(1)}, bf16[512,256]{1,0:T(8,128)(2,1)}, u32[]{:S(2)}) copy-start(bf16[512,256]{1,0:T(8,128)(2,1)} %down_ref.3) | copy-start | bytes 786436
  133.8 54.4 %copy-start.2 = (bf16[400,128]{1,0:T(8,128)(2,1)S(1)}, bf16[400,128]{1,0:T(8,128)(2,1)}, u32[]{:S(2)}) copy-start(bf16[400,128]{1,0:T(8,128)(2,1)} %first_ref.3) | copy-start | bytes 307204
  211.5 15.2 %all-to-all-start.10 = ((f32[16,8,128]{2,1,0:T(8,128)}), f32[16,8,128]{2,1,0:T(8,128)S(1)}, u32[]{:S(2)}, u32[]{:S(2)}) async-start(f32[16,8,128]{2,1,0:T(8,128)} %get-tuple-element.33), calls=%async_computation.10 | async-start | bytes 131072 | tf_op jit(solution)/shard_map/all_to_all | solution.py:295
Sparse Core Ops, SparseCore 0:
  26.4 72.4 all-gather.4
  141.7 37.4 all-gather.6

commit v6 on v5

--- a/solution.py
+++ b/solution.py
@@ -302,7 +302,8 @@
         pack_kernel,
         out_shape=struct((1152, 256), BF16),
         in_specs=[pl.BlockSpec(memory_space=pl.ANY)] * 3,
-        out_specs=pl.BlockSpec(memory_space=pl.ANY),
+        grid=(1,),
+        out_specs=full((1152, 256)),
         scratch_shapes=[pltpu.SemaphoreType.DMA((5,))],
     )(in_hbm(gate_w), in_hbm(up_w), in_hbm(proj_second))
     gathered = lax.all_gather(packed, OWNERS)
@@ -402,6 +403,7 @@
         scratch=[pltpu.VMEM((2, OWN, 128), BF16), pltpu.SemaphoreType.DMA],
         specs=[pl.BlockSpec(memory_space=pl.ANY)],
     )
+    message, first_grad, second_grad = lax.optimization_barrier((message, first_grad, second_grad))
     image_grad = call(
         norm_back_kernel, struct((1, VIS * SPLIT), F32), swap(message, OWNERS), hat, gains, scale
     )

time: 235 us -> 220 us (0.936)
  Pallas kernels: 39.7 us -> 23.4 us
  waiting for transfers between devices: 5.95 us -> 15.5 us
  blocking collectives: 166 us -> 161 us
  starting transfers between devices: 7.44 us -> 3.98 us
    pallas_call x1, Pallas kernels: 19 us -> 1.95 us  [on_device(): pl.pallas_call(pack_kernel, out_shape=struct((1152, 256), BF16), in_specs...]
    all_to_all x1, waiting for transfers between devices: 5.91 us -> 14.9 us  [swap(): return lax.all_to_all(blocks, axes, 0, 0, tiled=True)]
    all_to_all x10, blocking collectives: 166 us -> 161 us  [swap(): return lax.all_to_all(blocks, axes, 0, 0, tiled=True)]
    all_to_all x1, starting transfers between devices: 7.36 us -> 3.9 us  [swap(): return lax.all_to_all(blocks, axes, 0, 0, tiled=True)]
  transfers between devices with their start and end apart: 3 -> 3, of which waited for: 1 -> 2; matrix products, arithmetic and copies ran while one was open for 0% -> 0% of each run, Pallas kernels for 3% -> 3%
where the time goes in v6:
time: 220 us; the launch traced here: 219 us
  blocking collectives  161 us (73%)
  Pallas kernels  23.4 us (11%)
  waiting for transfers between devices  15.5 us (7%)
  between operations  14.1 us (6%)
  starting transfers between devices  3.98 us (2%)
    all_to_all x10, blocking collectives, swap(): return lax.all_to_all(blocks, axes, 0, 0, tiled=True)  161 us
    all_to_all x1, waiting for transfers between devices, swap(): return lax.all_to_all(blocks, axes, 0, 0, tiled=True)  14.9 us
    pallas_call x12, Pallas kernels, call(): pl.pallas_call(kernel, grid=(1,), out_shape=outs, in_specs=ins, out_specs...  13.7 us
    pallas_call x1, Pallas kernels, on_device(): pl.pallas_call(block_kernel, out_shape=(struct((RC, OWN, 128), BF16), str...  7.77 us
  transfers between devices with their start and end apart: 3, of which 2 were waited for; matrix products, arithmetic and copies ran while one was open for 0% of the time, Pallas kernels for 3%

profile of v6, /device:TPU:1, one launch (start us, length us, event | category | flops | bytes accessed | tf_op | source)
XLA Modules:
  0.0 218.9 jit_solution(11727143982445629833)
XLA Ops:
  7.2 1.9 shard_map.142
  9.2 0.8 reshape.14.gain_ref
  10.0 1.1 shard_map.138
  11.1 17.1 %all_to_all.55.arrived_ref = f32[16,8,128]{2,1,0:T(8,128)S(1)} all-to-all(f32[16,8,128]{2,1,0:T(8,128)S(1)} %get-tuple-element.25), channel_id=1, replica_groups=mesh['chip'=8,'core'=2,'row'=4,'col'=8] {'chip','core'}, dimensions={0} | all-to-all | bytes 131072 | tf_op jit(solution)/shard_map/all_to_all | solution.py:295
  28.2 0.7 shard_map.139
  29.0 28.5 %all_to_all.56.rows_ref = bf16[32,16,640]{2,1,0:T(8,128)(2,1)S(1)} all-to-all(bf16[32,16,640]{2,1,0:T(8,128)(2,1)S(1)} %shard_map.139), channel_id=1, replica_groups=mesh['chip'=8,'core'=2,'row'=4,'col'=8] {'row','col'}, dimensions={0} | all-to-all | bytes 1310720 | tf_op jit(solution)/shard_map/all_to_all | solution.py:295
  57.5 2.0 shard_map.140
  59.5 7.6 %all_to_all.57.arrived_ref = bf16[2,8,16,768]{3,2,1,0:T(8,128)(2,1)S(1)} all-to-all(bf16[2,8,16,768]{3,2,1,0:T(8,128)(2,1)S(1)} %get-tuple-element.27), channel_id=1, replica_groups=mesh['chip'=8,'core'=2,'row'=4,'col'=8] {'core'}, dimensions={0} | all-to-all | bytes 786432 | tf_op jit(solution)/shard_map/all_to_all | solution.py:295
  67.2 15.2 %all_to_all.58.arrived_ref.pieces_ref = bf16[8,16,768]{2,1,0:T(8,128)(2,1)S(1)} all-to-all(bf16[8,16,768]{2,1,0:T(8,128)(2,1)S(1)} %shard_map.141), channel_id=1, replica_groups=mesh['chip'=8,'core'=2,'row'=4,'col'=8] {'chip'}, dimensions={0} | all-to-all | bytes 393216 | tf_op jit(solution)/shard_map/all_to_all | solution.py:295
  82.9 1.6 shard_map.143
  84.6 19.6 %all_to_all.59.arrived_ref = bf16[32,16,128]{2,1,0:T(8,128)(2,1)S(1)} all-to-all(bf16[32,16,128]{2,1,0:T(8,128)(2,1)S(1)} %get-tuple-element.28), channel_id=1, replica_groups=mesh['chip'=8,'core'=2,'row'=4,'col'=8] {'row','col'}, dimensions={0} | all-to-all | bytes 262144 | tf_op jit(solution)/shard_map/all_to_all | solution.py:295
  104.2 13.4 %all_to_all.60.inputs_ref = bf16[32,16,128]{2,1,0:T(8,128)(2,1)S(1)} all-to-all(bf16[32,16,128]{2,1,0:T(8,128)(2,1)S(1)} %shard_map.144), channel_id=1, replica_groups=mesh['chip'=8,'core'=2,'row'=4,'col'=8] {'row','col'}, dimensions={0} | all-to-all | bytes 262144 | tf_op jit(solution)/shard_map/all_to_all | solution.py:295
  117.6 7.8 %shard_map.145 = (bf16[32,16,128]{2,1,0:T(8,128)(2,1)S(1)}, bf16[37,16,128]{2,1,0:T(8,128)(2,1)}) custom-call(bf16[32,16,128]{2,1,0:T(8,128)(2,1)S(1)} %all_to_all.60.inputs_ref, bf16[8,16,768]{2,1,0:T(8,128)(2,1)S(1)} %all_to_all.58.arrived_ref.pieces_ref, bf16[16,128]{1,0:T(8,128)(2,1)S(1)} %get-tuple-element.29.act_ref, bf16[16,1152,256]{2,1,0:T(8,128)(2,1)S(1)} %bitcast.5), custom_call_target="tpu_custom_call" | custom-call | tf_op jit(solution)/shard_map/pallas_call | solution.py:355
  125.4 12.7 %all_to_all.61.arrived_ref = bf16[32,16,128]{2,1,0:T(8,128)(2,1)S(1)} all-to-all(bf16[32,16,128]{2,1,0:T(8,128)(2,1)S(1)} %get-tuple-element.30), channel_id=1, replica_groups=mesh['chip'=8,'core'=2,'row'=4,'col'=8] {'row','col'}, dimensions={0} | all-to-all | bytes 262144 | tf_op jit(solution)/shard_map/all_to_all | solution.py:295
  138.2 12.7 %all_to_all.62.grad_ref = bf16[32,16,128]{2,1,0:T(8,128)(2,1)S(1)} all-to-all(bf16[32,16,128]{2,1,0:T(8,128)(2,1)S(1)} %shard_map.146), channel_id=1, replica_groups=mesh['chip'=8,'core'=2,'row'=4,'col'=8] {'row','col'}, dimensions={0} | all-to-all | bytes 262144 | tf_op jit(solution)/shard_map/all_to_all | solution.py:295
  150.9 1.6 shard_map.147
  152.5 19.5 %all_to_all.63.pieces_ref = bf16[16,16,384]{2,1,0:T(8,128)(2,1)S(1)} all-to-all(bf16[16,16,384]{2,1,0:T(8,128)(2,1)S(1)} %shard_map.147), channel_id=1, replica_groups=mesh['chip'=8,'core'=2,'row'=4,'col'=8] {'chip','core'}, dimensions={0} | all-to-all | bytes 393216 | tf_op jit(solution)/shard_map/all_to_all | solution.py:295
  172.0 2.4 %shard_map.148 = (bf16[32,16,640]{2,1,0:T(8,128)(2,1)}, bf16[512,128]{1,0:T(8,128)(2,1)S(1)}) custom-call(s32[8,512]{1,0:T(8,128)S(1)} %get-tuple-element.26.target_ref, bf16[16,16,384]{2,1,0:T(8,128)(2,1)S(1)} %all_to_all.63.pieces_ref, bf16[400,128]{1,0:T(8,128)(2,1)S(1)} %copy-done.2, bf16[512,256]{1,0:T(8,128)(2,1)S(1)} %copy-done.1, ...), custom_call_target="tpu_custom_call" | custom-call | tf_op jit(solution)/shard_map/pallas_call | solution.py:283
  174.4 3.9 %all-to-all-start.9 = ((bf16[32,16,640]{2,1,0:T(8,128)(2,1)}), bf16[32,16,640]{2,1,0:T(8,128)(2,1)S(1)}, u32[]{:S(2)}, u32[]{:S(2)}) async-start(bf16[32,16,640]{2,1,0:T(8,128)(2,1)} %get-tuple-element.34), calls=%async_computation.9 | async-start | bytes 1310720 | tf_op jit(solution)/shard_map/all_to_all | solution.py:295
  178.3 1.9 shard_map.150
  180.2 14.9 %all-to-all-done.9.arrived_ref = bf16[32,16,640]{2,1,0:T(8,128)(2,1)S(1)} async-done(((bf16[32,16,640]{2,1,0:T(8,128)(2,1)}), bf16[32,16,640]{2,1,0:T(8,128)(2,1)S(1)}, u32[]{:S(2)}, u32[]{:S(2)}) %all-to-all-start.9) | async-done | bytes 655392 | tf_op jit(solution)/shard_map/all_to_all | solution.py:295
  195.1 1.3 shard_map.149
  196.4 14.7 %all_to_all.64.arrived_ref = f32[16,8,128]{2,1,0:T(8,128)S(1)} all-to-all(f32[16,8,128]{2,1,0:T(8,128)S(1)} %get-tuple-element.40), channel_id=1, replica_groups=mesh['chip'=8,'core'=2,'row'=4,'col'=8] {'chip','core'}, dimensions={0} | all-to-all | bytes 131072 | tf_op jit(solution)/shard_map/all_to_all | solution.py:295
  211.2 0.9 shard_map.151
  (15 shorter events, 0.8 us)
Async XLA Ops:
  7.2 75.8 %all-gather.5.cloned.1.call-start = ((), (), s32[]{:S(2)}) async-start(), calls=%async_computation.11 | async-start | bytes 10027008 | tf_op jit(solution)/shard_map/all_gather | solution.py:309
  9.2 162.8 %all-gather.7.cloned.1.call-start = ((), (), s32[]{:S(2)}) async-start(), calls=%async_computation.12 | async-start | bytes 2576384 | tf_op jit(solution)/shard_map/all_gather | solution.py:372
  82.9 34.6 %copy-start = (bf16[18432,256]{1,0:T(8,128)(2,1)S(1)}, bf16[18432,256]{1,0:T(8,128)(2,1)}, u32[]{:S(2)}) copy-start(bf16[18432,256]{1,0:T(8,128)(2,1)} %all-gather.5.cloned.1.call-done) | copy-start | bytes 28311556
  117.6 54.4 %copy-start.1 = (bf16[512,256]{1,0:T(8,128)(2,1)S(1)}, bf16[512,256]{1,0:T(8,128)(2,1)}, u32[]{:S(2)}) copy-start(bf16[512,256]{1,0:T(8,128)(2,1)} %down_ref.3) | copy-start | bytes 786436
  117.6 54.4 %copy-start.2 = (bf16[400,128]{1,0:T(8,128)(2,1)S(1)}, bf16[400,128]{1,0:T(8,128)(2,1)}, u32[]{:S(2)}) copy-start(bf16[400,128]{1,0:T(8,128)(2,1)} %first_ref.3) | copy-start | bytes 307204
  174.4 20.7 %all-to-all-start.9 = ((bf16[32,16,640]{2,1,0:T(8,128)(2,1)}), bf16[32,16,640]{2,1,0:T(8,128)(2,1)S(1)}, u32[]{:S(2)}, u32[]{:S(2)}) async-start(bf16[32,16,640]{2,1,0:T(8,128)(2,1)} %get-tuple-element.34), calls=%async_computation.9 | async-start | bytes 1310720 | tf_op jit(solution)/shard_map/all_to_all | solution.py:295
Sparse Core Ops, SparseCore 0:
  10.1 72.7 all-gather.4
  125.5 37.4 all-gather.6

commit v7 on v6

--- a/solution.py
+++ b/solution.py
@@ -96,8 +96,21 @@
 
 
 def first_kernel(
-    counts_ref, order_ref, rows_ref, first_ref, second_ref, down_ref, out_ref, target_ref, weight, starts
+    counts_ref,
+    order_ref,
+    rows_ref,
+    first_ref,
+    second_ref,
+    down_ref,
+    bias_ref,
+    out_ref,
+    target_ref,
+    bias_out,
+    weight,
+    starts,
 ):
+    bias_out[...] = bias_ref[...]
+
     def body(j, total):
         block = order_ref[j]
         starts[block] = total
@@ -131,7 +144,11 @@
     out_ref[...] = (arrived_ref[0].astype(F32) + arrived_ref[1].astype(F32)).astype(BF16)
 
 
-def second_kernel(arrived_ref, bias_ref, weight_ref, out_ref, hidden_ref, slope_ref, back_ref):
+def second_kernel(
+    arrived_ref, bias_ref, weights_ref, out_ref, hidden_ref, slope_ref, back_ref, second_ref, sem
+):
+    copy = pltpu.make_async_copy(weights_ref.at[:, pl.ds(1024, 128), :], second_ref, sem)
+    copy.start()
     both = jnp.zeros((OWN, 256), F32)
     for v in range(CHIPS):
         both = both + arrived_ref[v, :, 512:768].astype(F32)
@@ -142,8 +159,9 @@
     hidden = (pre * cdf).astype(BF16)
     hidden_ref[...] = hidden
     slope_ref[...] = cdf + pre * density
-    for v in range(VIS):
-        y = dot(hidden, weight_ref[v]).astype(BF16)
+    copy.wait()
+    for v in range(VIS):
+        y = dot(hidden, second_ref[v]).astype(BF16)
         out_ref[2 * v] = y[:, 0:128]
         out_ref[2 * v + 1] = y[:, 128:256]
 
@@ -157,48 +175,33 @@
         out_ref[r] = own
 
 
-def block_kernel(inputs_ref, pieces_ref, act_ref, w_ref, out_ref, bundle_ref, gate, up, gate_b, up_b):
-    phase = pl.program_id(0)
-    v = pl.program_id(1)
-
-    @pl.when(jnp.logical_and(phase == 0, v == 0))
-    def _():
-        gate[...] = jnp.zeros_like(gate)
-        up[...] = jnp.zeros_like(up)
-        bundle_ref[36] = act_ref[...]
-
-    @pl.when(phase == 0)
-    def _():
-        bundle_ref[2 * v] = inputs_ref[0]
-        bundle_ref[2 * v + 1] = inputs_ref[1]
-        x = jnp.concatenate([inputs_ref[0], inputs_ref[1]], axis=1)
-        gate[:, 0:256] += dot(x, w_ref[0, 0:256, :])
-        gate[:, 256:512] += dot(x, w_ref[0, 256:512, :])
-        up[:, 0:256] += dot(x, w_ref[0, 512:768, :])
-        up[:, 256:512] += dot(x, w_ref[0, 768:1024, :])
-
-    @pl.when(jnp.logical_and(phase == 1, v == 0))
-    def _():
-        h = jnp.zeros((OWN, 512), F32)
-        for i in range(CHIPS):
-            h = h + pieces_ref[i].astype(F32)
-        g, u = gate[...], up[...]
-        s = jax.nn.sigmoid(g)
-        hidden = (g * s * u).astype(BF16)
+def block_kernel(inputs_ref, pieces_ref, act_ref, w_ref, out_ref, bundle_ref):
+    bundle_ref[0:RC] = inputs_ref[...]
+    bundle_ref[36] = act_ref[...]
+    sums = [jnp.zeros((OWN, 256), F32) for _ in range(4)]
+    for v in range(VIS):
+        x = jnp.concatenate([inputs_ref[2 * v], inputs_ref[2 * v + 1]], axis=1)
         for k in range(4):
-            bundle_ref[32 + k] = hidden[:, 128 * k : 128 * k + 128]
-        gate_b[...] = (h * u * s * (1.0 + g * (1.0 - s))).astype(BF16)
-        up_b[...] = (h * g * s).astype(BF16)
-
-    @pl.when(phase == 1)
-    def _():
-        y = dot(gate_b[:, 0:256], w_ref[0, 0:256, :], 1, 1)
-        y += dot(gate_b[:, 256:512], w_ref[0, 256:512, :], 1, 1)
-        y += dot(up_b[:, 0:256], w_ref[0, 512:768, :], 1, 1)
-        y += dot(up_b[:, 256:512], w_ref[0, 768:1024, :], 1, 1)
+            sums[k] = sums[k] + dot(x, w_ref[v, 256 * k : 256 * k + 256, :])
+    h = jnp.zeros((OWN, 512), F32)
+    for i in range(CHIPS):
+        h = h + pieces_ref[i, :, 0:512].astype(F32)
+    g = jnp.concatenate(sums[0:2], axis=1)
+    u = jnp.concatenate(sums[2:4], axis=1)
+    s = jax.nn.sigmoid(g)
+    hidden = (g * s * u).astype(BF16)
+    for k in range(4):
+        bundle_ref[RC + k] = hidden[:, 128 * k : 128 * k + 128]
+    gate_grad = (h * u * s * (1.0 + g * (1.0 - s))).astype(BF16)
+    up_grad = (h * g * s).astype(BF16)
+    grads = [gate_grad[:, 0:256], gate_grad[:, 256:512], up_grad[:, 0:256], up_grad[:, 256:512]]
+    for v in range(VIS):
+        y = dot(grads[0], w_ref[v, 0:256, :], 1, 1)
+        for k in range(1, 4):
+            y = y + dot(grads[k], w_ref[v, 256 * k : 256 * k + 256, :], 1, 1)
         y = y.astype(BF16)
-        out_ref[0] = y[:, 0:128]
-        out_ref[1] = y[:, 128:256]
+        out_ref[2 * v] = y[:, 0:128]
+        out_ref[2 * v + 1] = y[:, 128:256]
 
 
 def back_kernel(grad_ref, slope_ref, back_ref, second_ref, out_ref):
@@ -212,13 +215,18 @@
         out_ref[v, :, 256:384] = act
 
 
-def slot_kernel(target_ref, pieces_ref, first_ref, down_ref, hidden_ref, out_ref, act_ref, weight):
+def slot_kernel(
+    target_ref, pieces_ref, first_ref, down_ref, bundles_ref, out_ref, act_ref, weight, hidden_ref, sem
+):
+    copy = pltpu.make_async_copy(bundles_ref.at[:, pl.ds(RC, 4)], hidden_ref, sem)
+    copy.start()
     weight[SPLIT:LANES, :] = jnp.zeros((LANES - SPLIT, 128), BF16)
     weight[0:SPLIT, :] = first_ref[...]
     act = pieces_ref[:, :, 256:384].reshape(ROWS, 128)
     act = dot(selection(target_ref), act, 0, 0).astype(BF16)
     act_ref[...] = act
     out_ref[:, :, 0:LANES] = dot(act, weight[...], 1, 1).astype(BF16).reshape(RC, VIS, LANES)
+    copy.wait()
     hidden = jnp.concatenate([hidden_ref[:, k].reshape(ROWS, 128) for k in range(4)], axis=1)
     block = dot(hidden, down_ref[...])
     block = jnp.concatenate(
@@ -291,6 +299,18 @@
     )(*args)
 
 
+def local(kernel, outs, *args, scratch=(), remote=0):
+    ins = [pl.BlockSpec(memory_space=pltpu.VMEM)] * (len(args) - remote)
+    return pl.pallas_call(
+        kernel,
+        out_shape=outs,
+        in_specs=ins + [pl.BlockSpec(memory_space=pl.ANY)] * remote,
+        out_specs=jax.tree.map(lambda _: pl.BlockSpec(memory_space=pltpu.VMEM), outs),
+        scratch_shapes=list(scratch),
+        compiler_params=params(),
+    )(*args)
+
+
 def swap(blocks, axes):
     return lax.all_to_all(blocks, axes, 0, 0, tiled=True)
 
@@ -308,7 +328,6 @@
     )(in_hbm(gate_w), in_hbm(up_w), in_hbm(proj_second))
     gathered = lax.all_gather(packed, OWNERS)
     weights = in_hbm(gathered)
-    seconds = pl.BlockSpec((VIS, 128, 256), lambda i: (0, 8, 0))
     message, hat, gains, scale = call(
         norm_kernel,
         (
@@ -324,57 +343,55 @@
     arrived = swap(message, OWNERS)
     spread = call(spread_kernel, struct((RC, VIS, 640), BF16), arrived, in_hbm(cotangent))
     rows = swap(spread, GROUP)
-    partial, target = call(
+    partial, target, bias = call(
         first_kernel,
-        (struct((PAIR, CHIPS, OWN, 768), BF16), struct((8, RC * VIS), jnp.int32)),
+        (
+            struct((PAIR, CHIPS, OWN, 768), BF16),
+            struct((8, RC * VIS), jnp.int32),
+            struct((1, 128), F32),
+        ),
         in_hbm(counts),
         in_hbm(block_order),
         rows,
         in_hbm(proj_first),
         in_hbm(proj_second),
         in_hbm(down_w),
+        in_hbm(bias.reshape(1, -1)),
         scratch=[pltpu.VMEM((LANES, 128), BF16), pltpu.SMEM((VIS,), jnp.int32)],
     )
-    pairs = call(pair_kernel, struct((CHIPS, OWN, 768), BF16), swap(partial, "core"))
+    pairs = local(pair_kernel, struct((CHIPS, OWN, 768), BF16), swap(partial, "core"))
     pieces = swap(pairs, "chip")
-    input_part, hidden_proj, slope, back = call(
+    input_part, hidden_proj, slope, back, seconds = local(
         second_kernel,
         (
             struct((RC, OWN, 128), BF16),
             struct((OWN, 128), BF16),
             struct((OWN, 128), F32),
             struct((OWN, 128), F32),
+            struct((VIS, 128, 256), BF16),
         ),
         pieces,
-        in_hbm(bias.reshape(1, -1)),
+        bias,
         weights,
-        specs=[seconds],
-    )
-    spread = call(sum_kernel, struct((RC, OWN, 128), BF16), swap(input_part, GROUP))
+        scratch=[pltpu.SemaphoreType.DMA],
+        remote=1,
+    )
+    spread = local(sum_kernel, struct((RC, OWN, 128), BF16), swap(input_part, GROUP))
     inputs = swap(spread, GROUP)
-    block_part, bundle = pl.pallas_call(
+    block_part, bundle = local(
         block_kernel,
-        out_shape=(struct((RC, OWN, 128), BF16), struct((37, OWN, 128), BF16)),
-        grid=(2, VIS),
-        in_specs=[
-            pl.BlockSpec((2, OWN, 128), lambda p, v: ((1 - p) * v, 0, 0)),
-            pl.BlockSpec((CHIPS, OWN, 512), lambda p, v: (0, 0, 0)),
-            pl.BlockSpec((OWN, 128), lambda p, v: (0, 0)),
-            pl.BlockSpec((1, 1024, 256), lambda p, v: (v, 0, 0)),
-        ],
-        out_specs=(
-            pl.BlockSpec((2, OWN, 128), lambda p, v: (p * v, 0, 0)),
-            pl.BlockSpec((37, OWN, 128), lambda p, v: (0, 0, 0)),
-        ),
-        scratch_shapes=[pltpu.VMEM((OWN, 512), F32)] * 2 + [pltpu.VMEM((OWN, 512), BF16)] * 2,
-        compiler_params=params(),
-    )(inputs, pieces, hidden_proj, gathered)
+        (struct((RC, OWN, 128), BF16), struct((37, OWN, 128), BF16)),
+        inputs,
+        pieces,
+        hidden_proj,
+        gathered,
+    )
     bundles = in_hbm(lax.all_gather(bundle, OWNERS))
-    spread = call(sum_kernel, struct((RC, OWN, 128), BF16), swap(block_part, GROUP))
+    spread = local(sum_kernel, struct((RC, OWN, 128), BF16), swap(block_part, GROUP))
     whole = swap(spread, GROUP)
-    sent = call(back_kernel, struct((VIS, OWN, 384), BF16), whole, slope, back, weights, specs=[seconds])
+    sent = local(back_kernel, struct((VIS, OWN, 384), BF16), whole, slope, back, seconds)
     blocks = swap(sent, OWNERS)
-    slot_part, acts = call(
+    slot_part, acts = local(
         slot_kernel,
         (struct((RC, VIS, 640), BF16), struct((RC * VIS, 128), BF16)),
         target,
@@ -382,8 +399,12 @@
         proj_first,
         down_w,
         bundles,
-        scratch=[pltpu.VMEM((LANES, 128), BF16)],
-        specs=[pl.BlockSpec((VIS, 4, OWN, 128), lambda i: (0, 8, 0, 0))],
+        scratch=[
+            pltpu.VMEM((LANES, 128), BF16),
+            pltpu.VMEM((VIS, 4, OWN, 128), BF16),
+            pltpu.SemaphoreType.DMA,
+        ],
+        remote=1,
     )
     slots = swap(slot_part, GROUP)
     first_grad, second_grad = call(
@@ -395,16 +416,16 @@
         bundles,
         specs=[pl.BlockSpec((VIS, 1, OWN, 128), lambda i: (0, 36, 0, 0))],
     )
-    message, block_out = call(
+    message, block_out = local(
         slot_sum_kernel,
         (struct((VIS, 8, 128), F32), struct((8, 256), BF16)),
         slots,
         bundles,
         scratch=[pltpu.VMEM((2, OWN, 128), BF16), pltpu.SemaphoreType.DMA],
-        specs=[pl.BlockSpec(memory_space=pl.ANY)],
+        remote=1,
     )
     message, first_grad, second_grad = lax.optimization_barrier((message, first_grad, second_grad))
-    image_grad = call(
+    image_grad = local(
         norm_back_kernel, struct((1, VIS * SPLIT), F32), swap(message, OWNERS), hat, gains, scale
     )
     return block_out, image_grad, first_grad, second_grad

time: 220 us -> 216 us (0.982)
  Pallas kernels: 23.4 us -> 18.4 us
    pallas_call x12 -> x4, Pallas kernels: 13.7 us -> 5.75 us  [call(): pl.pallas_call(kernel, grid=(1,), out_shape=outs, in_specs=ins, out_specs...]
    pallas_call x1 -> x9, Pallas kernels: 7.77 us -> 10.7 us  [local(): pl.pallas_call(kernel, out_shape=outs, in_specs=ins + [pl.BlockSpec(memor...]
where the time goes in v7:
time: 216 us; the launch traced here: 215 us
  blocking collectives  163 us (75%)
  Pallas kernels  18.4 us (9%)
  waiting for transfers between devices  15.5 us (7%)
  between operations  14.1 us (7%)
  starting transfers between devices  3.99 us (2%)
    all_to_all x10, blocking collectives, swap(): return lax.all_to_all(blocks, axes, 0, 0, tiled=True)  163 us
    all_to_all x1, waiting for transfers between devices, swap(): return lax.all_to_all(blocks, axes, 0, 0, tiled=True)  14.9 us
    pallas_call x9, Pallas kernels, local(): pl.pallas_call(kernel, out_shape=outs, in_specs=ins + [pl.BlockSpec(memor...  10.7 us
    pallas_call x4, Pallas kernels, call(): pl.pallas_call(kernel, grid=(1,), out_shape=outs, in_specs=ins, out_specs...  5.75 us
  transfers between devices with their start and end apart: 3, of which 2 were waited for; matrix products, arithmetic and copies ran while one was open for 0% of the time, Pallas kernels for 3%

profile of v7, /device:TPU:1, one launch (start us, length us, event | category | flops | bytes accessed | tf_op | source)
XLA Modules:
  0.0 215.3 jit_solution(10410734983237069016)
XLA Ops:
  7.2 1.9 shard_map.142
  9.2 0.8 reshape.14.gain_ref
  10.0 1.1 shard_map.138
  11.1 17.1 %all_to_all.55.arrived_ref = f32[16,8,128]{2,1,0:T(8,128)S(1)} all-to-all(f32[16,8,128]{2,1,0:T(8,128)S(1)} %get-tuple-element.27), channel_id=1, replica_groups=mesh['chip'=8,'core'=2,'row'=4,'col'=8] {'chip','core'}, dimensions={0} | all-to-all | bytes 131072 | tf_op jit(solution)/shard_map/all_to_all | solution.py:315
  28.2 0.7 shard_map.139
  29.0 28.5 %all_to_all.56.rows_ref = bf16[32,16,640]{2,1,0:T(8,128)(2,1)S(1)} all-to-all(bf16[32,16,640]{2,1,0:T(8,128)(2,1)S(1)} %shard_map.139), channel_id=1, replica_groups=mesh['chip'=8,'core'=2,'row'=4,'col'=8] {'row','col'}, dimensions={0} | all-to-all | bytes 1310720 | tf_op jit(solution)/shard_map/all_to_all | solution.py:315
  57.5 2.0 shard_map.140
  59.6 7.6 %all_to_all.57.arrived_ref = bf16[2,8,16,768]{3,2,1,0:T(8,128)(2,1)S(1)} all-to-all(bf16[2,8,16,768]{3,2,1,0:T(8,128)(2,1)S(1)} %get-tuple-element.29), channel_id=1, replica_groups=mesh['chip'=8,'core'=2,'row'=4,'col'=8] {'core'}, dimensions={0} | all-to-all | bytes 786432 | tf_op jit(solution)/shard_map/all_to_all | solution.py:315
  67.2 15.2 %all_to_all.58.arrived_ref.pieces_ref = bf16[8,16,768]{2,1,0:T(8,128)(2,1)S(1)} all-to-all(bf16[8,16,768]{2,1,0:T(8,128)(2,1)S(1)} %shard_map.141), channel_id=1, replica_groups=mesh['chip'=8,'core'=2,'row'=4,'col'=8] {'chip'}, dimensions={0} | all-to-all | bytes 393216 | tf_op jit(solution)/shard_map/all_to_all | solution.py:315
  82.4 0.6 all-gather.5.cloned.1.call-done
  82.9 1.6 shard_map.143
  84.6 19.6 %all_to_all.59.arrived_ref = bf16[32,16,128]{2,1,0:T(8,128)(2,1)S(1)} all-to-all(bf16[32,16,128]{2,1,0:T(8,128)(2,1)S(1)} %get-tuple-element.31), channel_id=1, replica_groups=mesh['chip'=8,'core'=2,'row'=4,'col'=8] {'row','col'}, dimensions={0} | all-to-all | bytes 262144 | tf_op jit(solution)/shard_map/all_to_all | solution.py:315
  104.2 13.4 %all_to_all.60.inputs_ref = bf16[32,16,128]{2,1,0:T(8,128)(2,1)S(1)} all-to-all(bf16[32,16,128]{2,1,0:T(8,128)(2,1)S(1)} %shard_map.144), channel_id=1, replica_groups=mesh['chip'=8,'core'=2,'row'=4,'col'=8] {'row','col'}, dimensions={0} | all-to-all | bytes 262144 | tf_op jit(solution)/shard_map/all_to_all | solution.py:315
  117.6 4.0 %shard_map.145 = (bf16[32,16,128]{2,1,0:T(8,128)(2,1)S(1)}, bf16[37,16,128]{2,1,0:T(8,128)(2,1)}) custom-call(bf16[32,16,128]{2,1,0:T(8,128)(2,1)S(1)} %all_to_all.60.inputs_ref, bf16[8,16,768]{2,1,0:T(8,128)(2,1)S(1)} %all_to_all.58.arrived_ref.pieces_ref, bf16[16,128]{1,0:T(8,128)(2,1)S(1)} %get-tuple-element.32.act_ref, bf16[16,1152,256]{2,1,0:T(8,128)(2,1)S(1)} %bitcast.4), custom_call_target="tpu_custom_call" | custom-call | tf_op jit(solution)/shard_map/pallas_call | solution.py:304
  121.6 12.7 %all_to_all.61.arrived_ref = bf16[32,16,128]{2,1,0:T(8,128)(2,1)S(1)} all-to-all(bf16[32,16,128]{2,1,0:T(8,128)(2,1)S(1)} %get-tuple-element.33), channel_id=1, replica_groups=mesh['chip'=8,'core'=2,'row'=4,'col'=8] {'row','col'}, dimensions={0} | all-to-all | bytes 262144 | tf_op jit(solution)/shard_map/all_to_all | solution.py:315
  134.3 12.7 %all_to_all.62.grad_ref = bf16[32,16,128]{2,1,0:T(8,128)(2,1)S(1)} all-to-all(bf16[32,16,128]{2,1,0:T(8,128)(2,1)S(1)} %shard_map.146), channel_id=1, replica_groups=mesh['chip'=8,'core'=2,'row'=4,'col'=8] {'row','col'}, dimensions={0} | all-to-all | bytes 262144 | tf_op jit(solution)/shard_map/all_to_all | solution.py:315
  147.4 19.5 %all_to_all.63.pieces_ref = bf16[16,16,384]{2,1,0:T(8,128)(2,1)S(1)} all-to-all(bf16[16,16,384]{2,1,0:T(8,128)(2,1)S(1)} %shard_map.147), channel_id=1, replica_groups=mesh['chip'=8,'core'=2,'row'=4,'col'=8] {'chip','core'}, dimensions={0} | all-to-all | bytes 393216 | tf_op jit(solution)/shard_map/all_to_all | solution.py:315
  166.9 2.4 %shard_map.148 = (bf16[32,16,640]{2,1,0:T(8,128)(2,1)}, bf16[512,128]{1,0:T(8,128)(2,1)S(1)}) custom-call(s32[8,512]{1,0:T(8,128)S(1)} %get-tuple-element.28.target_ref, bf16[16,16,384]{2,1,0:T(8,128)(2,1)S(1)} %all_to_all.63.pieces_ref, bf16[400,128]{1,0:T(8,128)(2,1)S(1)} %copy-done.2, bf16[512,256]{1,0:T(8,128)(2,1)S(1)} %copy-done.1, ...), custom_call_target="tpu_custom_call" | custom-call | tf_op jit(solution)/shard_map/pallas_call | solution.py:304
  169.4 3.9 %all-to-all-start.9 = ((bf16[32,16,640]{2,1,0:T(8,128)(2,1)}), bf16[32,16,640]{2,1,0:T(8,128)(2,1)S(1)}, u32[]{:S(2)}, u32[]{:S(2)}) async-start(bf16[32,16,640]{2,1,0:T(8,128)(2,1)} %get-tuple-element.38), calls=%async_computation.9 | async-start | bytes 1310720 | tf_op jit(solution)/shard_map/all_to_all | solution.py:315
  173.3 1.9 shard_map.150
  175.2 14.9 %all-to-all-done.9.arrived_ref = bf16[32,16,640]{2,1,0:T(8,128)(2,1)S(1)} async-done(((bf16[32,16,640]{2,1,0:T(8,128)(2,1)}), bf16[32,16,640]{2,1,0:T(8,128)(2,1)S(1)}, u32[]{:S(2)}, u32[]{:S(2)}) %all-to-all-start.9) | async-done | bytes 655392 | tf_op jit(solution)/shard_map/all_to_all | solution.py:315
  190.0 1.3 shard_map.149
  191.4 16.2 %all_to_all.64.arrived_ref = f32[16,8,128]{2,1,0:T(8,128)S(1)} all-to-all(f32[16,8,128]{2,1,0:T(8,128)S(1)} %get-tuple-element.44), channel_id=1, replica_groups=mesh['chip'=8,'core'=2,'row'=4,'col'=8] {'chip','core'}, dimensions={0} | all-to-all | bytes 131072 | tf_op jit(solution)/shard_map/all_to_all | solution.py:315
  207.6 0.8 shard_map.151
  (15 shorter events, 0.7 us)
Async XLA Ops:
  7.2 75.8 %all-gather.5.cloned.1.call-start = ((), (), s32[]{:S(2)}) async-start(), calls=%async_computation.11 | async-start | bytes 10027008 | tf_op jit(solution)/shard_map/all_gather | solution.py:329
  9.2 157.8 %all-gather.7.cloned.1.call-start = ((), (), s32[]{:S(2)}) async-start(), calls=%async_computation.12 | async-start | bytes 2576384 | tf_op jit(solution)/shard_map/all_gather | solution.py:389
  82.9 34.6 %copy-start = (bf16[18432,256]{1,0:T(8,128)(2,1)S(1)}, bf16[18432,256]{1,0:T(8,128)(2,1)}, u32[]{:S(2)}) copy-start(bf16[18432,256]{1,0:T(8,128)(2,1)} %all-gather.5.cloned.1.call-done) | copy-start | bytes 28311556
  82.9 84.0 %copy-start.1 = (bf16[512,256]{1,0:T(8,128)(2,1)S(1)}, bf16[512,256]{1,0:T(8,128)(2,1)}, u32[]{:S(2)}) copy-start(bf16[512,256]{1,0:T(8,128)(2,1)} %down_ref.3) | copy-start | bytes 786436
  82.9 84.0 %copy-start.2 = (bf16[400,128]{1,0:T(8,128)(2,1)S(1)}, bf16[400,128]{1,0:T(8,128)(2,1)}, u32[]{:S(2)}) copy-start(bf16[400,128]{1,0:T(8,128)(2,1)} %first_ref.3) | copy-start | bytes 307204
  169.4 20.7 %all-to-all-start.9 = ((bf16[32,16,640]{2,1,0:T(8,128)(2,1)}), bf16[32,16,640]{2,1,0:T(8,128)(2,1)S(1)}, u32[]{:S(2)}, u32[]{:S(2)}) async-start(bf16[32,16,640]{2,1,0:T(8,128)(2,1)} %get-tuple-element.38), calls=%async_computation.9 | async-start | bytes 1310720 | tf_op jit(solution)/shard_map/all_to_all | solution.py:315
Sparse Core Ops, SparseCore 0:
  10.1 72.7 all-gather.4
  121.7 37.4 all-gather.6

commit v8 on v7

--- a/solution.py
+++ b/solution.py
@@ -16,6 +16,8 @@
 BF16 = jnp.bfloat16
 PAIR = 2
 CHIPS = VIS // PAIR
+FIRST = 37
+BUNDLE = 62
 GROUP = ("row", "col")
 OWNERS = ("chip", "core")
 
@@ -30,6 +32,10 @@
 
 def dot(a, b, ca=1, cb=0):
     return lax.dot_general(a, b, (((ca,), (cb,)), ((), ())), preferred_element_type=F32)
+
+
+def owner_index():
+    return lax.axis_index("chip") * PAIR + lax.axis_index("core")
 
 
 def group_index():
@@ -106,6 +112,7 @@
     out_ref,
     target_ref,
     bias_out,
+    mine_ref,
     weight,
     starts,
 ):
@@ -117,6 +124,9 @@
         return total + counts_ref[block]
 
     lax.fori_loop(0, VIS, body, jnp.int32(0))
+    me = owner_index()
+    mine_ref[0] = jnp.full((8, 128), starts[me], jnp.int32)
+    mine_ref[1] = jnp.full((8, 128), counts_ref[me], jnp.int32)
     lane = lax.broadcasted_iota(jnp.int32, (8, RC * VIS), 1)
     owner = lane % VIS
     slot = lane // VIS
@@ -175,7 +185,8 @@
         out_ref[r] = own
 
 
-def block_kernel(inputs_ref, pieces_ref, act_ref, w_ref, out_ref, bundle_ref):
+def block_kernel(inputs_ref, pieces_ref, act_ref, first_ref, w_ref, out_ref, bundle_ref):
+    bundle_ref[FIRST : FIRST + 25] = first_ref[...].reshape(25, OWN, 128)
     bundle_ref[0:RC] = inputs_ref[...]
     bundle_ref[36] = act_ref[...]
     sums = [jnp.zeros((OWN, 256), F32) for _ in range(4)]
@@ -216,17 +227,29 @@
 
 
 def slot_kernel(
-    target_ref, pieces_ref, first_ref, down_ref, bundles_ref, out_ref, act_ref, weight, hidden_ref, sem
+    mine_ref, pieces_ref, down_ref, bundles_ref, out_ref, first_ref, hidden_ref, spread, sems
 ):
-    copy = pltpu.make_async_copy(bundles_ref.at[:, pl.ds(RC, 4)], hidden_ref, sem)
-    copy.start()
-    weight[SPLIT:LANES, :] = jnp.zeros((LANES - SPLIT, 128), BF16)
-    weight[0:SPLIT, :] = first_ref[...]
-    act = pieces_ref[:, :, 256:384].reshape(ROWS, 128)
-    act = dot(selection(target_ref), act, 0, 0).astype(BF16)
-    act_ref[...] = act
-    out_ref[:, :, 0:LANES] = dot(act, weight[...], 1, 1).astype(BF16).reshape(RC, VIS, LANES)
-    copy.wait()
+    copy_first = pltpu.make_async_copy(
+        bundles_ref.at[:, pl.ds(FIRST, 25)], first_ref.at[:, pl.ds(0, 25)], sems.at[0]
+    )
+    copy_hidden = pltpu.make_async_copy(bundles_ref.at[:, pl.ds(RC, 4)], hidden_ref, sems.at[1])
+    copy_first.start()
+    copy_hidden.start()
+    first_ref[:, 25:32] = jnp.zeros((VIS, 7, OWN, 128), BF16)
+    language = lax.broadcasted_iota(jnp.int32, (RC, ROWS), 1)
+    slot = lax.broadcasted_iota(jnp.int32, (RC, ROWS), 0)
+    hit = jnp.logical_and(slot < mine_ref[1, 0:1, 0:1], language == slot + mine_ref[0, 0:1, 0:1])
+    act = dot(
+        jnp.where(hit, 1.0, 0.0).astype(BF16), pieces_ref[:, :, 256:384].reshape(ROWS, 128)
+    ).astype(BF16)
+    copy_first.wait()
+    for v in range(VIS):
+        y = dot(act, first_ref[v].reshape(LANES, 128), 1, 1)
+        for k in range(4):
+            spread[k, pl.ds(v, RC, stride=VIS), :] = y[:, 128 * k : 128 * k + 128]
+    for k in range(4):
+        out_ref[:, :, 128 * k : 128 * k + 128] = spread[k].astype(BF16).reshape(RC, VIS, 128)
+    copy_hidden.wait()
     hidden = jnp.concatenate([hidden_ref[:, k].reshape(ROWS, 128) for k in range(4)], axis=1)
     block = dot(hidden, down_ref[...])
     block = jnp.concatenate(
@@ -235,41 +258,42 @@
     out_ref[:, :, LANES : LANES + 128] = block.astype(BF16)
 
 
-def weight_grad_kernel(pieces_ref, act_ref, rows_ref, hidden_ref, first_ref, second_ref):
-    hidden = hidden_ref[:, 0].reshape(ROWS, 128)
+def weight_grad_kernel(
+    target_ref, pieces_ref, rows_ref, bundles_ref, first_ref, second_ref, own_ref, hidden_ref, inputs, sems
+):
+    r = group_index()
+    copy_hidden = pltpu.make_async_copy(bundles_ref.at[:, 36], hidden_ref, sems.at[0])
+    copy_inputs = pltpu.make_async_copy(
+        bundles_ref.at[r // 2, pl.ds(2 * owner_index(), 2)], inputs, sems.at[1]
+    )
+    copy_hidden.start()
+    copy_inputs.start()
+    act = pieces_ref[:, :, 256:384].reshape(ROWS, 128)
+    act = dot(selection(target_ref), act, 0, 0).astype(BF16)
+    rows = rows_ref[:, :, 0:LANES].reshape(RC * VIS, LANES)
+    first_ref[...] = dot(rows, act, 0, 0)[0:SPLIT, :]
     ig = pieces_ref[:, :, 0:256].reshape(ROWS, 256).astype(F32) + language_cotangent(rows_ref)
-    second_ref[...] = dot(hidden, ig.astype(BF16), 0, 0)
-    rows = rows_ref[:, :, 0:LANES].reshape(RC * VIS, LANES)
-    first_ref[...] = dot(rows, act_ref[...], 0, 0)[0:SPLIT, :]
-
-
-def slot_sum_kernel(arrived_ref, bundles_ref, message_ref, out_ref, inputs, sem):
-    r = group_index()
-    v = lax.axis_index("chip") * PAIR + lax.axis_index("core")
-    copy = pltpu.make_async_copy(bundles_ref.at[r // 2, pl.ds(2 * v, 2)], inputs, sem)
-    copy.start()
+    copy_hidden.wait()
+    second_ref[...] = dot(hidden_ref[...].reshape(ROWS, 128), ig.astype(BF16), 0, 0)
+    copy_inputs.wait()
+    piece = jnp.concatenate([inputs[0].astype(F32), inputs[1].astype(F32)], axis=1)
+    own_ref[...] = jnp.where(r % 2 == 0, piece[0:8], piece[8:16])
+
+
+def last_kernel(arrived_ref, own_ref, hat_ref, gain_ref, scale_ref, image_ref, out_ref):
     total = jnp.zeros((VIS, LANES + 128), F32)
     for i in range(RC):
         total = total + arrived_ref[i].astype(F32)
-    message_ref[...] = jnp.zeros_like(message_ref)
-    for j in range(4):
-        message_ref[:, j, :] = total[:, 128 * j : 128 * j + 128]
     part = total[:, LANES : LANES + 128]
     part = jnp.concatenate([part[0:8], part[8:16]], axis=1)
-    copy.wait()
-    piece = jnp.concatenate([inputs[0].astype(F32), inputs[1].astype(F32)], axis=1)
-    out_ref[...] = (jnp.where(r % 2 == 0, piece[0:8], piece[8:16]) + part).astype(BF16)
-
-
-def norm_back_kernel(arrived_ref, hat_ref, gain_ref, scale_ref, out_ref):
-    total = jnp.concatenate([arrived_ref[:, j, :] for j in range(4)], axis=1)
+    out_ref[...] = (own_ref[...] + part).astype(BF16)
     hat = hat_ref[...]
-    g = total * gain_ref[...]
+    g = total[:, 0:LANES] * gain_ref[...]
     mean = jnp.sum(g, keepdims=True) * (1.0 / (VIS * SPLIT))
     cross = jnp.sum(g * hat, keepdims=True) * (1.0 / (VIS * SPLIT))
     result = scale_ref[0:1, 0:1] * (g - mean - hat * cross)
     for v in range(VIS):
-        out_ref[:, v * SPLIT : (v + 1) * SPLIT] = result[v : v + 1, 0:SPLIT]
+        image_ref[:, v * SPLIT : (v + 1) * SPLIT] = result[v : v + 1, 0:SPLIT]
 
 
 def full(shape):
@@ -343,12 +367,13 @@
     arrived = swap(message, OWNERS)
     spread = call(spread_kernel, struct((RC, VIS, 640), BF16), arrived, in_hbm(cotangent))
     rows = swap(spread, GROUP)
-    partial, target, bias = call(
+    partial, target, bias, mine = call(
         first_kernel,
         (
             struct((PAIR, CHIPS, OWN, 768), BF16),
             struct((8, RC * VIS), jnp.int32),
             struct((1, 128), F32),
+            struct((2, 8, 128), jnp.int32),
         ),
         in_hbm(counts),
         in_hbm(block_order),
@@ -380,10 +405,11 @@
     inputs = swap(spread, GROUP)
     block_part, bundle = local(
         block_kernel,
-        (struct((RC, OWN, 128), BF16), struct((37, OWN, 128), BF16)),
+        (struct((RC, OWN, 128), BF16), struct((BUNDLE, OWN, 128), BF16)),
         inputs,
         pieces,
         hidden_proj,
+        proj_first,
         gathered,
     )
     bundles = in_hbm(lax.all_gather(bundle, OWNERS))
@@ -391,42 +417,44 @@
     whole = swap(spread, GROUP)
     sent = local(back_kernel, struct((VIS, OWN, 384), BF16), whole, slope, back, seconds)
     blocks = swap(sent, OWNERS)
-    slot_part, acts = local(
+    slot_part = local(
         slot_kernel,
-        (struct((RC, VIS, 640), BF16), struct((RC * VIS, 128), BF16)),
-        target,
+        struct((RC, VIS, 640), BF16),
+        mine,
         blocks,
-        proj_first,
         down_w,
         bundles,
         scratch=[
-            pltpu.VMEM((LANES, 128), BF16),
+            pltpu.VMEM((VIS, 32, OWN, 128), BF16),
             pltpu.VMEM((VIS, 4, OWN, 128), BF16),
-            pltpu.SemaphoreType.DMA,
+            pltpu.VMEM((4, RC * VIS, 128), F32),
+            pltpu.SemaphoreType.DMA((2,)),
         ],
         remote=1,
     )
     slots = swap(slot_part, GROUP)
-    first_grad, second_grad = call(
+    first_grad, second_grad, own_inputs = local(
         weight_grad_kernel,
-        (struct((SPLIT, 128), F32), struct((128, 256), F32)),
+        (struct((SPLIT, 128), F32), struct((128, 256), F32), struct((8, 256), F32)),
+        target,
         blocks,
-        acts,
         rows,
         bundles,
-        specs=[pl.BlockSpec((VIS, 1, OWN, 128), lambda i: (0, 36, 0, 0))],
-    )
-    message, block_out = local(
-        slot_sum_kernel,
-        (struct((VIS, 8, 128), F32), struct((8, 256), BF16)),
+        scratch=[
+            pltpu.VMEM((VIS, OWN, 128), BF16),
+            pltpu.VMEM((2, OWN, 128), BF16),
+            pltpu.SemaphoreType.DMA((2,)),
+        ],
+        remote=1,
+    )
+    image_grad, block_out = local(
+        last_kernel,
+        (struct((1, VIS * SPLIT), F32), struct((8, 256), BF16)),
         slots,
-        bundles,
-        scratch=[pltpu.VMEM((2, OWN, 128), BF16), pltpu.SemaphoreType.DMA],
-        remote=1,
-    )
-    message, first_grad, second_grad = lax.optimization_barrier((message, first_grad, second_grad))
-    image_grad = local(
-        norm_back_kernel, struct((1, VIS * SPLIT), F32), swap(message, OWNERS), hat, gains, scale
+        own_inputs,
+        hat,
+        gains,
+        scale,
     )
     return block_out, image_grad, first_grad, second_grad
 

time: 216 us -> 206 us (0.954); the launches traced: 215 us -> 202 us
  blocking collectives: 163 us -> 146 us
  starting transfers between devices: 3.99 us -> 7.67 us
    all_to_all x10 -> x9, blocking collectives: 163 us -> 146 us  [swap(): return lax.all_to_all(blocks, axes, 0, 0, tiled=True)]
    all_to_all x1, starting transfers between devices: 3.91 us -> 7.59 us  [swap(): return lax.all_to_all(blocks, axes, 0, 0, tiled=True)]
    pallas_call x4 -> x3, Pallas kernels: 5.75 us -> 3.87 us  [call(): pl.pallas_call(kernel, grid=(1,), out_shape=outs, in_specs=ins, out_specs...]
where the time goes in v8:
time: 206 us; the launch traced here: 202 us
  blocking collectives  146 us (71%)
  Pallas kernels  18.3 us (9%)
  waiting for transfers between devices  15.4 us (7%)
  between operations  14.1 us (7%)
  starting transfers between devices  7.67 us (4%)
    all_to_all x9, blocking collectives, swap(): return lax.all_to_all(blocks, axes, 0, 0, tiled=True)  146 us
    all_to_all x1, waiting for transfers between devices, swap(): return lax.all_to_all(blocks, axes, 0, 0, tiled=True)  14.8 us
    pallas_call x9, Pallas kernels, local(): pl.pallas_call(kernel, out_shape=outs, in_specs=ins + [pl.BlockSpec(memor...  12.5 us
    all_to_all x1, starting transfers between devices, swap(): return lax.all_to_all(blocks, axes, 0, 0, tiled=True)  7.59 us
  transfers between devices with their start and end apart: 3, of which 2 were waited for; matrix products, arithmetic and copies ran while one was open for 0% of the time, Pallas kernels for 3%

profile of v8, /device:TPU:1, one launch (start us, length us, event | category | flops | bytes accessed | tf_op | source)
XLA Modules:
  0.0 202.3 jit_solution(14169301103173159316)
XLA Ops:
  7.2 2.0 shard_map.142
  9.2 0.0 all-gather.7.cloned.1.call-start
  9.3 0.8 reshape.14.gain_ref
  10.0 1.1 shard_map.138
  11.2 17.1 %all_to_all.50.arrived_ref = f32[16,8,128]{2,1,0:T(8,128)S(1)} all-to-all(f32[16,8,128]{2,1,0:T(8,128)S(1)} %get-tuple-element.24), channel_id=1, replica_groups=mesh['chip'=8,'core'=2,'row'=4,'col'=8] {'chip','core'}, dimensions={0} | all-to-all | bytes 131072 | tf_op jit(solution)/shard_map/all_to_all | solution.py:339
  28.3 0.7 shard_map.139
  29.0 28.5 %all_to_all.51.rows_ref = bf16[32,16,640]{2,1,0:T(8,128)(2,1)S(1)} all-to-all(bf16[32,16,640]{2,1,0:T(8,128)(2,1)S(1)} %shard_map.139), channel_id=1, replica_groups=mesh['chip'=8,'core'=2,'row'=4,'col'=8] {'row','col'}, dimensions={0} | all-to-all | bytes 1310720 | tf_op jit(solution)/shard_map/all_to_all | solution.py:339
  57.6 2.0 shard_map.140
  59.6 7.6 %all_to_all.52.arrived_ref = bf16[2,8,16,768]{3,2,1,0:T(8,128)(2,1)S(1)} all-to-all(bf16[2,8,16,768]{3,2,1,0:T(8,128)(2,1)S(1)} %get-tuple-element.26), channel_id=1, replica_groups=mesh['chip'=8,'core'=2,'row'=4,'col'=8] {'core'}, dimensions={0} | all-to-all | bytes 786432 | tf_op jit(solution)/shard_map/all_to_all | solution.py:339
  67.2 15.2 %all_to_all.53.arrived_ref.pieces_ref = bf16[8,16,768]{2,1,0:T(8,128)(2,1)S(1)} all-to-all(bf16[8,16,768]{2,1,0:T(8,128)(2,1)S(1)} %shard_map.141), channel_id=1, replica_groups=mesh['chip'=8,'core'=2,'row'=4,'col'=8] {'chip'}, dimensions={0} | all-to-all | bytes 393216 | tf_op jit(solution)/shard_map/all_to_all | solution.py:339
  82.4 0.6 all-gather.5.cloned.1.call-done
  82.9 1.6 shard_map.143
  84.6 19.6 %all_to_all.54.arrived_ref = bf16[32,16,128]{2,1,0:T(8,128)(2,1)S(1)} all-to-all(bf16[32,16,128]{2,1,0:T(8,128)(2,1)S(1)} %get-tuple-element.28), channel_id=1, replica_groups=mesh['chip'=8,'core'=2,'row'=4,'col'=8] {'row','col'}, dimensions={0} | all-to-all | bytes 262144 | tf_op jit(solution)/shard_map/all_to_all | solution.py:339
  104.2 13.4 %all_to_all.55.inputs_ref = bf16[32,16,128]{2,1,0:T(8,128)(2,1)S(1)} all-to-all(bf16[32,16,128]{2,1,0:T(8,128)(2,1)S(1)} %shard_map.144), channel_id=1, replica_groups=mesh['chip'=8,'core'=2,'row'=4,'col'=8] {'row','col'}, dimensions={0} | all-to-all | bytes 262144 | tf_op jit(solution)/shard_map/all_to_all | solution.py:339
  117.6 4.0 %shard_map.145 = (bf16[32,16,128]{2,1,0:T(8,128)(2,1)S(1)}, bf16[62,16,128]{2,1,0:T(8,128)(2,1)}) custom-call(bf16[32,16,128]{2,1,0:T(8,128)(2,1)S(1)} %all_to_all.55.inputs_ref, bf16[8,16,768]{2,1,0:T(8,128)(2,1)S(1)} %all_to_all.53.arrived_ref.pieces_ref, bf16[16,128]{1,0:T(8,128)(2,1)S(1)} %get-tuple-element.29.act_ref, bf16[400,128]{1,0:T(8,128)(2,1)S(1)} %copy-done.2, ...), custom_call_target="tpu_custom_call" | custom-call | tf_op jit(solution)/shard_map/pallas_call | solution.py:328
  121.6 12.7 %all_to_all.56.arrived_ref = bf16[32,16,128]{2,1,0:T(8,128)(2,1)S(1)} all-to-all(bf16[32,16,128]{2,1,0:T(8,128)(2,1)S(1)} %get-tuple-element.30), channel_id=1, replica_groups=mesh['chip'=8,'core'=2,'row'=4,'col'=8] {'row','col'}, dimensions={0} | all-to-all | bytes 262144 | tf_op jit(solution)/shard_map/all_to_all | solution.py:339
  134.4 12.7 %all_to_all.57.grad_ref = bf16[32,16,128]{2,1,0:T(8,128)(2,1)S(1)} all-to-all(bf16[32,16,128]{2,1,0:T(8,128)(2,1)S(1)} %shard_map.146), channel_id=1, replica_groups=mesh['chip'=8,'core'=2,'row'=4,'col'=8] {'row','col'}, dimensions={0} | all-to-all | bytes 262144 | tf_op jit(solution)/shard_map/all_to_all | solution.py:339
  147.1 0.4 shard_map.147
  147.5 19.2 %all_to_all.58.pieces_ref = bf16[16,16,384]{2,1,0:T(8,128)(2,1)S(1)} all-to-all(bf16[16,16,384]{2,1,0:T(8,128)(2,1)S(1)} %shard_map.147), channel_id=1, replica_groups=mesh['chip'=8,'core'=2,'row'=4,'col'=8] {'chip','core'}, dimensions={0} | all-to-all | bytes 393216 | tf_op jit(solution)/shard_map/all_to_all | solution.py:339
  166.7 3.6 %shard_map.148 = bf16[32,16,640]{2,1,0:T(8,128)(2,1)} custom-call(s32[2,8,128]{2,1,0:T(8,128)S(1)} %get-tuple-element.25.mine_ref, bf16[16,16,384]{2,1,0:T(8,128)(2,1)S(1)} %all_to_all.58.pieces_ref, bf16[512,256]{1,0:T(8,128)(2,1)S(1)} %copy-done.1, bf16[16,62,16,128]{3,2,1,0:T(8,128)(2,1)} %bitcast.5), custom_call_target="tpu_custom_call" | custom-call | tf_op jit(solution)/shard_map/pallas_call | solution.py:328
  170.3 7.6 %all-to-all-start.9 = ((bf16[32,16,640]{2,1,0:T(8,128)(2,1)}), bf16[32,16,640]{2,1,0:T(8,128)(2,1)S(1)}, u32[]{:S(2)}, u32[]{:S(2)}) async-start(bf16[32,16,640]{2,1,0:T(8,128)(2,1)} %shard_map.148), calls=%async_computation.9 | async-start | bytes 1310720 | tf_op jit(solution)/shard_map/all_to_all | solution.py:339
  177.9 1.8 shard_map.149
  179.8 14.8 %all-to-all-done.9.arrived_ref = bf16[32,16,640]{2,1,0:T(8,128)(2,1)S(1)} async-done(((bf16[32,16,640]{2,1,0:T(8,128)(2,1)}), bf16[32,16,640]{2,1,0:T(8,128)(2,1)S(1)}, u32[]{:S(2)}, u32[]{:S(2)}) %all-to-all-start.9) | async-done | bytes 655392 | tf_op jit(solution)/shard_map/all_to_all | solution.py:339
  194.6 0.9 shard_map.150
  (13 shorter events, 0.2 us)
Async XLA Ops:
  7.2 110.4 %copy-start.2 = (bf16[400,128]{1,0:T(8,128)(2,1)S(1)}, bf16[400,128]{1,0:T(8,128)(2,1)}, u32[]{:S(2)}) copy-start(bf16[400,128]{1,0:T(8,128)(2,1)} %first_ref.3) | copy-start | bytes 307204
  7.2 75.8 %all-gather.5.cloned.1.call-start = ((), (), s32[]{:S(2)}) async-start(), calls=%async_computation.10 | async-start | bytes 10027008 | tf_op jit(solution)/shard_map/all_gather | solution.py:353
  9.2 157.5 %all-gather.7.cloned.1.call-start = ((), (), s32[]{:S(2)}) async-start(), calls=%async_computation.11 | async-start | bytes 4317184 | tf_op jit(solution)/shard_map/all_gather | solution.py:415
  82.9 34.6 %copy-start = (bf16[18432,256]{1,0:T(8,128)(2,1)S(1)}, bf16[18432,256]{1,0:T(8,128)(2,1)}, u32[]{:S(2)}) copy-start(bf16[18432,256]{1,0:T(8,128)(2,1)} %all-gather.5.cloned.1.call-done) | copy-start | bytes 28311556
  82.9 83.8 %copy-start.1 = (bf16[512,256]{1,0:T(8,128)(2,1)S(1)}, bf16[512,256]{1,0:T(8,128)(2,1)}, u32[]{:S(2)}) copy-start(bf16[512,256]{1,0:T(8,128)(2,1)} %down_ref.3) | copy-start | bytes 786436
  170.3 24.2 %all-to-all-start.9 = ((bf16[32,16,640]{2,1,0:T(8,128)(2,1)}), bf16[32,16,640]{2,1,0:T(8,128)(2,1)S(1)}, u32[]{:S(2)}, u32[]{:S(2)}) async-start(bf16[32,16,640]{2,1,0:T(8,128)(2,1)} %shard_map.148), calls=%async_computation.9 | async-start | bytes 1310720 | tf_op jit(solution)/shard_map/all_to_all | solution.py:339
Sparse Core Ops, SparseCore 0:
  10.1 72.7 all-gather.4
  121.7 39.5 all-gather.6

commit v9 on v8

--- a/solution.py
+++ b/solution.py
@@ -16,8 +16,9 @@
 BF16 = jnp.bfloat16
 PAIR = 2
 CHIPS = VIS // PAIR
-FIRST = 37
-BUNDLE = 62
+HIDDEN = 2
+FIRST = 6
+BUNDLE = 31
 GROUP = ("row", "col")
 OWNERS = ("chip", "core")
 
@@ -185,10 +186,15 @@
         out_ref[r] = own
 
 
-def block_kernel(inputs_ref, pieces_ref, act_ref, first_ref, w_ref, out_ref, bundle_ref):
+def own_sum_kernel(arrived_ref, out_ref, own_ref):
+    sum_kernel(arrived_ref, out_ref)
+    own_ref[...] = out_ref[0]
+
+
+def block_kernel(inputs_ref, pieces_ref, act_ref, own_ref, first_ref, w_ref, out_ref, bundle_ref):
+    bundle_ref[0] = own_ref[...]
+    bundle_ref[1] = act_ref[...]
     bundle_ref[FIRST : FIRST + 25] = first_ref[...].reshape(25, OWN, 128)
-    bundle_ref[0:RC] = inputs_ref[...]
-    bundle_ref[36] = act_ref[...]
     sums = [jnp.zeros((OWN, 256), F32) for _ in range(4)]
     for v in range(VIS):
         x = jnp.concatenate([inputs_ref[2 * v], inputs_ref[2 * v + 1]], axis=1)
@@ -202,7 +208,7 @@
     s = jax.nn.sigmoid(g)
     hidden = (g * s * u).astype(BF16)
     for k in range(4):
-        bundle_ref[RC + k] = hidden[:, 128 * k : 128 * k + 128]
+        bundle_ref[HIDDEN + k] = hidden[:, 128 * k : 128 * k + 128]
     gate_grad = (h * u * s * (1.0 + g * (1.0 - s))).astype(BF16)
     up_grad = (h * g * s).astype(BF16)
     grads = [gate_grad[:, 0:256], gate_grad[:, 256:512], up_grad[:, 0:256], up_grad[:, 256:512]]
@@ -227,14 +233,16 @@
 
 
 def slot_kernel(
-    mine_ref, pieces_ref, down_ref, bundles_ref, out_ref, first_ref, hidden_ref, spread, sems
+    mine_ref, pieces_ref, down_ref, bundles_ref, out_ref, first_ref, hidden_ref, own_ref, spread, sems
 ):
+    copy_hidden = pltpu.make_async_copy(bundles_ref.at[:, pl.ds(HIDDEN, 4)], hidden_ref, sems.at[0])
+    copy_own = pltpu.make_async_copy(bundles_ref.at[:, 0], own_ref, sems.at[1])
     copy_first = pltpu.make_async_copy(
-        bundles_ref.at[:, pl.ds(FIRST, 25)], first_ref.at[:, pl.ds(0, 25)], sems.at[0]
-    )
-    copy_hidden = pltpu.make_async_copy(bundles_ref.at[:, pl.ds(RC, 4)], hidden_ref, sems.at[1])
+        bundles_ref.at[:, pl.ds(FIRST, 25)], first_ref.at[:, pl.ds(0, 25)], sems.at[2]
+    )
+    copy_hidden.start()
+    copy_own.start()
     copy_first.start()
-    copy_hidden.start()
     first_ref[:, 25:32] = jnp.zeros((VIS, 7, OWN, 128), BF16)
     language = lax.broadcasted_iota(jnp.int32, (RC, ROWS), 1)
     slot = lax.broadcasted_iota(jnp.int32, (RC, ROWS), 0)
@@ -242,51 +250,45 @@
     act = dot(
         jnp.where(hit, 1.0, 0.0).astype(BF16), pieces_ref[:, :, 256:384].reshape(ROWS, 128)
     ).astype(BF16)
+    r = group_index()
+    v = owner_index()
+    copy_hidden.wait()
+    copy_own.wait()
+    hidden = jnp.concatenate([hidden_ref[:, k].reshape(ROWS, 128) for k in range(4)], axis=1)
+    block = dot(hidden, down_ref[...])
+    own = own_ref[...].reshape(ROWS, 128).astype(F32)
+    left = block[:, 0:128] + jnp.where(r == 2 * v, own, 0.0)
+    right = block[:, 128:256] + jnp.where(r == 2 * v + 1, own, 0.0)
+    block = jnp.concatenate([left.reshape(RC, 8, 128), right.reshape(RC, 8, 128)], axis=1)
+    out_ref[:, :, LANES : LANES + 128] = block.astype(BF16)
     copy_first.wait()
-    for v in range(VIS):
-        y = dot(act, first_ref[v].reshape(LANES, 128), 1, 1)
+    for i in range(VIS):
+        y = dot(act, first_ref[i].reshape(LANES, 128), 1, 1)
         for k in range(4):
-            spread[k, pl.ds(v, RC, stride=VIS), :] = y[:, 128 * k : 128 * k + 128]
+            spread[k, pl.ds(i, RC, stride=VIS), :] = y[:, 128 * k : 128 * k + 128]
     for k in range(4):
         out_ref[:, :, 128 * k : 128 * k + 128] = spread[k].astype(BF16).reshape(RC, VIS, 128)
-    copy_hidden.wait()
-    hidden = jnp.concatenate([hidden_ref[:, k].reshape(ROWS, 128) for k in range(4)], axis=1)
-    block = dot(hidden, down_ref[...])
-    block = jnp.concatenate(
-        [block[:, 0:128].reshape(RC, 8, 128), block[:, 128:256].reshape(RC, 8, 128)], axis=1
-    )
-    out_ref[:, :, LANES : LANES + 128] = block.astype(BF16)
-
-
-def weight_grad_kernel(
-    target_ref, pieces_ref, rows_ref, bundles_ref, first_ref, second_ref, own_ref, hidden_ref, inputs, sems
-):
-    r = group_index()
-    copy_hidden = pltpu.make_async_copy(bundles_ref.at[:, 36], hidden_ref, sems.at[0])
-    copy_inputs = pltpu.make_async_copy(
-        bundles_ref.at[r // 2, pl.ds(2 * owner_index(), 2)], inputs, sems.at[1]
-    )
-    copy_hidden.start()
-    copy_inputs.start()
+
+
+def weight_grad_kernel(target_ref, pieces_ref, rows_ref, bundles_ref, first_ref, second_ref, hidden_ref, sem):
+    copy = pltpu.make_async_copy(bundles_ref.at[:, 1], hidden_ref, sem)
+    copy.start()
     act = pieces_ref[:, :, 256:384].reshape(ROWS, 128)
     act = dot(selection(target_ref), act, 0, 0).astype(BF16)
     rows = rows_ref[:, :, 0:LANES].reshape(RC * VIS, LANES)
     first_ref[...] = dot(rows, act, 0, 0)[0:SPLIT, :]
     ig = pieces_ref[:, :, 0:256].reshape(ROWS, 256).astype(F32) + language_cotangent(rows_ref)
-    copy_hidden.wait()
+    copy.wait()
     second_ref[...] = dot(hidden_ref[...].reshape(ROWS, 128), ig.astype(BF16), 0, 0)
-    copy_inputs.wait()
-    piece = jnp.concatenate([inputs[0].astype(F32), inputs[1].astype(F32)], axis=1)
-    own_ref[...] = jnp.where(r % 2 == 0, piece[0:8], piece[8:16])
-
-
-def last_kernel(arrived_ref, own_ref, hat_ref, gain_ref, scale_ref, image_ref, out_ref):
+
+
+def last_kernel(arrived_ref, hat_ref, gain_ref, scale_ref, image_ref, out_ref):
     total = jnp.zeros((VIS, LANES + 128), F32)
     for i in range(RC):
         total = total + arrived_ref[i].astype(F32)
     part = total[:, LANES : LANES + 128]
     part = jnp.concatenate([part[0:8], part[8:16]], axis=1)
-    out_ref[...] = (own_ref[...] + part).astype(BF16)
+    out_ref[...] = part.astype(BF16)
     hat = hat_ref[...]
     g = total[:, 0:LANES] * gain_ref[...]
     mean = jnp.sum(g, keepdims=True) * (1.0 / (VIS * SPLIT))
@@ -401,7 +403,9 @@
         scratch=[pltpu.SemaphoreType.DMA],
         remote=1,
     )
-    spread = local(sum_kernel, struct((RC, OWN, 128), BF16), swap(input_part, GROUP))
+    spread, own = local(
+        own_sum_kernel, (struct((RC, OWN, 128), BF16), struct((OWN, 128), BF16)), swap(input_part, GROUP)
+    )
     inputs = swap(spread, GROUP)
     block_part, bundle = local(
         block_kernel,
@@ -409,6 +413,7 @@
         inputs,
         pieces,
         hidden_proj,
+        own,
         proj_first,
         gathered,
     )
@@ -427,31 +432,27 @@
         scratch=[
             pltpu.VMEM((VIS, 32, OWN, 128), BF16),
             pltpu.VMEM((VIS, 4, OWN, 128), BF16),
+            pltpu.VMEM((VIS, OWN, 128), BF16),
             pltpu.VMEM((4, RC * VIS, 128), F32),
-            pltpu.SemaphoreType.DMA((2,)),
+            pltpu.SemaphoreType.DMA((3,)),
         ],
         remote=1,
     )
     slots = swap(slot_part, GROUP)
-    first_grad, second_grad, own_inputs = local(
+    first_grad, second_grad = local(
         weight_grad_kernel,
-        (struct((SPLIT, 128), F32), struct((128, 256), F32), struct((8, 256), F32)),
+        (struct((SPLIT, 128), F32), struct((128, 256), F32)),
         target,
         blocks,
         rows,
         bundles,
-        scratch=[
-            pltpu.VMEM((VIS, OWN, 128), BF16),
-            pltpu.VMEM((2, OWN, 128), BF16),
-            pltpu.SemaphoreType.DMA((2,)),
-        ],
+        scratch=[pltpu.VMEM((VIS, OWN, 128), BF16), pltpu.SemaphoreType.DMA],
         remote=1,
     )
     image_grad, block_out = local(
         last_kernel,
         (struct((1, VIS * SPLIT), F32), struct((8, 256), BF16)),
         slots,
-        own_inputs,
         hat,
         gains,
         scale,

time: 206 us -> 202 us (0.981)
  starting transfers between devices: 7.67 us -> 4.07 us
    all_to_all x1, starting transfers between devices: 7.59 us -> 3.99 us  [swap(): return lax.all_to_all(blocks, axes, 0, 0, tiled=True)]
where the time goes in v9:
time: 202 us; the launch traced here: 199 us
  blocking collectives  146 us (72%)
  Pallas kernels  18 us (9%)
  waiting for transfers between devices  15.7 us (8%)
  between operations  14.1 us (7%)
  starting transfers between devices  4.07 us (2%)
    all_to_all x9, blocking collectives, swap(): return lax.all_to_all(blocks, axes, 0, 0, tiled=True)  146 us
    all_to_all x1, waiting for transfers between devices, swap(): return lax.all_to_all(blocks, axes, 0, 0, tiled=True)  15.1 us
    pallas_call x9, Pallas kernels, local(): pl.pallas_call(kernel, out_shape=outs, in_specs=ins + [pl.BlockSpec(memor...  12.2 us
  transfers between devices with their start and end apart: 3, of which 2 were waited for; matrix products, arithmetic and copies ran while one was open for 0% of the time, Pallas kernels for 3%

profile of v9, /device:TPU:1, one launch (start us, length us, event | category | flops | bytes accessed | tf_op | source)
XLA Modules:
  0.0 199.0 jit_solution(4696357205837702124)
XLA Ops:
  7.2 1.9 shard_map.142
  9.2 0.0 all-gather.7.cloned.1.call-start
  9.3 0.8 reshape.14.gain_ref
  10.0 1.1 shard_map.138
  11.1 17.1 %all_to_all.50.arrived_ref = f32[16,8,128]{2,1,0:T(8,128)S(1)} all-to-all(f32[16,8,128]{2,1,0:T(8,128)S(1)} %get-tuple-element.25), channel_id=1, replica_groups=mesh['chip'=8,'core'=2,'row'=4,'col'=8] {'chip','core'}, dimensions={0} | all-to-all | bytes 131072 | tf_op jit(solution)/shard_map/all_to_all | solution.py:341
  28.3 0.7 shard_map.139
  29.0 28.5 %all_to_all.51.rows_ref = bf16[32,16,640]{2,1,0:T(8,128)(2,1)S(1)} all-to-all(bf16[32,16,640]{2,1,0:T(8,128)(2,1)S(1)} %shard_map.139), channel_id=1, replica_groups=mesh['chip'=8,'core'=2,'row'=4,'col'=8] {'row','col'}, dimensions={0} | all-to-all | bytes 1310720 | tf_op jit(solution)/shard_map/all_to_all | solution.py:341
  57.5 2.0 %shard_map.140 = (bf16[2,8,16,768]{3,2,1,0:T(8,128)(2,1)S(1)}, s32[8,512]{1,0:T(8,128)S(1)}, f32[1,128]{1,0:T(1,128)S(1)}, s32[2,8,128]{2,1,0:T(8,128)S(1)}) custom-call(s32[16]{0:T(128)} %counts_ref.1, s32[16]{0:T(128)} %order_ref.1, bf16[32,16,640]{2,1,0:T(8,128)(2,1)S(1)} %all_to_all.51.rows_ref, bf16[400,128]{1,0:T(8,128)(2,1)} %first_ref.3, ...), custom_call_target="tpu_custom_call" | custom-call | tf_op jit(solution)/shard_map/pallas_call | solution.py:317
  59.6 7.6 %all_to_all.52.arrived_ref = bf16[2,8,16,768]{3,2,1,0:T(8,128)(2,1)S(1)} all-to-all(bf16[2,8,16,768]{3,2,1,0:T(8,128)(2,1)S(1)} %get-tuple-element.27), channel_id=1, replica_groups=mesh['chip'=8,'core'=2,'row'=4,'col'=8] {'core'}, dimensions={0} | all-to-all | bytes 786432 | tf_op jit(solution)/shard_map/all_to_all | solution.py:341
  67.2 15.2 %all_to_all.53.arrived_ref.pieces_ref = bf16[8,16,768]{2,1,0:T(8,128)(2,1)S(1)} all-to-all(bf16[8,16,768]{2,1,0:T(8,128)(2,1)S(1)} %shard_map.141), channel_id=1, replica_groups=mesh['chip'=8,'core'=2,'row'=4,'col'=8] {'chip'}, dimensions={0} | all-to-all | bytes 393216 | tf_op jit(solution)/shard_map/all_to_all | solution.py:341
  82.4 0.6 all-gather.5.cloned.1.call-done
  82.9 1.6 shard_map.143
  84.6 19.6 %all_to_all.54.arrived_ref = bf16[32,16,128]{2,1,0:T(8,128)(2,1)S(1)} all-to-all(bf16[32,16,128]{2,1,0:T(8,128)(2,1)S(1)} %get-tuple-element.29), channel_id=1, replica_groups=mesh['chip'=8,'core'=2,'row'=4,'col'=8] {'row','col'}, dimensions={0} | all-to-all | bytes 262144 | tf_op jit(solution)/shard_map/all_to_all | solution.py:341
  104.2 13.4 %all_to_all.55.inputs_ref = bf16[32,16,128]{2,1,0:T(8,128)(2,1)S(1)} all-to-all(bf16[32,16,128]{2,1,0:T(8,128)(2,1)S(1)} %get-tuple-element.30), channel_id=1, replica_groups=mesh['chip'=8,'core'=2,'row'=4,'col'=8] {'row','col'}, dimensions={0} | all-to-all | bytes 262144 | tf_op jit(solution)/shard_map/all_to_all | solution.py:341
  117.6 4.0 %shard_map.145 = (bf16[32,16,128]{2,1,0:T(8,128)(2,1)S(1)}, bf16[31,16,128]{2,1,0:T(8,128)(2,1)}) custom-call(bf16[32,16,128]{2,1,0:T(8,128)(2,1)S(1)} %all_to_all.55.inputs_ref, bf16[8,16,768]{2,1,0:T(8,128)(2,1)S(1)} %all_to_all.53.arrived_ref.pieces_ref, bf16[16,128]{1,0:T(8,128)(2,1)S(1)} %get-tuple-element.31.act_ref, ...), custom_call_target="tpu_custom_call" | custom-call | tf_op jit(solution)/shard_map/pallas_call | solution.py:330
  121.6 12.7 %all_to_all.56.arrived_ref = bf16[32,16,128]{2,1,0:T(8,128)(2,1)S(1)} all-to-all(bf16[32,16,128]{2,1,0:T(8,128)(2,1)S(1)} %get-tuple-element.33), channel_id=1, replica_groups=mesh['chip'=8,'core'=2,'row'=4,'col'=8] {'row','col'}, dimensions={0} | all-to-all | bytes 262144 | tf_op jit(solution)/shard_map/all_to_all | solution.py:341
  134.3 12.7 %all_to_all.57.grad_ref = bf16[32,16,128]{2,1,0:T(8,128)(2,1)S(1)} all-to-all(bf16[32,16,128]{2,1,0:T(8,128)(2,1)S(1)} %shard_map.146), channel_id=1, replica_groups=mesh['chip'=8,'core'=2,'row'=4,'col'=8] {'row','col'}, dimensions={0} | all-to-all | bytes 262144 | tf_op jit(solution)/shard_map/all_to_all | solution.py:341
  147.0 0.4 shard_map.147
  147.4 19.5 %all_to_all.58.pieces_ref = bf16[16,16,384]{2,1,0:T(8,128)(2,1)S(1)} all-to-all(bf16[16,16,384]{2,1,0:T(8,128)(2,1)S(1)} %shard_map.147), channel_id=1, replica_groups=mesh['chip'=8,'core'=2,'row'=4,'col'=8] {'chip','core'}, dimensions={0} | all-to-all | bytes 393216 | tf_op jit(solution)/shard_map/all_to_all | solution.py:341
  166.9 3.4 %shard_map.148 = bf16[32,16,640]{2,1,0:T(8,128)(2,1)} custom-call(s32[2,8,128]{2,1,0:T(8,128)S(1)} %get-tuple-element.26.mine_ref, bf16[16,16,384]{2,1,0:T(8,128)(2,1)S(1)} %all_to_all.58.pieces_ref, bf16[512,256]{1,0:T(8,128)(2,1)S(1)} %copy-done.1, bf16[16,31,16,128]{3,2,1,0:T(8,128)(2,1)} %bitcast.5), custom_call_target="tpu_custom_call" | custom-call | tf_op jit(solution)/shard_map/pallas_call | solution.py:330
  170.4 4.0 %all-to-all-start.9 = ((bf16[32,16,640]{2,1,0:T(8,128)(2,1)}), bf16[32,16,640]{2,1,0:T(8,128)(2,1)S(1)}, u32[]{:S(2)}, u32[]{:S(2)}) async-start(bf16[32,16,640]{2,1,0:T(8,128)(2,1)} %shard_map.148), calls=%async_computation.9 | async-start | bytes 1310720 | tf_op jit(solution)/shard_map/all_to_all | solution.py:341
  174.4 1.7 shard_map.150
  176.1 15.1 %all-to-all-done.9.arrived_ref = bf16[32,16,640]{2,1,0:T(8,128)(2,1)S(1)} async-done(((bf16[32,16,640]{2,1,0:T(8,128)(2,1)}), bf16[32,16,640]{2,1,0:T(8,128)(2,1)S(1)}, u32[]{:S(2)}, u32[]{:S(2)}) %all-to-all-start.9) | async-done | bytes 655392 | tf_op jit(solution)/shard_map/all_to_all | solution.py:341
  191.3 0.9 shard_map.149
  (13 shorter events, 0.2 us)
Async XLA Ops:
  7.2 110.4 %copy-start.2 = (bf16[400,128]{1,0:T(8,128)(2,1)S(1)}, bf16[400,128]{1,0:T(8,128)(2,1)}, u32[]{:S(2)}) copy-start(bf16[400,128]{1,0:T(8,128)(2,1)} %first_ref.3) | copy-start | bytes 307204
  7.2 75.8 %all-gather.5.cloned.1.call-start = ((), (), s32[]{:S(2)}) async-start(), calls=%async_computation.10 | async-start | bytes 10027008 | tf_op jit(solution)/shard_map/all_gather | solution.py:355
  9.2 157.7 %all-gather.7.cloned.1.call-start = ((), (), s32[]{:S(2)}) async-start(), calls=%async_computation.11 | async-start | bytes 2158592 | tf_op jit(solution)/shard_map/all_gather | solution.py:420
  82.9 34.6 %copy-start = (bf16[18432,256]{1,0:T(8,128)(2,1)S(1)}, bf16[18432,256]{1,0:T(8,128)(2,1)}, u32[]{:S(2)}) copy-start(bf16[18432,256]{1,0:T(8,128)(2,1)} %all-gather.5.cloned.1.call-done) | copy-start | bytes 28311556
  82.9 84.0 %copy-start.1 = (bf16[512,256]{1,0:T(8,128)(2,1)S(1)}, bf16[512,256]{1,0:T(8,128)(2,1)}, u32[]{:S(2)}) copy-start(bf16[512,256]{1,0:T(8,128)(2,1)} %down_ref.3) | copy-start | bytes 786436
  170.4 20.9 %all-to-all-start.9 = ((bf16[32,16,640]{2,1,0:T(8,128)(2,1)}), bf16[32,16,640]{2,1,0:T(8,128)(2,1)S(1)}, u32[]{:S(2)}, u32[]{:S(2)}) async-start(bf16[32,16,640]{2,1,0:T(8,128)(2,1)} %shard_map.148), calls=%async_computation.9 | async-start | bytes 1310720 | tf_op jit(solution)/shard_map/all_to_all | solution.py:341
Sparse Core Ops, SparseCore 0:
  10.1 72.7 all-gather.4
  121.7 36.9 all-gather.6

commit v10 on v9

--- a/solution.py
+++ b/solution.py
@@ -156,10 +156,14 @@
 
 
 def second_kernel(
-    arrived_ref, bias_ref, weights_ref, out_ref, hidden_ref, slope_ref, back_ref, second_ref, sem
+    arrived_ref, bias_ref, weights_ref, out_ref, hidden_ref, slope_ref, back_ref, second_ref, sems
 ):
-    copy = pltpu.make_async_copy(weights_ref.at[:, pl.ds(1024, 128), :], second_ref, sem)
-    copy.start()
+    copies = [
+        pltpu.make_async_copy(weights_ref.at[v, pl.ds(1024, 128), :], second_ref.at[v], sems.at[v])
+        for v in range(VIS)
+    ]
+    for copy in copies:
+        copy.start()
     both = jnp.zeros((OWN, 256), F32)
     for v in range(CHIPS):
         both = both + arrived_ref[v, :, 512:768].astype(F32)
@@ -170,8 +174,8 @@
     hidden = (pre * cdf).astype(BF16)
     hidden_ref[...] = hidden
     slope_ref[...] = cdf + pre * density
-    copy.wait()
-    for v in range(VIS):
+    for v in range(VIS):
+        copies[v].wait()
         y = dot(hidden, second_ref[v]).astype(BF16)
         out_ref[2 * v] = y[:, 0:128]
         out_ref[2 * v + 1] = y[:, 128:256]
@@ -237,12 +241,16 @@
 ):
     copy_hidden = pltpu.make_async_copy(bundles_ref.at[:, pl.ds(HIDDEN, 4)], hidden_ref, sems.at[0])
     copy_own = pltpu.make_async_copy(bundles_ref.at[:, 0], own_ref, sems.at[1])
-    copy_first = pltpu.make_async_copy(
-        bundles_ref.at[:, pl.ds(FIRST, 25)], first_ref.at[:, pl.ds(0, 25)], sems.at[2]
-    )
+    copies = [
+        pltpu.make_async_copy(
+            bundles_ref.at[i, pl.ds(FIRST, 25)], first_ref.at[i, pl.ds(0, 25)], sems.at[2 + i]
+        )
+        for i in range(VIS)
+    ]
     copy_hidden.start()
     copy_own.start()
-    copy_first.start()
+    for copy in copies:
+        copy.start()
     first_ref[:, 25:32] = jnp.zeros((VIS, 7, OWN, 128), BF16)
     language = lax.broadcasted_iota(jnp.int32, (RC, ROWS), 1)
     slot = lax.broadcasted_iota(jnp.int32, (RC, ROWS), 0)
@@ -261,8 +269,8 @@
     right = block[:, 128:256] + jnp.where(r == 2 * v + 1, own, 0.0)
     block = jnp.concatenate([left.reshape(RC, 8, 128), right.reshape(RC, 8, 128)], axis=1)
     out_ref[:, :, LANES : LANES + 128] = block.astype(BF16)
-    copy_first.wait()
     for i in range(VIS):
+        copies[i].wait()
         y = dot(act, first_ref[i].reshape(LANES, 128), 1, 1)
         for k in range(4):
             spread[k, pl.ds(i, RC, stride=VIS), :] = y[:, 128 * k : 128 * k + 128]
@@ -400,9 +408,10 @@
         pieces,
         bias,
         weights,
-        scratch=[pltpu.SemaphoreType.DMA],
+        scratch=[pltpu.SemaphoreType.DMA((VIS,))],
         remote=1,
     )
+    gathered, input_part = lax.optimization_barrier((gathered, input_part))
     spread, own = local(
         own_sum_kernel, (struct((RC, OWN, 128), BF16), struct((OWN, 128), BF16)), swap(input_part, GROUP)
     )
@@ -434,7 +443,7 @@
             pltpu.VMEM((VIS, 4, OWN, 128), BF16),
             pltpu.VMEM((VIS, OWN, 128), BF16),
             pltpu.VMEM((4, RC * VIS, 128), F32),
-            pltpu.SemaphoreType.DMA((3,)),
+            pltpu.SemaphoreType.DMA((2 + VIS,)),
         ],
         remote=1,
     )

time: 202 us -> 205 us (1.015)
  Pallas kernels: 18 us -> 21.4 us
    pallas_call x9, Pallas kernels: 12.2 us -> 15.6 us  [local(): pl.pallas_call(kernel, out_shape=outs, in_specs=ins + [pl.BlockSpec(memor...]
where the time goes in v10:
time: 205 us; the launch traced here: 202 us
  blocking collectives  146 us (71%)
  Pallas kernels  21.4 us (10%)
  waiting for transfers between devices  15.7 us (8%)
  between operations  14.1 us (7%)
  starting transfers between devices  4.07 us (2%)
    all_to_all x9, blocking collectives, swap(): return lax.all_to_all(blocks, axes, 0, 0, tiled=True)  146 us
    pallas_call x9, Pallas kernels, local(): pl.pallas_call(kernel, out_shape=outs, in_specs=ins + [pl.BlockSpec(memor...  15.6 us
    all_to_all x1, waiting for transfers between devices, swap(): return lax.all_to_all(blocks, axes, 0, 0, tiled=True)  15.1 us
  transfers between devices with their start and end apart: 3, of which 2 were waited for; matrix products, arithmetic and copies ran while one was open for 0% of the time, Pallas kernels for 3%

profile of v10, /device:TPU:1, one launch (start us, length us, event | category | flops | bytes accessed | tf_op | source)
XLA Modules:
  0.0 202.1 jit_solution(5492077080565762134)
XLA Ops:
  7.2 1.9 shard_map.141
  9.2 0.0 all-gather.7.cloned.1.call-start
  9.3 0.8 reshape.14.gain_ref
  10.0 1.1 shard_map.138
  11.1 17.1 %all_to_all.50.arrived_ref = f32[16,8,128]{2,1,0:T(8,128)S(1)} all-to-all(f32[16,8,128]{2,1,0:T(8,128)S(1)} %get-tuple-element.27), channel_id=1, replica_groups=mesh['chip'=8,'core'=2,'row'=4,'col'=8] {'chip','core'}, dimensions={0} | all-to-all | bytes 131072 | tf_op jit(solution)/shard_map/all_to_all | solution.py:349
  28.3 0.7 shard_map.139
  29.0 28.5 %all_to_all.51.rows_ref = bf16[32,16,640]{2,1,0:T(8,128)(2,1)S(1)} all-to-all(bf16[32,16,640]{2,1,0:T(8,128)(2,1)S(1)} %shard_map.139), channel_id=1, replica_groups=mesh['chip'=8,'core'=2,'row'=4,'col'=8] {'row','col'}, dimensions={0} | all-to-all | bytes 1310720 | tf_op jit(solution)/shard_map/all_to_all | solution.py:349
  57.5 2.0 shard_map.140
  59.6 7.6 %all_to_all.52.arrived_ref = bf16[2,8,16,768]{3,2,1,0:T(8,128)(2,1)S(1)} all-to-all(bf16[2,8,16,768]{3,2,1,0:T(8,128)(2,1)S(1)} %get-tuple-element.29), channel_id=1, replica_groups=mesh['chip'=8,'core'=2,'row'=4,'col'=8] {'core'}, dimensions={0} | all-to-all | bytes 786432 | tf_op jit(solution)/shard_map/all_to_all | solution.py:349
  67.2 15.2 %all_to_all.53.arrived_ref.pieces_ref = bf16[8,16,768]{2,1,0:T(8,128)(2,1)S(1)} all-to-all(bf16[8,16,768]{2,1,0:T(8,128)(2,1)S(1)} %shard_map.142), channel_id=1, replica_groups=mesh['chip'=8,'core'=2,'row'=4,'col'=8] {'chip'}, dimensions={0} | all-to-all | bytes 393216 | tf_op jit(solution)/shard_map/all_to_all | solution.py:349
  82.4 0.6 all-gather.5.cloned.1.call-done
  82.9 3.3 %shard_map.143 = (bf16[32,16,128]{2,1,0:T(8,128)(2,1)S(1)}, bf16[16,128]{1,0:T(8,128)(2,1)S(1)}, f32[16,128]{1,0:T(8,128)S(1)}, f32[16,128]{1,0:T(8,128)S(1)}, bf16[16,128,256]{2,1,0:T(8,128)(2,1)S(1)}) custom-call(bf16[8,16,768]{2,1,0:T(8,128)(2,1)S(1)} %all_to_all.53.arrived_ref.pieces_ref, f32[1,128]{1,0:T(1,128)S(1)} %get-tuple-element.30.bias_ref, ...), custom_call_target="tpu_custom_call" | custom-call | tf_op jit(solution)/shard_map/pallas_call | solution.py:338
  86.2 19.3 %all_to_all.54.arrived_ref = bf16[32,16,128]{2,1,0:T(8,128)(2,1)S(1)} all-to-all(bf16[32,16,128]{2,1,0:T(8,128)(2,1)S(1)} %get-tuple-element.32), channel_id=1, replica_groups=mesh['chip'=8,'core'=2,'row'=4,'col'=8] {'row','col'}, dimensions={0} | all-to-all | bytes 262144 | tf_op jit(solution)/shard_map/all_to_all | solution.py:349
  105.6 13.4 %all_to_all.55.inputs_ref = bf16[32,16,128]{2,1,0:T(8,128)(2,1)S(1)} all-to-all(bf16[32,16,128]{2,1,0:T(8,128)(2,1)S(1)} %get-tuple-element.33), channel_id=1, replica_groups=mesh['chip'=8,'core'=2,'row'=4,'col'=8] {'row','col'}, dimensions={0} | all-to-all | bytes 262144 | tf_op jit(solution)/shard_map/all_to_all | solution.py:349
  119.0 4.0 %shard_map.145 = (bf16[32,16,128]{2,1,0:T(8,128)(2,1)S(1)}, bf16[31,16,128]{2,1,0:T(8,128)(2,1)}) custom-call(bf16[32,16,128]{2,1,0:T(8,128)(2,1)S(1)} %all_to_all.55.inputs_ref, bf16[8,16,768]{2,1,0:T(8,128)(2,1)S(1)} %all_to_all.53.arrived_ref.pieces_ref, bf16[16,128]{1,0:T(8,128)(2,1)S(1)} %get-tuple-element.34.act_ref, ...), custom_call_target="tpu_custom_call" | custom-call | tf_op jit(solution)/shard_map/pallas_call | solution.py:338
  122.9 12.7 %all_to_all.56.arrived_ref = bf16[32,16,128]{2,1,0:T(8,128)(2,1)S(1)} all-to-all(bf16[32,16,128]{2,1,0:T(8,128)(2,1)S(1)} %get-tuple-element.37), channel_id=1, replica_groups=mesh['chip'=8,'core'=2,'row'=4,'col'=8] {'row','col'}, dimensions={0} | all-to-all | bytes 262144 | tf_op jit(solution)/shard_map/all_to_all | solution.py:349
  135.7 12.7 %all_to_all.57.grad_ref = bf16[32,16,128]{2,1,0:T(8,128)(2,1)S(1)} all-to-all(bf16[32,16,128]{2,1,0:T(8,128)(2,1)S(1)} %shard_map.146), channel_id=1, replica_groups=mesh['chip'=8,'core'=2,'row'=4,'col'=8] {'row','col'}, dimensions={0} | all-to-all | bytes 262144 | tf_op jit(solution)/shard_map/all_to_all | solution.py:349
  148.4 0.4 shard_map.147
  148.8 19.5 %all_to_all.58.pieces_ref = bf16[16,16,384]{2,1,0:T(8,128)(2,1)S(1)} all-to-all(bf16[16,16,384]{2,1,0:T(8,128)(2,1)S(1)} %shard_map.147), channel_id=1, replica_groups=mesh['chip'=8,'core'=2,'row'=4,'col'=8] {'chip','core'}, dimensions={0} | all-to-all | bytes 393216 | tf_op jit(solution)/shard_map/all_to_all | solution.py:349
  168.3 5.2 %shard_map.148 = bf16[32,16,640]{2,1,0:T(8,128)(2,1)} custom-call(s32[2,8,128]{2,1,0:T(8,128)S(1)} %get-tuple-element.28.mine_ref, bf16[16,16,384]{2,1,0:T(8,128)(2,1)S(1)} %all_to_all.58.pieces_ref, bf16[512,256]{1,0:T(8,128)(2,1)S(1)} %copy-done.1, bf16[16,31,16,128]{3,2,1,0:T(8,128)(2,1)} %bitcast.5), custom_call_target="tpu_custom_call" | custom-call | tf_op jit(solution)/shard_map/pallas_call | solution.py:338
  173.5 4.0 %all-to-all-start.9 = ((bf16[32,16,640]{2,1,0:T(8,128)(2,1)}), bf16[32,16,640]{2,1,0:T(8,128)(2,1)S(1)}, u32[]{:S(2)}, u32[]{:S(2)}) async-start(bf16[32,16,640]{2,1,0:T(8,128)(2,1)} %shard_map.148), calls=%async_computation.9 | async-start | bytes 1310720 | tf_op jit(solution)/shard_map/all_to_all | solution.py:349
  177.5 1.8 shard_map.150
  179.3 15.1 %all-to-all-done.9.arrived_ref = bf16[32,16,640]{2,1,0:T(8,128)(2,1)S(1)} async-done(((bf16[32,16,640]{2,1,0:T(8,128)(2,1)}), bf16[32,16,640]{2,1,0:T(8,128)(2,1)S(1)}, u32[]{:S(2)}, u32[]{:S(2)}) %all-to-all-start.9) | async-done | bytes 655392 | tf_op jit(solution)/shard_map/all_to_all | solution.py:349
  194.4 0.9 shard_map.149
  (13 shorter events, 0.2 us)
Async XLA Ops:
  7.2 111.8 %copy-start.2 = (bf16[400,128]{1,0:T(8,128)(2,1)S(1)}, bf16[400,128]{1,0:T(8,128)(2,1)}, u32[]{:S(2)}) copy-start(bf16[400,128]{1,0:T(8,128)(2,1)} %first_ref.3) | copy-start | bytes 307204
  7.2 75.8 %all-gather.5.cloned.1.call-start = ((), (), s32[]{:S(2)}) async-start(), calls=%async_computation.10 | async-start | bytes 10027008 | tf_op jit(solution)/shard_map/all_gather | solution.py:363
  9.2 159.1 %all-gather.7.cloned.1.call-start = ((), (), s32[]{:S(2)}) async-start(), calls=%async_computation.11 | async-start | bytes 2158592 | tf_op jit(solution)/shard_map/all_gather | solution.py:429
  82.9 36.0 %copy-start = (bf16[18432,256]{1,0:T(8,128)(2,1)S(1)}, bf16[18432,256]{1,0:T(8,128)(2,1)}, u32[]{:S(2)}) copy-start(bf16[18432,256]{1,0:T(8,128)(2,1)} %all-gather.5.cloned.1.call-done) | copy-start | bytes 28311556
  82.9 85.4 %copy-start.1 = (bf16[512,256]{1,0:T(8,128)(2,1)S(1)}, bf16[512,256]{1,0:T(8,128)(2,1)}, u32[]{:S(2)}) copy-start(bf16[512,256]{1,0:T(8,128)(2,1)} %down_ref.3) | copy-start | bytes 786436
  173.5 20.9 %all-to-all-start.9 = ((bf16[32,16,640]{2,1,0:T(8,128)(2,1)}), bf16[32,16,640]{2,1,0:T(8,128)(2,1)S(1)}, u32[]{:S(2)}, u32[]{:S(2)}) async-start(bf16[32,16,640]{2,1,0:T(8,128)(2,1)} %shard_map.148), calls=%async_computation.9 | async-start | bytes 1310720 | tf_op jit(solution)/shard_map/all_to_all | solution.py:349
Sparse Core Ops, SparseCore 0:
  10.1 72.7 all-gather.4
  123.1 36.9 all-gather.6

commit v11 on v9

--- a/solution.py
+++ b/solution.py
@@ -43,19 +43,21 @@
     return lax.axis_index("row") * lax.axis_size("col") + lax.axis_index("col")
 
 
-def pack_kernel(gate_ref, up_ref, second_ref, out_ref, sems):
+def pack_kernel(gate_ref, up_ref, second_ref, out_ref, block, sems):
     parts = [(gate_ref, 0), (gate_ref, 256), (up_ref, 0), (up_ref, 256), (second_ref, 0)]
-    copies = []
+    arrive, leave = [], []
     for i, (ref, column) in enumerate(parts):
-        rows = ref.shape[0]
-        copies.append(
-            pltpu.make_async_copy(
-                ref.at[:, pl.ds(column, 256)], out_ref.at[pl.ds(256 * i, rows), :], sems.at[i]
-            )
+        own = pl.ds(256 * i, ref.shape[0])
+        arrive.append(
+            pltpu.make_async_copy(ref.at[:, pl.ds(column, 256)], block.at[own, :], sems.at[0, i])
         )
-    for copy in copies:
+        leave.append(pltpu.make_async_copy(block.at[own, :], out_ref.at[own, :], sems.at[1, i]))
+    for copy in arrive:
         copy.start()
-    for copy in copies:
+    for first, second in zip(arrive, leave):
+        first.wait()
+        second.start()
+    for copy in leave:
         copy.wait()
 
 
@@ -156,7 +158,16 @@
 
 
 def second_kernel(
-    arrived_ref, bias_ref, weights_ref, out_ref, hidden_ref, slope_ref, back_ref, second_ref, sem
+    arrived_ref,
+    bias_ref,
+    weights_ref,
+    out_ref,
+    hidden_ref,
+    slope_ref,
+    back_ref,
+    second_ref,
+    grad_ref,
+    sem,
 ):
     copy = pltpu.make_async_copy(weights_ref.at[:, pl.ds(1024, 128), :], second_ref, sem)
     copy.start()
@@ -170,6 +181,10 @@
     hidden = (pre * cdf).astype(BF16)
     hidden_ref[...] = hidden
     slope_ref[...] = cdf + pre * density
+    grad = jnp.zeros((OWN, 512), F32)
+    for v in range(CHIPS):
+        grad = grad + arrived_ref[v, :, 0:512].astype(F32)
+    grad_ref[...] = grad
     copy.wait()
     for v in range(VIS):
         y = dot(hidden, second_ref[v]).astype(BF16)
@@ -191,7 +206,7 @@
     own_ref[...] = out_ref[0]
 
 
-def block_kernel(inputs_ref, pieces_ref, act_ref, own_ref, first_ref, w_ref, out_ref, bundle_ref):
+def block_kernel(inputs_ref, grad_ref, act_ref, own_ref, first_ref, w_ref, out_ref, bundle_ref):
     bundle_ref[0] = own_ref[...]
     bundle_ref[1] = act_ref[...]
     bundle_ref[FIRST : FIRST + 25] = first_ref[...].reshape(25, OWN, 128)
@@ -200,9 +215,7 @@
         x = jnp.concatenate([inputs_ref[2 * v], inputs_ref[2 * v + 1]], axis=1)
         for k in range(4):
             sums[k] = sums[k] + dot(x, w_ref[v, 256 * k : 256 * k + 256, :])
-    h = jnp.zeros((OWN, 512), F32)
-    for i in range(CHIPS):
-        h = h + pieces_ref[i, :, 0:512].astype(F32)
+    h = grad_ref[...]
     g = jnp.concatenate(sums[0:2], axis=1)
     u = jnp.concatenate(sums[2:4], axis=1)
     s = jax.nn.sigmoid(g)
@@ -233,15 +246,13 @@
 
 
 def slot_kernel(
-    mine_ref, pieces_ref, down_ref, bundles_ref, out_ref, first_ref, hidden_ref, own_ref, spread, sems
+    mine_ref, pieces_ref, down_ref, bundles_ref, out_ref, first_ref, hidden_ref, spread, sems
 ):
-    copy_hidden = pltpu.make_async_copy(bundles_ref.at[:, pl.ds(HIDDEN, 4)], hidden_ref, sems.at[0])
-    copy_own = pltpu.make_async_copy(bundles_ref.at[:, 0], own_ref, sems.at[1])
+    copy_hidden = pltpu.make_async_copy(bundles_ref.at[:, pl.ds(0, FIRST)], hidden_ref, sems.at[0])
     copy_first = pltpu.make_async_copy(
-        bundles_ref.at[:, pl.ds(FIRST, 25)], first_ref.at[:, pl.ds(0, 25)], sems.at[2]
+        bundles_ref.at[:, pl.ds(FIRST, 25)], first_ref.at[:, pl.ds(0, 25)], sems.at[1]
     )
     copy_hidden.start()
-    copy_own.start()
     copy_first.start()
     first_ref[:, 25:32] = jnp.zeros((VIS, 7, OWN, 128), BF16)
     language = lax.broadcasted_iota(jnp.int32, (RC, ROWS), 1)
@@ -253,10 +264,11 @@
     r = group_index()
     v = owner_index()
     copy_hidden.wait()
-    copy_own.wait()
-    hidden = jnp.concatenate([hidden_ref[:, k].reshape(ROWS, 128) for k in range(4)], axis=1)
+    hidden = jnp.concatenate(
+        [hidden_ref[:, HIDDEN + k].reshape(ROWS, 128) for k in range(4)], axis=1
+    )
     block = dot(hidden, down_ref[...])
-    own = own_ref[...].reshape(ROWS, 128).astype(F32)
+    own = hidden_ref[:, 0].reshape(ROWS, 128).astype(F32)
     left = block[:, 0:128] + jnp.where(r == 2 * v, own, 0.0)
     right = block[:, 128:256] + jnp.where(r == 2 * v + 1, own, 0.0)
     block = jnp.concatenate([left.reshape(RC, 8, 128), right.reshape(RC, 8, 128)], axis=1)
@@ -348,9 +360,8 @@
         pack_kernel,
         out_shape=struct((1152, 256), BF16),
         in_specs=[pl.BlockSpec(memory_space=pl.ANY)] * 3,
-        grid=(1,),
-        out_specs=full((1152, 256)),
-        scratch_shapes=[pltpu.SemaphoreType.DMA((5,))],
+        out_specs=pl.BlockSpec(memory_space=pl.ANY),
+        scratch_shapes=[pltpu.VMEM((1152, 256), BF16), pltpu.SemaphoreType.DMA((2, 5))],
     )(in_hbm(gate_w), in_hbm(up_w), in_hbm(proj_second))
     gathered = lax.all_gather(packed, OWNERS)
     weights = in_hbm(gathered)
@@ -388,7 +399,7 @@
     )
     pairs = local(pair_kernel, struct((CHIPS, OWN, 768), BF16), swap(partial, "core"))
     pieces = swap(pairs, "chip")
-    input_part, hidden_proj, slope, back, seconds = local(
+    input_part, hidden_proj, slope, back, seconds, grad = local(
         second_kernel,
         (
             struct((RC, OWN, 128), BF16),
@@ -396,6 +407,7 @@
             struct((OWN, 128), F32),
             struct((OWN, 128), F32),
             struct((VIS, 128, 256), BF16),
+            struct((OWN, 512), F32),
         ),
         pieces,
         bias,
@@ -411,7 +423,7 @@
         block_kernel,
         (struct((RC, OWN, 128), BF16), struct((BUNDLE, OWN, 128), BF16)),
         inputs,
-        pieces,
+        grad,
         hidden_proj,
         own,
         proj_first,
@@ -431,10 +443,9 @@
         bundles,
         scratch=[
             pltpu.VMEM((VIS, 32, OWN, 128), BF16),
-            pltpu.VMEM((VIS, 4, OWN, 128), BF16),
-            pltpu.VMEM((VIS, OWN, 128), BF16),
+            pltpu.VMEM((VIS, FIRST, OWN, 128), BF16),
             pltpu.VMEM((4, RC * VIS, 128), F32),
-            pltpu.SemaphoreType.DMA((3,)),
+            pltpu.SemaphoreType.DMA((2,)),
         ],
         remote=1,
     )

time: 202 us -> 202 us (level)
  no operation moved by 1% of the time
where the time goes in v11:
time: 202 us; the launch traced here: 199 us
  blocking collectives  146 us (72%)
  Pallas kernels  17.9 us (9%)
  waiting for transfers between devices  15.9 us (8%)
  between operations  14.1 us (7%)
  starting transfers between devices  4.06 us (2%)
    all_to_all x9, blocking collectives, swap(): return lax.all_to_all(blocks, axes, 0, 0, tiled=True)  146 us
    all_to_all x1, waiting for transfers between devices, swap(): return lax.all_to_all(blocks, axes, 0, 0, tiled=True)  15.1 us
    pallas_call x9, Pallas kernels, local(): pl.pallas_call(kernel, out_shape=outs, in_specs=ins + [pl.BlockSpec(memor...  12.2 us
  transfers between devices with their start and end apart: 3, of which 2 were waited for; matrix products, arithmetic and copies ran while one was open for 0% of the time, Pallas kernels for 3%

profile of v11, /device:TPU:1, one launch (start us, length us, event | category | flops | bytes accessed | tf_op | source)
XLA Modules:
  0.0 199.0 jit_solution(17708018551745312687)
XLA Ops:
  7.2 1.9 shard_map.142
  9.1 0.0 all-gather.7.cloned.1.call-start
  9.2 0.8 reshape.14.gain_ref
  9.9 1.1 shard_map.138
  11.0 17.1 %all_to_all.50.arrived_ref = f32[16,8,128]{2,1,0:T(8,128)S(1)} all-to-all(f32[16,8,128]{2,1,0:T(8,128)S(1)} %get-tuple-element.26), channel_id=1, replica_groups=mesh['chip'=8,'core'=2,'row'=4,'col'=8] {'chip','core'}, dimensions={0} | all-to-all | bytes 131072 | tf_op jit(solution)/shard_map/all_to_all | solution.py:353
  28.2 0.7 shard_map.139
  28.9 28.5 %all_to_all.51.rows_ref = bf16[32,16,640]{2,1,0:T(8,128)(2,1)S(1)} all-to-all(bf16[32,16,640]{2,1,0:T(8,128)(2,1)S(1)} %shard_map.139), channel_id=1, replica_groups=mesh['chip'=8,'core'=2,'row'=4,'col'=8] {'row','col'}, dimensions={0} | all-to-all | bytes 1310720 | tf_op jit(solution)/shard_map/all_to_all | solution.py:353
  57.5 2.0 %shard_map.140 = (bf16[2,8,16,768]{3,2,1,0:T(8,128)(2,1)S(1)}, s32[8,512]{1,0:T(8,128)S(1)}, f32[1,128]{1,0:T(1,128)S(1)}, s32[2,8,128]{2,1,0:T(8,128)S(1)}) custom-call(s32[16]{0:T(128)} %counts_ref.1, s32[16]{0:T(128)} %order_ref.1, bf16[32,16,640]{2,1,0:T(8,128)(2,1)S(1)} %all_to_all.51.rows_ref, bf16[400,128]{1,0:T(8,128)(2,1)} %first_ref.3, ...), custom_call_target="tpu_custom_call" | custom-call | tf_op jit(solution)/shard_map/pallas_call | solution.py:329
  59.5 7.6 %all_to_all.52.arrived_ref = bf16[2,8,16,768]{3,2,1,0:T(8,128)(2,1)S(1)} all-to-all(bf16[2,8,16,768]{3,2,1,0:T(8,128)(2,1)S(1)} %get-tuple-element.28), channel_id=1, replica_groups=mesh['chip'=8,'core'=2,'row'=4,'col'=8] {'core'}, dimensions={0} | all-to-all | bytes 786432 | tf_op jit(solution)/shard_map/all_to_all | solution.py:353
  67.1 15.1 %all_to_all.53.arrived_ref = bf16[8,16,768]{2,1,0:T(8,128)(2,1)S(1)} all-to-all(bf16[8,16,768]{2,1,0:T(8,128)(2,1)S(1)} %shard_map.141), channel_id=1, replica_groups=mesh['chip'=8,'core'=2,'row'=4,'col'=8] {'chip'}, dimensions={0} | all-to-all | bytes 393216 | tf_op jit(solution)/shard_map/all_to_all | solution.py:353
  82.3 0.8 all-gather.5.cloned.1.call-done
  83.0 1.6 shard_map.143
  84.7 19.5 %all_to_all.54.arrived_ref = bf16[32,16,128]{2,1,0:T(8,128)(2,1)S(1)} all-to-all(bf16[32,16,128]{2,1,0:T(8,128)(2,1)S(1)} %get-tuple-element.30), channel_id=1, replica_groups=mesh['chip'=8,'core'=2,'row'=4,'col'=8] {'row','col'}, dimensions={0} | all-to-all | bytes 262144 | tf_op jit(solution)/shard_map/all_to_all | solution.py:353
  104.3 13.4 %all_to_all.55.inputs_ref = bf16[32,16,128]{2,1,0:T(8,128)(2,1)S(1)} all-to-all(bf16[32,16,128]{2,1,0:T(8,128)(2,1)S(1)} %get-tuple-element.31), channel_id=1, replica_groups=mesh['chip'=8,'core'=2,'row'=4,'col'=8] {'row','col'}, dimensions={0} | all-to-all | bytes 262144 | tf_op jit(solution)/shard_map/all_to_all | solution.py:353
  117.6 4.0 %shard_map.145 = (bf16[32,16,128]{2,1,0:T(8,128)(2,1)S(1)}, bf16[31,16,128]{2,1,0:T(8,128)(2,1)}) custom-call(bf16[32,16,128]{2,1,0:T(8,128)(2,1)S(1)} %all_to_all.55.inputs_ref, f32[16,512]{1,0:T(8,128)S(1)} %get-tuple-element.32.grad_ref, bf16[16,128]{1,0:T(8,128)(2,1)S(1)} %get-tuple-element.33.act_ref, bf16[16,128]{1,0:T(8,128)(2,1)S(1)} %get-tuple-element.34.own_ref, ...), custom_call_target="tpu_custom_call" | custom-call | tf_op jit(solution)/shard_map/pallas_call | solution.py:342
  121.6 12.7 %all_to_all.56.arrived_ref = bf16[32,16,128]{2,1,0:T(8,128)(2,1)S(1)} all-to-all(bf16[32,16,128]{2,1,0:T(8,128)(2,1)S(1)} %get-tuple-element.35), channel_id=1, replica_groups=mesh['chip'=8,'core'=2,'row'=4,'col'=8] {'row','col'}, dimensions={0} | all-to-all | bytes 262144 | tf_op jit(solution)/shard_map/all_to_all | solution.py:353
  134.4 12.7 %all_to_all.57.grad_ref = bf16[32,16,128]{2,1,0:T(8,128)(2,1)S(1)} all-to-all(bf16[32,16,128]{2,1,0:T(8,128)(2,1)S(1)} %shard_map.146), channel_id=1, replica_groups=mesh['chip'=8,'core'=2,'row'=4,'col'=8] {'row','col'}, dimensions={0} | all-to-all | bytes 262144 | tf_op jit(solution)/shard_map/all_to_all | solution.py:353
  147.1 0.4 shard_map.147
  147.5 19.5 %all_to_all.58.pieces_ref = bf16[16,16,384]{2,1,0:T(8,128)(2,1)S(1)} all-to-all(bf16[16,16,384]{2,1,0:T(8,128)(2,1)S(1)} %shard_map.147), channel_id=1, replica_groups=mesh['chip'=8,'core'=2,'row'=4,'col'=8] {'chip','core'}, dimensions={0} | all-to-all | bytes 393216 | tf_op jit(solution)/shard_map/all_to_all | solution.py:353
  167.0 3.4 %shard_map.148 = bf16[32,16,640]{2,1,0:T(8,128)(2,1)} custom-call(s32[2,8,128]{2,1,0:T(8,128)S(1)} %get-tuple-element.27.mine_ref, bf16[16,16,384]{2,1,0:T(8,128)(2,1)S(1)} %all_to_all.58.pieces_ref, bf16[512,256]{1,0:T(8,128)(2,1)S(1)} %copy-done.1, bf16[16,31,16,128]{3,2,1,0:T(8,128)(2,1)} %bitcast.5), custom_call_target="tpu_custom_call" | custom-call | tf_op jit(solution)/shard_map/pallas_call | solution.py:342
  170.4 4.0 %all-to-all-start.9 = ((bf16[32,16,640]{2,1,0:T(8,128)(2,1)}), bf16[32,16,640]{2,1,0:T(8,128)(2,1)S(1)}, u32[]{:S(2)}, u32[]{:S(2)}) async-start(bf16[32,16,640]{2,1,0:T(8,128)(2,1)} %shard_map.148), calls=%async_computation.9 | async-start | bytes 1310720 | tf_op jit(solution)/shard_map/all_to_all | solution.py:353
  174.4 1.7 shard_map.150
  176.2 15.1 %all-to-all-done.9.arrived_ref = bf16[32,16,640]{2,1,0:T(8,128)(2,1)S(1)} async-done(((bf16[32,16,640]{2,1,0:T(8,128)(2,1)}), bf16[32,16,640]{2,1,0:T(8,128)(2,1)S(1)}, u32[]{:S(2)}, u32[]{:S(2)}) %all-to-all-start.9) | async-done | bytes 655392 | tf_op jit(solution)/shard_map/all_to_all | solution.py:353
  191.3 0.9 shard_map.149
  (13 shorter events, 0.2 us)
Async XLA Ops:
  7.2 110.5 %copy-start.2 = (bf16[400,128]{1,0:T(8,128)(2,1)S(1)}, bf16[400,128]{1,0:T(8,128)(2,1)}, u32[]{:S(2)}) copy-start(bf16[400,128]{1,0:T(8,128)(2,1)} %first_ref.3) | copy-start | bytes 307204
  7.2 75.8 %all-gather.5.cloned.1.call-start = ((), (), s32[]{:S(2)}) async-start(), calls=%async_computation.10 | async-start | bytes 10027008 | tf_op jit(solution)/shard_map/all_gather | solution.py:366
  9.1 157.9 %all-gather.7.cloned.1.call-start = ((), (), s32[]{:S(2)}) async-start(), calls=%async_computation.11 | async-start | bytes 2158592 | tf_op jit(solution)/shard_map/all_gather | solution.py:432
  83.0 34.6 %copy-start = (bf16[18432,256]{1,0:T(8,128)(2,1)S(1)}, bf16[18432,256]{1,0:T(8,128)(2,1)}, u32[]{:S(2)}) copy-start(bf16[18432,256]{1,0:T(8,128)(2,1)} %all-gather.5.cloned.1.call-done) | copy-start | bytes 28311556
  83.0 83.9 %copy-start.1 = (bf16[512,256]{1,0:T(8,128)(2,1)S(1)}, bf16[512,256]{1,0:T(8,128)(2,1)}, u32[]{:S(2)}) copy-start(bf16[512,256]{1,0:T(8,128)(2,1)} %down_ref.3) | copy-start | bytes 786436
  170.4 20.9 %all-to-all-start.9 = ((bf16[32,16,640]{2,1,0:T(8,128)(2,1)}), bf16[32,16,640]{2,1,0:T(8,128)(2,1)S(1)}, u32[]{:S(2)}, u32[]{:S(2)}) async-start(bf16[32,16,640]{2,1,0:T(8,128)(2,1)} %shard_map.148), calls=%async_computation.9 | async-start | bytes 1310720 | tf_op jit(solution)/shard_map/all_to_all | solution.py:353
Sparse Core Ops, SparseCore 0:
  10.1 72.8 all-gather.4
  121.7 36.9 all-gather.6

commit v12 on v11

--- a/solution.py
+++ b/solution.py
@@ -245,16 +245,10 @@
         out_ref[v, :, 256:384] = act
 
 
-def slot_kernel(
-    mine_ref, pieces_ref, down_ref, bundles_ref, out_ref, first_ref, hidden_ref, spread, sems
-):
-    copy_hidden = pltpu.make_async_copy(bundles_ref.at[:, pl.ds(0, FIRST)], hidden_ref, sems.at[0])
-    copy_first = pltpu.make_async_copy(
-        bundles_ref.at[:, pl.ds(FIRST, 25)], first_ref.at[:, pl.ds(0, 25)], sems.at[1]
-    )
-    copy_hidden.start()
-    copy_first.start()
-    first_ref[:, 25:32] = jnp.zeros((VIS, 7, OWN, 128), BF16)
+def slot_kernel(mine_ref, pieces_ref, down_ref, bundles_ref, out_ref, bundle, spread, sem):
+    copy = pltpu.make_async_copy(bundles_ref, bundle.at[:, pl.ds(0, BUNDLE)], sem)
+    copy.start()
+    bundle[:, BUNDLE : FIRST + 32] = jnp.zeros((VIS, FIRST + 32 - BUNDLE, OWN, 128), BF16)
     language = lax.broadcasted_iota(jnp.int32, (RC, ROWS), 1)
     slot = lax.broadcasted_iota(jnp.int32, (RC, ROWS), 0)
     hit = jnp.logical_and(slot < mine_ref[1, 0:1, 0:1], language == slot + mine_ref[0, 0:1, 0:1])
@@ -263,19 +257,18 @@
     ).astype(BF16)
     r = group_index()
     v = owner_index()
-    copy_hidden.wait()
+    copy.wait()
     hidden = jnp.concatenate(
-        [hidden_ref[:, HIDDEN + k].reshape(ROWS, 128) for k in range(4)], axis=1
+        [bundle[:, HIDDEN + k].reshape(ROWS, 128) for k in range(4)], axis=1
     )
     block = dot(hidden, down_ref[...])
-    own = hidden_ref[:, 0].reshape(ROWS, 128).astype(F32)
+    own = bundle[:, 0].reshape(ROWS, 128).astype(F32)
     left = block[:, 0:128] + jnp.where(r == 2 * v, own, 0.0)
     right = block[:, 128:256] + jnp.where(r == 2 * v + 1, own, 0.0)
     block = jnp.concatenate([left.reshape(RC, 8, 128), right.reshape(RC, 8, 128)], axis=1)
     out_ref[:, :, LANES : LANES + 128] = block.astype(BF16)
-    copy_first.wait()
     for i in range(VIS):
-        y = dot(act, first_ref[i].reshape(LANES, 128), 1, 1)
+        y = dot(act, bundle[i, FIRST : FIRST + 32].reshape(LANES, 128), 1, 1)
         for k in range(4):
             spread[k, pl.ds(i, RC, stride=VIS), :] = y[:, 128 * k : 128 * k + 128]
     for k in range(4):
@@ -442,10 +435,9 @@
         down_w,
         bundles,
         scratch=[
-            pltpu.VMEM((VIS, 32, OWN, 128), BF16),
-            pltpu.VMEM((VIS, FIRST, OWN, 128), BF16),
+            pltpu.VMEM((VIS, FIRST + 32, OWN, 128), BF16),
             pltpu.VMEM((4, RC * VIS, 128), F32),
-            pltpu.SemaphoreType.DMA((2,)),
+            pltpu.SemaphoreType.DMA,
         ],
         remote=1,
     )

time: 202 us -> 202 us (level)
  no operation moved by 1% of the time
where the time goes in v12:
time: 202 us; the launch traced here: 199 us
  blocking collectives  146 us (72%)
  Pallas kernels  18 us (9%)
  waiting for transfers between devices  15.9 us (8%)
  between operations  14.1 us (7%)
  starting transfers between devices  4.07 us (2%)
    all_to_all x9, blocking collectives, swap(): return lax.all_to_all(blocks, axes, 0, 0, tiled=True)  146 us
    all_to_all x1, waiting for transfers between devices, swap(): return lax.all_to_all(blocks, axes, 0, 0, tiled=True)  15.1 us
    pallas_call x9, Pallas kernels, local(): pl.pallas_call(kernel, out_shape=outs, in_specs=ins + [pl.BlockSpec(memor...  12.3 us
  transfers between devices with their start and end apart: 3, of which 2 were waited for; matrix products, arithmetic and copies ran while one was open for 0% of the time, Pallas kernels for 3%

profile of v12, /device:TPU:1, one launch (start us, length us, event | category | flops | bytes accessed | tf_op | source)
XLA Modules:
  0.0 199.1 jit_solution(15579487818796498480)
XLA Ops:
  7.2 1.9 shard_map.142
  9.1 0.0 all-gather.7.cloned.1.call-start
  9.2 0.8 reshape.14.gain_ref
  9.9 1.1 shard_map.138
  11.0 17.1 %all_to_all.50.arrived_ref = f32[16,8,128]{2,1,0:T(8,128)S(1)} all-to-all(f32[16,8,128]{2,1,0:T(8,128)S(1)} %get-tuple-element.26), channel_id=1, replica_groups=mesh['chip'=8,'core'=2,'row'=4,'col'=8] {'chip','core'}, dimensions={0} | all-to-all | bytes 131072 | tf_op jit(solution)/shard_map/all_to_all | solution.py:346
  28.2 0.7 shard_map.139
  28.9 28.5 %all_to_all.51.rows_ref = bf16[32,16,640]{2,1,0:T(8,128)(2,1)S(1)} all-to-all(bf16[32,16,640]{2,1,0:T(8,128)(2,1)S(1)} %shard_map.139), channel_id=1, replica_groups=mesh['chip'=8,'core'=2,'row'=4,'col'=8] {'row','col'}, dimensions={0} | all-to-all | bytes 1310720 | tf_op jit(solution)/shard_map/all_to_all | solution.py:346
  57.5 2.0 %shard_map.140 = (bf16[2,8,16,768]{3,2,1,0:T(8,128)(2,1)S(1)}, s32[8,512]{1,0:T(8,128)S(1)}, f32[1,128]{1,0:T(1,128)S(1)}, s32[2,8,128]{2,1,0:T(8,128)S(1)}) custom-call(s32[16]{0:T(128)} %counts_ref.1, s32[16]{0:T(128)} %order_ref.1, bf16[32,16,640]{2,1,0:T(8,128)(2,1)S(1)} %all_to_all.51.rows_ref, bf16[400,128]{1,0:T(8,128)(2,1)} %first_ref.3, ...), custom_call_target="tpu_custom_call" | custom-call | tf_op jit(solution)/shard_map/pallas_call | solution.py:322
  59.5 7.6 %all_to_all.52.arrived_ref = bf16[2,8,16,768]{3,2,1,0:T(8,128)(2,1)S(1)} all-to-all(bf16[2,8,16,768]{3,2,1,0:T(8,128)(2,1)S(1)} %get-tuple-element.28), channel_id=1, replica_groups=mesh['chip'=8,'core'=2,'row'=4,'col'=8] {'core'}, dimensions={0} | all-to-all | bytes 786432 | tf_op jit(solution)/shard_map/all_to_all | solution.py:346
  67.1 15.1 %all_to_all.53.arrived_ref = bf16[8,16,768]{2,1,0:T(8,128)(2,1)S(1)} all-to-all(bf16[8,16,768]{2,1,0:T(8,128)(2,1)S(1)} %shard_map.141), channel_id=1, replica_groups=mesh['chip'=8,'core'=2,'row'=4,'col'=8] {'chip'}, dimensions={0} | all-to-all | bytes 393216 | tf_op jit(solution)/shard_map/all_to_all | solution.py:346
  82.3 0.8 all-gather.5.cloned.1.call-done
  83.0 1.6 shard_map.143
  84.7 19.5 %all_to_all.54.arrived_ref = bf16[32,16,128]{2,1,0:T(8,128)(2,1)S(1)} all-to-all(bf16[32,16,128]{2,1,0:T(8,128)(2,1)S(1)} %get-tuple-element.30), channel_id=1, replica_groups=mesh['chip'=8,'core'=2,'row'=4,'col'=8] {'row','col'}, dimensions={0} | all-to-all | bytes 262144 | tf_op jit(solution)/shard_map/all_to_all | solution.py:346
  104.3 13.4 %all_to_all.55.inputs_ref = bf16[32,16,128]{2,1,0:T(8,128)(2,1)S(1)} all-to-all(bf16[32,16,128]{2,1,0:T(8,128)(2,1)S(1)} %get-tuple-element.31), channel_id=1, replica_groups=mesh['chip'=8,'core'=2,'row'=4,'col'=8] {'row','col'}, dimensions={0} | all-to-all | bytes 262144 | tf_op jit(solution)/shard_map/all_to_all | solution.py:346
  117.6 4.0 %shard_map.145 = (bf16[32,16,128]{2,1,0:T(8,128)(2,1)S(1)}, bf16[31,16,128]{2,1,0:T(8,128)(2,1)}) custom-call(bf16[32,16,128]{2,1,0:T(8,128)(2,1)S(1)} %all_to_all.55.inputs_ref, f32[16,512]{1,0:T(8,128)S(1)} %get-tuple-element.32.grad_ref, bf16[16,128]{1,0:T(8,128)(2,1)S(1)} %get-tuple-element.33.act_ref, bf16[16,128]{1,0:T(8,128)(2,1)S(1)} %get-tuple-element.34.own_ref, ...), custom_call_target="tpu_custom_call" | custom-call | tf_op jit(solution)/shard_map/pallas_call | solution.py:335
  121.6 12.7 %all_to_all.56.arrived_ref = bf16[32,16,128]{2,1,0:T(8,128)(2,1)S(1)} all-to-all(bf16[32,16,128]{2,1,0:T(8,128)(2,1)S(1)} %get-tuple-element.35), channel_id=1, replica_groups=mesh['chip'=8,'core'=2,'row'=4,'col'=8] {'row','col'}, dimensions={0} | all-to-all | bytes 262144 | tf_op jit(solution)/shard_map/all_to_all | solution.py:346
  134.4 12.7 %all_to_all.57.grad_ref = bf16[32,16,128]{2,1,0:T(8,128)(2,1)S(1)} all-to-all(bf16[32,16,128]{2,1,0:T(8,128)(2,1)S(1)} %shard_map.146), channel_id=1, replica_groups=mesh['chip'=8,'core'=2,'row'=4,'col'=8] {'row','col'}, dimensions={0} | all-to-all | bytes 262144 | tf_op jit(solution)/shard_map/all_to_all | solution.py:346
  147.1 0.4 shard_map.147
  147.5 19.5 %all_to_all.58.pieces_ref = bf16[16,16,384]{2,1,0:T(8,128)(2,1)S(1)} all-to-all(bf16[16,16,384]{2,1,0:T(8,128)(2,1)S(1)} %shard_map.147), channel_id=1, replica_groups=mesh['chip'=8,'core'=2,'row'=4,'col'=8] {'chip','core'}, dimensions={0} | all-to-all | bytes 393216 | tf_op jit(solution)/shard_map/all_to_all | solution.py:346
  167.0 3.5 %shard_map.148 = bf16[32,16,640]{2,1,0:T(8,128)(2,1)} custom-call(s32[2,8,128]{2,1,0:T(8,128)S(1)} %get-tuple-element.27.mine_ref, bf16[16,16,384]{2,1,0:T(8,128)(2,1)S(1)} %all_to_all.58.pieces_ref, bf16[512,256]{1,0:T(8,128)(2,1)S(1)} %copy-done.1, bf16[16,31,16,128]{3,2,1,0:T(8,128)(2,1)} %bitcast.5), custom_call_target="tpu_custom_call" | custom-call | tf_op jit(solution)/shard_map/pallas_call | solution.py:335
  170.5 4.0 %all-to-all-start.9 = ((bf16[32,16,640]{2,1,0:T(8,128)(2,1)}), bf16[32,16,640]{2,1,0:T(8,128)(2,1)S(1)}, u32[]{:S(2)}, u32[]{:S(2)}) async-start(bf16[32,16,640]{2,1,0:T(8,128)(2,1)} %shard_map.148), calls=%async_computation.9 | async-start | bytes 1310720 | tf_op jit(solution)/shard_map/all_to_all | solution.py:346
  174.5 1.8 shard_map.150
  176.3 15.1 %all-to-all-done.9.arrived_ref = bf16[32,16,640]{2,1,0:T(8,128)(2,1)S(1)} async-done(((bf16[32,16,640]{2,1,0:T(8,128)(2,1)}), bf16[32,16,640]{2,1,0:T(8,128)(2,1)S(1)}, u32[]{:S(2)}, u32[]{:S(2)}) %all-to-all-start.9) | async-done | bytes 655392 | tf_op jit(solution)/shard_map/all_to_all | solution.py:346
  191.4 0.9 shard_map.149
  (13 shorter events, 0.2 us)
Async XLA Ops:
  7.2 110.5 %copy-start.2 = (bf16[400,128]{1,0:T(8,128)(2,1)S(1)}, bf16[400,128]{1,0:T(8,128)(2,1)}, u32[]{:S(2)}) copy-start(bf16[400,128]{1,0:T(8,128)(2,1)} %first_ref.3) | copy-start | bytes 307204
  7.2 75.8 %all-gather.5.cloned.1.call-start = ((), (), s32[]{:S(2)}) async-start(), calls=%async_computation.10 | async-start | bytes 10027008 | tf_op jit(solution)/shard_map/all_gather | solution.py:359
  9.1 157.9 %all-gather.7.cloned.1.call-start = ((), (), s32[]{:S(2)}) async-start(), calls=%async_computation.11 | async-start | bytes 2158592 | tf_op jit(solution)/shard_map/all_gather | solution.py:425
  83.0 34.6 %copy-start = (bf16[18432,256]{1,0:T(8,128)(2,1)S(1)}, bf16[18432,256]{1,0:T(8,128)(2,1)}, u32[]{:S(2)}) copy-start(bf16[18432,256]{1,0:T(8,128)(2,1)} %all-gather.5.cloned.1.call-done) | copy-start | bytes 28311556
  83.0 83.9 %copy-start.1 = (bf16[512,256]{1,0:T(8,128)(2,1)S(1)}, bf16[512,256]{1,0:T(8,128)(2,1)}, u32[]{:S(2)}) copy-start(bf16[512,256]{1,0:T(8,128)(2,1)} %down_ref.3) | copy-start | bytes 786436
  170.5 20.9 %all-to-all-start.9 = ((bf16[32,16,640]{2,1,0:T(8,128)(2,1)}), bf16[32,16,640]{2,1,0:T(8,128)(2,1)S(1)}, u32[]{:S(2)}, u32[]{:S(2)}) async-start(bf16[32,16,640]{2,1,0:T(8,128)(2,1)} %shard_map.148), calls=%async_computation.9 | async-start | bytes 1310720 | tf_op jit(solution)/shard_map/all_to_all | solution.py:346
Sparse Core Ops, SparseCore 0:
  10.1 72.8 all-gather.4
  121.7 36.9 all-gather.6

commit v13 on v11

--- a/solution.py
+++ b/solution.py
@@ -192,10 +192,15 @@
         out_ref[2 * v + 1] = y[:, 128:256]
 
 
+def pairwise(ref):
+    terms = [ref[i].astype(F32) for i in range(RC)]
+    while len(terms) > 1:
+        terms = [x + y for x, y in zip(terms[::2], terms[1::2])]
+    return terms[0]
+
+
 def sum_kernel(arrived_ref, out_ref):
-    total = jnp.zeros((OWN, 128), F32)
-    for r in range(RC):
-        total = total + arrived_ref[r].astype(F32)
+    total = pairwise(arrived_ref)
     own = total.astype(BF16)
     for r in range(RC):
         out_ref[r] = own
@@ -295,9 +300,7 @@
 
 
 def last_kernel(arrived_ref, hat_ref, gain_ref, scale_ref, image_ref, out_ref):
-    total = jnp.zeros((VIS, LANES + 128), F32)
-    for i in range(RC):
-        total = total + arrived_ref[i].astype(F32)
+    total = pairwise(arrived_ref)
     part = total[:, LANES : LANES + 128]
     part = jnp.concatenate([part[0:8], part[8:16]], axis=1)
     out_ref[...] = part.astype(BF16)

time: 202 us -> 202 us (level)
  no operation moved by 1% of the time
where the time goes in v13:
time: 202 us; the launch traced here: 199 us
  blocking collectives  146 us (72%)
  Pallas kernels  17.9 us (9%)
  waiting for transfers between devices  15.9 us (8%)
  between operations  14.1 us (7%)
  starting transfers between devices  4.05 us (2%)
    all_to_all x9, blocking collectives, swap(): return lax.all_to_all(blocks, axes, 0, 0, tiled=True)  146 us
    all_to_all x1, waiting for transfers between devices, swap(): return lax.all_to_all(blocks, axes, 0, 0, tiled=True)  15.1 us
    pallas_call x9, Pallas kernels, local(): pl.pallas_call(kernel, out_shape=outs, in_specs=ins + [pl.BlockSpec(memor...  12.2 us
  transfers between devices with their start and end apart: 3, of which 2 were waited for; matrix products, arithmetic and copies ran while one was open for 0% of the time, Pallas kernels for 3%

profile of v13, /device:TPU:1, one launch (start us, length us, event | category | flops | bytes accessed | tf_op | source)
XLA Modules:
  0.0 199.0 jit_solution(8044635925947254152)
XLA Ops:
  7.2 1.9 shard_map.142
  9.1 0.0 all-gather.7.cloned.1.call-start
  9.2 0.8 reshape.14.gain_ref
  9.9 1.1 shard_map.138
  11.0 17.1 %all_to_all.50.arrived_ref = f32[16,8,128]{2,1,0:T(8,128)S(1)} all-to-all(f32[16,8,128]{2,1,0:T(8,128)S(1)} %get-tuple-element.26), channel_id=1, replica_groups=mesh['chip'=8,'core'=2,'row'=4,'col'=8] {'chip','core'}, dimensions={0} | all-to-all | bytes 131072 | tf_op jit(solution)/shard_map/all_to_all | solution.py:356
  28.2 0.7 shard_map.139
  28.9 28.5 %all_to_all.51.rows_ref = bf16[32,16,640]{2,1,0:T(8,128)(2,1)S(1)} all-to-all(bf16[32,16,640]{2,1,0:T(8,128)(2,1)S(1)} %shard_map.139), channel_id=1, replica_groups=mesh['chip'=8,'core'=2,'row'=4,'col'=8] {'row','col'}, dimensions={0} | all-to-all | bytes 1310720 | tf_op jit(solution)/shard_map/all_to_all | solution.py:356
  57.5 2.0 %shard_map.140 = (bf16[2,8,16,768]{3,2,1,0:T(8,128)(2,1)S(1)}, s32[8,512]{1,0:T(8,128)S(1)}, f32[1,128]{1,0:T(1,128)S(1)}, s32[2,8,128]{2,1,0:T(8,128)S(1)}) custom-call(s32[16]{0:T(128)} %counts_ref.1, s32[16]{0:T(128)} %order_ref.1, bf16[32,16,640]{2,1,0:T(8,128)(2,1)S(1)} %all_to_all.51.rows_ref, bf16[400,128]{1,0:T(8,128)(2,1)} %first_ref.3, ...), custom_call_target="tpu_custom_call" | custom-call | tf_op jit(solution)/shard_map/pallas_call | solution.py:332
  59.5 7.6 %all_to_all.52.arrived_ref = bf16[2,8,16,768]{3,2,1,0:T(8,128)(2,1)S(1)} all-to-all(bf16[2,8,16,768]{3,2,1,0:T(8,128)(2,1)S(1)} %get-tuple-element.28), channel_id=1, replica_groups=mesh['chip'=8,'core'=2,'row'=4,'col'=8] {'core'}, dimensions={0} | all-to-all | bytes 786432 | tf_op jit(solution)/shard_map/all_to_all | solution.py:356
  67.1 15.1 %all_to_all.53.arrived_ref = bf16[8,16,768]{2,1,0:T(8,128)(2,1)S(1)} all-to-all(bf16[8,16,768]{2,1,0:T(8,128)(2,1)S(1)} %shard_map.141), channel_id=1, replica_groups=mesh['chip'=8,'core'=2,'row'=4,'col'=8] {'chip'}, dimensions={0} | all-to-all | bytes 393216 | tf_op jit(solution)/shard_map/all_to_all | solution.py:356
  82.3 0.8 all-gather.5.cloned.1.call-done
  83.0 1.6 shard_map.143
  84.7 19.5 %all_to_all.54.arrived_ref = bf16[32,16,128]{2,1,0:T(8,128)(2,1)S(1)} all-to-all(bf16[32,16,128]{2,1,0:T(8,128)(2,1)S(1)} %get-tuple-element.30), channel_id=1, replica_groups=mesh['chip'=8,'core'=2,'row'=4,'col'=8] {'row','col'}, dimensions={0} | all-to-all | bytes 262144 | tf_op jit(solution)/shard_map/all_to_all | solution.py:356
  104.2 13.4 %all_to_all.55.inputs_ref = bf16[32,16,128]{2,1,0:T(8,128)(2,1)S(1)} all-to-all(bf16[32,16,128]{2,1,0:T(8,128)(2,1)S(1)} %get-tuple-element.31), channel_id=1, replica_groups=mesh['chip'=8,'core'=2,'row'=4,'col'=8] {'row','col'}, dimensions={0} | all-to-all | bytes 262144 | tf_op jit(solution)/shard_map/all_to_all | solution.py:356
  117.6 4.0 %shard_map.145 = (bf16[32,16,128]{2,1,0:T(8,128)(2,1)S(1)}, bf16[31,16,128]{2,1,0:T(8,128)(2,1)}) custom-call(bf16[32,16,128]{2,1,0:T(8,128)(2,1)S(1)} %all_to_all.55.inputs_ref, f32[16,512]{1,0:T(8,128)S(1)} %get-tuple-element.32.grad_ref, bf16[16,128]{1,0:T(8,128)(2,1)S(1)} %get-tuple-element.33.act_ref, bf16[16,128]{1,0:T(8,128)(2,1)S(1)} %get-tuple-element.34.own_ref, ...), custom_call_target="tpu_custom_call" | custom-call | tf_op jit(solution)/shard_map/pallas_call | solution.py:345
  121.6 12.7 %all_to_all.56.arrived_ref = bf16[32,16,128]{2,1,0:T(8,128)(2,1)S(1)} all-to-all(bf16[32,16,128]{2,1,0:T(8,128)(2,1)S(1)} %get-tuple-element.35), channel_id=1, replica_groups=mesh['chip'=8,'core'=2,'row'=4,'col'=8] {'row','col'}, dimensions={0} | all-to-all | bytes 262144 | tf_op jit(solution)/shard_map/all_to_all | solution.py:356
  134.4 12.7 %all_to_all.57.grad_ref = bf16[32,16,128]{2,1,0:T(8,128)(2,1)S(1)} all-to-all(bf16[32,16,128]{2,1,0:T(8,128)(2,1)S(1)} %shard_map.146), channel_id=1, replica_groups=mesh['chip'=8,'core'=2,'row'=4,'col'=8] {'row','col'}, dimensions={0} | all-to-all | bytes 262144 | tf_op jit(solution)/shard_map/all_to_all | solution.py:356
  147.1 0.4 shard_map.147
  147.5 19.5 %all_to_all.58.pieces_ref = bf16[16,16,384]{2,1,0:T(8,128)(2,1)S(1)} all-to-all(bf16[16,16,384]{2,1,0:T(8,128)(2,1)S(1)} %shard_map.147), channel_id=1, replica_groups=mesh['chip'=8,'core'=2,'row'=4,'col'=8] {'chip','core'}, dimensions={0} | all-to-all | bytes 393216 | tf_op jit(solution)/shard_map/all_to_all | solution.py:356
  166.9 3.4 %shard_map.148 = bf16[32,16,640]{2,1,0:T(8,128)(2,1)} custom-call(s32[2,8,128]{2,1,0:T(8,128)S(1)} %get-tuple-element.27.mine_ref, bf16[16,16,384]{2,1,0:T(8,128)(2,1)S(1)} %all_to_all.58.pieces_ref, bf16[512,256]{1,0:T(8,128)(2,1)S(1)} %copy-done.1, bf16[16,31,16,128]{3,2,1,0:T(8,128)(2,1)} %bitcast.5), custom_call_target="tpu_custom_call" | custom-call | tf_op jit(solution)/shard_map/pallas_call | solution.py:345
  170.4 4.0 %all-to-all-start.9 = ((bf16[32,16,640]{2,1,0:T(8,128)(2,1)}), bf16[32,16,640]{2,1,0:T(8,128)(2,1)S(1)}, u32[]{:S(2)}, u32[]{:S(2)}) async-start(bf16[32,16,640]{2,1,0:T(8,128)(2,1)} %shard_map.148), calls=%async_computation.9 | async-start | bytes 1310720 | tf_op jit(solution)/shard_map/all_to_all | solution.py:356
  174.4 1.8 shard_map.150
  176.1 15.1 %all-to-all-done.9.arrived_ref = bf16[32,16,640]{2,1,0:T(8,128)(2,1)S(1)} async-done(((bf16[32,16,640]{2,1,0:T(8,128)(2,1)}), bf16[32,16,640]{2,1,0:T(8,128)(2,1)S(1)}, u32[]{:S(2)}, u32[]{:S(2)}) %all-to-all-start.9) | async-done | bytes 655392 | tf_op jit(solution)/shard_map/all_to_all | solution.py:356
  191.2 1.0 shard_map.149
  (13 shorter events, 0.2 us)
Async XLA Ops:
  7.2 110.4 %copy-start.2 = (bf16[400,128]{1,0:T(8,128)(2,1)S(1)}, bf16[400,128]{1,0:T(8,128)(2,1)}, u32[]{:S(2)}) copy-start(bf16[400,128]{1,0:T(8,128)(2,1)} %first_ref.3) | copy-start | bytes 307204
  7.2 75.8 %all-gather.5.cloned.1.call-start = ((), (), s32[]{:S(2)}) async-start(), calls=%async_computation.10 | async-start | bytes 10027008 | tf_op jit(solution)/shard_map/all_gather | solution.py:369
  9.1 157.8 %all-gather.7.cloned.1.call-start = ((), (), s32[]{:S(2)}) async-start(), calls=%async_computation.11 | async-start | bytes 2158592 | tf_op jit(solution)/shard_map/all_gather | solution.py:435
  83.0 34.6 %copy-start = (bf16[18432,256]{1,0:T(8,128)(2,1)S(1)}, bf16[18432,256]{1,0:T(8,128)(2,1)}, u32[]{:S(2)}) copy-start(bf16[18432,256]{1,0:T(8,128)(2,1)} %all-gather.5.cloned.1.call-done) | copy-start | bytes 28311556
  83.0 83.9 %copy-start.1 = (bf16[512,256]{1,0:T(8,128)(2,1)S(1)}, bf16[512,256]{1,0:T(8,128)(2,1)}, u32[]{:S(2)}) copy-start(bf16[512,256]{1,0:T(8,128)(2,1)} %down_ref.3) | copy-start | bytes 786436
  170.4 20.9 %all-to-all-start.9 = ((bf16[32,16,640]{2,1,0:T(8,128)(2,1)}), bf16[32,16,640]{2,1,0:T(8,128)(2,1)S(1)}, u32[]{:S(2)}, u32[]{:S(2)}) async-start(bf16[32,16,640]{2,1,0:T(8,128)(2,1)} %shard_map.148), calls=%async_computation.9 | async-start | bytes 1310720 | tf_op jit(solution)/shard_map/all_to_all | solution.py:356
Sparse Core Ops, SparseCore 0:
  10.1 72.8 all-gather.4
  121.7 36.9 all-gather.6
